TPU v7x, 32 devices: a whole 2x2x4 slice. The times are simulated.
32 devices in a mesh: req: 8 (over y, x, core), tp: 4 (over z).
Axes of the slice: x: 2, y: 2, z: 4, core: 2. Of those that a mesh axis runs over, the one named last changes fastest.
Arguments:
- tokens: bfloat16 [64, 2048], P('req'), may hold values from -6 to 6
- first_gain: float32 [2048], replicated, may hold values from 0.1 to 1.9
- query_weight: bfloat16 [2048, 2048], P(None, 'tp'), may hold values from -0.125 to 0.125
- key_weight: bfloat16 [2048, 2048], P(None, 'tp'), may hold values from -0.125 to 0.125
- value_weight: bfloat16 [2048, 2048], P(None, 'tp'), may hold values from -0.125 to 0.125
- out_weight: bfloat16 [2048, 2048], P('tp'), may hold values from -0.125 to 0.125
- second_gain: float32 [2048], replicated, may hold values from 0.1 to 1.9
- up_weight: bfloat16 [2048, 8192], P(None, ('req', 'tp')), may hold values from -0.125 to 0.125
- down_weight: bfloat16 [8192, 2048], P(('req', 'tp')), may hold values from -0.0625 to 0.0625
- cache_keys: bfloat16 [32768, 2048], P('req', 'tp'), may hold values from -480 to 480
- cache_values: bfloat16 [32768, 2048], P('req', 'tp'), may hold values from -6 to 6
- lengths: int32 [64], replicated, may hold values from 1 to 8192, 32768 in all
- stream_order: int32 [64], replicated, may hold values from 0 to 63, each once
Outputs:
- hidden: bfloat16 [64, 2048], P('req', 'tp')
- new_keys: bfloat16 [64, 2048], P('req', 'tp')
- new_values: bfloat16 [64, 2048], P('req', 'tp')
Inputs may be any that keep to these rules, and one draw needn't show every extreme that they name: Every request's cache holds at least one row; the lengths sum to 32768 and the longest is exactly 8192. `stream_order`: each request appears exactly once.
All inputs are finite; a program needn't handle non-finite values.
Results may differ from a plain program's by a relative error of at most 0.0055.
The roundings to bfloat16 on the way count: a program that leaves them out, or rounds other values in their place, can miss the bound.
Values may be sent and summed in bfloat16 or wider, within the bound.
No kernel may reach another device: no remote copies, remote signals or barrier semaphores. Data moves between devices by JAX's collectives and lax.ppermute only.
A program may use at most 128 MiB of HBM per device.

v0:
```python
import jax
import jax.numpy as jnp
from jax import lax
from jax.sharding import PartitionSpec as P

HEAD_DIM = 128


def merged_2(x, axis, combine):
    everything = jax.tree.map(lambda part: lax.all_gather(part, axis), x)
    first = jax.tree.map(lambda part: part[0], everything)

    def turn(k, so_far):
        return combine(so_far, jax.tree.map(lambda part: part[k], everything))

    return lax.fori_loop(1, lax.axis_size(axis), turn, first)


def layer_norm(values, gain_vector):
    center = jnp.mean(values, axis=-1, keepdims=True)
    shifted = values - center
    spread = jnp.mean(shifted * shifted, axis=-1, keepdims=True)
    return shifted * lax.rsqrt(spread + 1e-05) * gain_vector


def combine_parts(left_part, right_part):
    peak_left, mass_left, out_left = left_part
    peak_right, mass_right, out_right = right_part
    ceiling = jnp.maximum(peak_left, peak_right)
    scale_left = jnp.exp(peak_left - ceiling)
    scale_right = jnp.exp(peak_right - ceiling)
    mass_both = mass_left * scale_left + mass_right * scale_right
    out_both = out_left * jnp.repeat(scale_left, HEAD_DIM, axis=1) + out_right * jnp.repeat(
        scale_right, HEAD_DIM, axis=1
    )
    return (ceiling, mass_both, out_both)


def body(
    tokens,
    first_gain,
    query_weight,
    key_weight,
    value_weight,
    out_weight,
    second_gain,
    up_weight,
    down_weight,
    cache_keys,
    cache_values,
    lengths,
    stream_order,
):
    req_count = lax.axis_size("req")
    tp_count = lax.axis_size("tp")
    own_rows = tokens.shape[0]
    width = tokens.shape[1]
    head_width = query_weight.shape[1]
    local_heads = head_width // HEAD_DIM
    requests = own_rows * req_count
    cache_rows = cache_keys.shape[0]
    column_width = width // tp_count
    residual = tokens.astype(jnp.float32)
    normed = layer_norm(residual, first_gain).astype(jnp.bfloat16)
    queries = (
        jnp.dot(normed, query_weight, preferred_element_type=jnp.float32) * HEAD_DIM ** (-0.5)
    ).astype(jnp.bfloat16)
    new_keys = jnp.dot(normed, key_weight, preferred_element_type=jnp.float32).astype(jnp.bfloat16)
    new_values = jnp.dot(normed, value_weight, preferred_element_type=jnp.float32).astype(
        jnp.bfloat16
    )
    every_query = lax.all_gather(queries, "req", axis=0, tiled=True)
    stream_len = jnp.take(lengths, stream_order)
    bounds = jnp.cumsum(stream_len)
    positions = lax.axis_index("req") * cache_rows + jnp.arange(cache_rows, dtype=jnp.int32)
    slots = jnp.searchsorted(bounds, positions, side="right")
    row_owner = jnp.take(stream_order, slots)
    owner_ids = jnp.arange(requests, dtype=jnp.int32)
    member = row_owner[:, None] == owner_ids[None, :]
    select = member.astype(jnp.bfloat16)
    row_query = (
        jnp.dot(select, every_query, preferred_element_type=jnp.float32)
        .astype(jnp.bfloat16)
        .reshape(cache_rows, local_heads, HEAD_DIM)
    )
    key_rows = cache_keys.reshape(cache_rows, local_heads, HEAD_DIM)
    scores = jnp.einsum("rhd,rhd->rh", row_query, key_rows, preferred_element_type=jnp.float32)
    member_wide = member[:, :, None]
    peak = jnp.max(jnp.where(member_wide, scores[:, None, :], jnp.float32(-1e30)), axis=0)
    row_peak = jnp.sum(jnp.where(member_wide, peak[None, :, :], jnp.float32(0.0)), axis=1)
    expo = jnp.exp(scores - row_peak)
    mass = jnp.einsum(
        "pr,ph->rh", member.astype(jnp.float32), expo, precision=lax.Precision.HIGHEST
    )
    weights = expo.astype(jnp.bfloat16)
    masked_weights = jnp.transpose(select)[None, :, :] * jnp.transpose(weights)[:, None, :]
    value_rows = cache_values.reshape(cache_rows, local_heads, HEAD_DIM)
    partial_value = jnp.einsum(
        "hrp,phd->rhd", masked_weights, value_rows, preferred_element_type=jnp.float32
    ).reshape(requests, head_width)
    merged = merged_2((peak, mass, partial_value), "req", combine_parts)
    offset = lax.axis_index("req") * own_rows
    peak_own = lax.dynamic_slice_in_dim(merged[0], offset, own_rows, 0)
    mass_own = lax.dynamic_slice_in_dim(merged[1], offset, own_rows, 0)
    out_own = lax.dynamic_slice_in_dim(merged[2], offset, own_rows, 0)
    self_score = jnp.einsum(
        "rhd,rhd->rh",
        queries.reshape(own_rows, local_heads, HEAD_DIM),
        new_keys.reshape(own_rows, local_heads, HEAD_DIM),
        preferred_element_type=jnp.float32,
    )
    ceiling = jnp.maximum(peak_own, self_score)
    self_weight = jnp.exp(self_score - ceiling)
    older_weight = jnp.exp(peak_own - ceiling)
    total = self_weight + mass_own * older_weight
    summed = jnp.repeat(self_weight, HEAD_DIM, axis=1) * new_values.astype(
        jnp.float32
    ) + out_own * jnp.repeat(older_weight, HEAD_DIM, axis=1)
    attended = (summed / jnp.repeat(total, HEAD_DIM, axis=1)).astype(jnp.bfloat16)
    partial_middle = jnp.dot(attended, out_weight, preferred_element_type=jnp.float32)
    middle = residual + lax.psum(partial_middle, "tp")
    normed_two = layer_norm(middle, second_gain).astype(jnp.bfloat16)
    tp_offset = lax.axis_index("tp") * column_width
    unit_count = up_weight.shape[1]
    all_normed = lax.all_gather(normed_two, "req", axis=0, tiled=True)
    activation = jax.nn.gelu(
        jnp.dot(all_normed, up_weight, preferred_element_type=jnp.float32), approximate=False
    ).astype(jnp.bfloat16)
    shaped_act = activation.reshape(req_count, own_rows, unit_count)
    shaped_down = down_weight.reshape(unit_count, tp_count, column_width)
    term = jnp.einsum("arf,ftc->atrc", shaped_act, shaped_down, preferred_element_type=jnp.float32)
    term = term.reshape(req_count * tp_count, own_rows, column_width)
    mlp_out = lax.psum_scatter(term, ("req", "tp"), scatter_dimension=0, tiled=True).reshape(
        own_rows, column_width
    )
    middle_columns = lax.dynamic_slice_in_dim(middle, tp_offset, column_width, 1)
    hidden = (middle_columns + mlp_out).astype(jnp.bfloat16)
    return (hidden, new_keys, new_values)


def solution(mesh):
    return jax.shard_map(
        body,
        mesh=mesh,
        in_specs=(
            P("req", None),
            P(),
            P(None, "tp"),
            P(None, "tp"),
            P(None, "tp"),
            P("tp", None),
            P(),
            P(None, ("req", "tp")),
            P(("req", "tp"), None),
            P("req", "tp"),
            P("req", "tp"),
            P(),
            P(),
        ),
        out_specs=(P("req", "tp"), P("req", "tp"), P("req", "tp")),
        check_vma=False,
    )
```

profile of v0, /device:TPU:0, one launch (start us, length us, event | category | flops | bytes accessed | tf_op | source)
XLA Modules:
  0.0 914.4 jit_solution(7077700806579220168)
XLA Ops:
  18.1 582.3 %while.44 = (s32[]{:T(128)}, u32[4096]{0:T(1024)S(1)}, u32[4096]{0:T(1024)S(1)}, s32[64]{0:T(128)S(1)}, s32[]{:T(128)}, /*index=5*/s32[]{:T(128)}, s32[]{:T(128)}) while((s32[]{:T(128)}, u32[4096]{0:T(1024)S(1)}, u32[4096]{0:T(1024)S(1)}, s32[64]{0:T(128)S(1)}, s32[]{:T(128)}, /*index=5*/s32[]{:T(128)}, s32[]{:T(128)}) %tuple.202), condition=%wide.region_4.5_spmd.clone, body=%wide.region_3.4_spmd.clone.sunk | while | flops 1097731 | bytes 132192 | solution.py:76
  21.0 40.2 %fusion.153 = u32[4096]{0:T(1024)S(1)} fusion(u32[4096]{0:T(1024)S(1)} %get-tuple-element.653, u32[4096]{0:T(1024)S(1)} %get-tuple-element.652, s32[]{:T(128)} %get-tuple-element.662, s32[]{:T(128)} %bitcast.301, s32[]{:T(128)} %bitcast.302, s32[]{:T(128)} %bitcast.303, s32[]{:T(128)} %bitcast.304, s32[]{:T(128)} %bitcast.305, s32[]{:T(128)} %bitcast.306, ...), kind=kLoop, calls=%fused_computation.12.clone.1 | loop fusion | flops 548864 | bytes 49413 | tf_op jit(solution)/shard_map/jit(searchsorted)/jit(_searchsorted_scan_impl)/vmap(jit(_searchsorted_scan_impl))/while/body/eval_jaxpr/select_n | solution.py:76
  61.2 40.1 %fusion.152 = u32[4096]{0:T(1024)S(1)} fusion(u32[4096]{0:T(1024)S(1)} %get-tuple-element.653, u32[4096]{0:T(1024)S(1)} %get-tuple-element.652, s32[]{:T(128)} %get-tuple-element.662, s32[]{:T(128)} %bitcast.301, s32[]{:T(128)} %bitcast.302, s32[]{:T(128)} %bitcast.303, s32[]{:T(128)} %bitcast.304, s32[]{:T(128)} %bitcast.305, s32[]{:T(128)} %bitcast.306, ...), kind=kLoop, calls=%fused_computation.13.clone.1 | loop fusion | flops 548864 | bytes 49413 | tf_op jit(solution)/shard_map/jit(searchsorted)/jit(_searchsorted_scan_impl)/vmap(jit(_searchsorted_scan_impl))/while/body/eval_jaxpr/select_n | solution.py:76
  104.2 40.2 %fusion.153 = u32[4096]{0:T(1024)S(1)} fusion(u32[4096]{0:T(1024)S(1)} %get-tuple-element.653, u32[4096]{0:T(1024)S(1)} %get-tuple-element.652, s32[]{:T(128)} %get-tuple-element.662, s32[]{:T(128)} %bitcast.301, s32[]{:T(128)} %bitcast.302, s32[]{:T(128)} %bitcast.303, s32[]{:T(128)} %bitcast.304, s32[]{:T(128)} %bitcast.305, s32[]{:T(128)} %bitcast.306, ...), kind=kLoop, calls=%fused_computation.12.clone.1 | loop fusion | flops 548864 | bytes 49413 | tf_op jit(solution)/shard_map/jit(searchsorted)/jit(_searchsorted_scan_impl)/vmap(jit(_searchsorted_scan_impl))/while/body/eval_jaxpr/select_n | solution.py:76
  144.3 40.1 %fusion.152 = u32[4096]{0:T(1024)S(1)} fusion(u32[4096]{0:T(1024)S(1)} %get-tuple-element.653, u32[4096]{0:T(1024)S(1)} %get-tuple-element.652, s32[]{:T(128)} %get-tuple-element.662, s32[]{:T(128)} %bitcast.301, s32[]{:T(128)} %bitcast.302, s32[]{:T(128)} %bitcast.303, s32[]{:T(128)} %bitcast.304, s32[]{:T(128)} %bitcast.305, s32[]{:T(128)} %bitcast.306, ...), kind=kLoop, calls=%fused_computation.13.clone.1 | loop fusion | flops 548864 | bytes 49413 | tf_op jit(solution)/shard_map/jit(searchsorted)/jit(_searchsorted_scan_impl)/vmap(jit(_searchsorted_scan_impl))/while/body/eval_jaxpr/select_n | solution.py:76
  187.4 40.2 %fusion.153 = u32[4096]{0:T(1024)S(1)} fusion(u32[4096]{0:T(1024)S(1)} %get-tuple-element.653, u32[4096]{0:T(1024)S(1)} %get-tuple-element.652, s32[]{:T(128)} %get-tuple-element.662, s32[]{:T(128)} %bitcast.301, s32[]{:T(128)} %bitcast.302, s32[]{:T(128)} %bitcast.303, s32[]{:T(128)} %bitcast.304, s32[]{:T(128)} %bitcast.305, s32[]{:T(128)} %bitcast.306, ...), kind=kLoop, calls=%fused_computation.12.clone.1 | loop fusion | flops 548864 | bytes 49413 | tf_op jit(solution)/shard_map/jit(searchsorted)/jit(_searchsorted_scan_impl)/vmap(jit(_searchsorted_scan_impl))/while/body/eval_jaxpr/select_n | solution.py:76
  227.5 40.1 %fusion.152 = u32[4096]{0:T(1024)S(1)} fusion(u32[4096]{0:T(1024)S(1)} %get-tuple-element.653, u32[4096]{0:T(1024)S(1)} %get-tuple-element.652, s32[]{:T(128)} %get-tuple-element.662, s32[]{:T(128)} %bitcast.301, s32[]{:T(128)} %bitcast.302, s32[]{:T(128)} %bitcast.303, s32[]{:T(128)} %bitcast.304, s32[]{:T(128)} %bitcast.305, s32[]{:T(128)} %bitcast.306, ...), kind=kLoop, calls=%fused_computation.13.clone.1 | loop fusion | flops 548864 | bytes 49413 | tf_op jit(solution)/shard_map/jit(searchsorted)/jit(_searchsorted_scan_impl)/vmap(jit(_searchsorted_scan_impl))/while/body/eval_jaxpr/select_n | solution.py:76
  270.6 40.2 %fusion.153 = u32[4096]{0:T(1024)S(1)} fusion(u32[4096]{0:T(1024)S(1)} %get-tuple-element.653, u32[4096]{0:T(1024)S(1)} %get-tuple-element.652, s32[]{:T(128)} %get-tuple-element.662, s32[]{:T(128)} %bitcast.301, s32[]{:T(128)} %bitcast.302, s32[]{:T(128)} %bitcast.303, s32[]{:T(128)} %bitcast.304, s32[]{:T(128)} %bitcast.305, s32[]{:T(128)} %bitcast.306, ...), kind=kLoop, calls=%fused_computation.12.clone.1 | loop fusion | flops 548864 | bytes 49413 | tf_op jit(solution)/shard_map/jit(searchsorted)/jit(_searchsorted_scan_impl)/vmap(jit(_searchsorted_scan_impl))/while/body/eval_jaxpr/select_n | solution.py:76
  310.7 40.1 %fusion.152 = u32[4096]{0:T(1024)S(1)} fusion(u32[4096]{0:T(1024)S(1)} %get-tuple-element.653, u32[4096]{0:T(1024)S(1)} %get-tuple-element.652, s32[]{:T(128)} %get-tuple-element.662, s32[]{:T(128)} %bitcast.301, s32[]{:T(128)} %bitcast.302, s32[]{:T(128)} %bitcast.303, s32[]{:T(128)} %bitcast.304, s32[]{:T(128)} %bitcast.305, s32[]{:T(128)} %bitcast.306, ...), kind=kLoop, calls=%fused_computation.13.clone.1 | loop fusion | flops 548864 | bytes 49413 | tf_op jit(solution)/shard_map/jit(searchsorted)/jit(_searchsorted_scan_impl)/vmap(jit(_searchsorted_scan_impl))/while/body/eval_jaxpr/select_n | solution.py:76
  353.7 40.2 %fusion.153 = u32[4096]{0:T(1024)S(1)} fusion(u32[4096]{0:T(1024)S(1)} %get-tuple-element.653, u32[4096]{0:T(1024)S(1)} %get-tuple-element.652, s32[]{:T(128)} %get-tuple-element.662, s32[]{:T(128)} %bitcast.301, s32[]{:T(128)} %bitcast.302, s32[]{:T(128)} %bitcast.303, s32[]{:T(128)} %bitcast.304, s32[]{:T(128)} %bitcast.305, s32[]{:T(128)} %bitcast.306, ...), kind=kLoop, calls=%fused_computation.12.clone.1 | loop fusion | flops 548864 | bytes 49413 | tf_op jit(solution)/shard_map/jit(searchsorted)/jit(_searchsorted_scan_impl)/vmap(jit(_searchsorted_scan_impl))/while/body/eval_jaxpr/select_n | solution.py:76
  393.9 40.1 %fusion.152 = u32[4096]{0:T(1024)S(1)} fusion(u32[4096]{0:T(1024)S(1)} %get-tuple-element.653, u32[4096]{0:T(1024)S(1)} %get-tuple-element.652, s32[]{:T(128)} %get-tuple-element.662, s32[]{:T(128)} %bitcast.301, s32[]{:T(128)} %bitcast.302, s32[]{:T(128)} %bitcast.303, s32[]{:T(128)} %bitcast.304, s32[]{:T(128)} %bitcast.305, s32[]{:T(128)} %bitcast.306, ...), kind=kLoop, calls=%fused_computation.13.clone.1 | loop fusion | flops 548864 | bytes 49413 | tf_op jit(solution)/shard_map/jit(searchsorted)/jit(_searchsorted_scan_impl)/vmap(jit(_searchsorted_scan_impl))/while/body/eval_jaxpr/select_n | solution.py:76
  436.9 40.2 %fusion.153 = u32[4096]{0:T(1024)S(1)} fusion(u32[4096]{0:T(1024)S(1)} %get-tuple-element.653, u32[4096]{0:T(1024)S(1)} %get-tuple-element.652, s32[]{:T(128)} %get-tuple-element.662, s32[]{:T(128)} %bitcast.301, s32[]{:T(128)} %bitcast.302, s32[]{:T(128)} %bitcast.303, s32[]{:T(128)} %bitcast.304, s32[]{:T(128)} %bitcast.305, s32[]{:T(128)} %bitcast.306, ...), kind=kLoop, calls=%fused_computation.12.clone.1 | loop fusion | flops 548864 | bytes 49413 | tf_op jit(solution)/shard_map/jit(searchsorted)/jit(_searchsorted_scan_impl)/vmap(jit(_searchsorted_scan_impl))/while/body/eval_jaxpr/select_n | solution.py:76
  477.1 40.1 %fusion.152 = u32[4096]{0:T(1024)S(1)} fusion(u32[4096]{0:T(1024)S(1)} %get-tuple-element.653, u32[4096]{0:T(1024)S(1)} %get-tuple-element.652, s32[]{:T(128)} %get-tuple-element.662, s32[]{:T(128)} %bitcast.301, s32[]{:T(128)} %bitcast.302, s32[]{:T(128)} %bitcast.303, s32[]{:T(128)} %bitcast.304, s32[]{:T(128)} %bitcast.305, s32[]{:T(128)} %bitcast.306, ...), kind=kLoop, calls=%fused_computation.13.clone.1 | loop fusion | flops 548864 | bytes 49413 | tf_op jit(solution)/shard_map/jit(searchsorted)/jit(_searchsorted_scan_impl)/vmap(jit(_searchsorted_scan_impl))/while/body/eval_jaxpr/select_n | solution.py:76
  520.1 40.2 %fusion.153 = u32[4096]{0:T(1024)S(1)} fusion(u32[4096]{0:T(1024)S(1)} %get-tuple-element.653, u32[4096]{0:T(1024)S(1)} %get-tuple-element.652, s32[]{:T(128)} %get-tuple-element.662, s32[]{:T(128)} %bitcast.301, s32[]{:T(128)} %bitcast.302, s32[]{:T(128)} %bitcast.303, s32[]{:T(128)} %bitcast.304, s32[]{:T(128)} %bitcast.305, s32[]{:T(128)} %bitcast.306, ...), kind=kLoop, calls=%fused_computation.12.clone.1 | loop fusion | flops 548864 | bytes 49413 | tf_op jit(solution)/shard_map/jit(searchsorted)/jit(_searchsorted_scan_impl)/vmap(jit(_searchsorted_scan_impl))/while/body/eval_jaxpr/select_n | solution.py:76
  560.3 40.1 %fusion.152 = u32[4096]{0:T(1024)S(1)} fusion(u32[4096]{0:T(1024)S(1)} %get-tuple-element.653, u32[4096]{0:T(1024)S(1)} %get-tuple-element.652, s32[]{:T(128)} %get-tuple-element.662, s32[]{:T(128)} %bitcast.301, s32[]{:T(128)} %bitcast.302, s32[]{:T(128)} %bitcast.303, s32[]{:T(128)} %bitcast.304, s32[]{:T(128)} %bitcast.305, s32[]{:T(128)} %bitcast.306, ...), kind=kLoop, calls=%fused_computation.13.clone.1 | loop fusion | flops 548864 | bytes 49413 | tf_op jit(solution)/shard_map/jit(searchsorted)/jit(_searchsorted_scan_impl)/vmap(jit(_searchsorted_scan_impl))/while/body/eval_jaxpr/select_n | solution.py:76
  600.4 39.9 %select_select_fusion.9 = s32[4096]{0:T(1024)S(1)} fusion(u32[4096]{0:T(1024)S(1)} %get-tuple-element.246, s32[]{:T(128)} %bitcast.6, s32[]{:T(128)} %bitcast.7, s32[]{:T(128)} %bitcast.8, s32[]{:T(128)} %bitcast.9, s32[]{:T(128)} %bitcast.10, s32[]{:T(128)} %bitcast.11, s32[]{:T(128)} %bitcast.12, s32[]{:T(128)} %bitcast.13, s32[]{:T(128)} %bitcast.14, ...), kind=kLoop, calls=%fused_computation.120 | loop fusion | flops 548864 | bytes 33024 | tf_op jit(solution)/shard_map/jit(_take)/select_n | solution.py:77
  643.0 10.7 %all_gather.21 = bf16[64,512]{1,0:T(8,128)(2,1)S(1)} all-gather(bf16[8,512]{1,0:T(8,128)(2,1)S(1)} %fusion.16), channel_id=1, replica_groups=mesh['req'=8,'tp'=4] {'req'}, dimensions={0}, use_global_device_ids=true | all-gather | bytes 73728 | tf_op jit(solution)/shard_map/all_gather | solution.py:72
  671.8 10.4 %multiply_reduce_fusion = f32[4096,4]{1,0:T(8,128)} fusion(f32[4096,4,128]{2,1,0:T(4,128)} %copy.52, bf16[4096,4,128]{2,1,0:T(4,128)(2,1)} %reshape.176), kind=kLoop, calls=%fused_computation.24 | loop fusion | flops 6275072 | bytes 12648448
  690.1 8.9 all-gather.3
  699.0 7.9 all-gather.2
  714.3 10.4 %while.43 = (s32[]{:T(128)}, f32[64,4]{0,1:T(4,128)S(1)}, f32[64,4]{0,1:T(4,128)S(1)}, f32[64,512]{1,0:T(8,128)S(1)}, f32[8,64,4]{1,2,0:T(4,128)S(1)}, /*index=5...) while((s32[]{:T(128)}, f32[64,4]{0,1:T(4,128)S(1)}, ...), condition=%wide.region_8.9_spmd, body=%wide.region_7.8_spmd.sunk | while | flops 99845 | bytes 931991 | solution.py:16
  726.0 34.1 %all-reduce.2.cloned.1.call-done = f32[8,2048]{1,0:T(8,128)} async-done(((f32[8,2048]{1,0:T(8,128)}), f32[8,2048]{1,0:T(8,128)}) %all-reduce.2.cloned.1.call-update) | async-done | bytes 65552 | tf_op jit(solution)/shard_map/psum | solution.py:121
  761.4 9.3 %all_gather.27 = bf16[64,2048]{1,0:T(8,128)(2,1)S(1)} all-gather(bf16[8,2048]{1,0:T(8,128)(2,1)S(1)} %multiply_convert_fusion), channel_id=1, replica_groups=mesh['req'=8,'tp'=4] {'req'}, dimensions={0}, use_global_device_ids=true | all-gather | bytes 294912 | tf_op jit(solution)/shard_map/all_gather | solution.py:125
  773.6 133.0 %reduce-scatter.2.cloned.1.call-done = f32[1,8,512]{2,1,0:T(8,128)} async-done(((f32[32,8,512]{2,1,0:T(8,128)}), f32[1,8,512]{2,1,0:T(8,128)}) %reduce-scatter.2.cloned.1.call-update) | async-done | bytes 16400 | tf_op jit(solution)/shard_map/reduce_scatter | solution.py:133
  (141 shorter events, 83.9 us)
Async XLA Ops:
  7.2 717.7 %copy-start = (bf16[512,2048]{1,0:T(8,128)(2,1)S(1)}, bf16[512,2048]{1,0:T(8,128)(2,1)}, u32[]{:S(2)}) copy-start(bf16[512,2048]{1,0:T(8,128)(2,1)} %param.22) | copy-start | bytes 6291460
  7.2 633.4 %copy-start.1 = (bf16[8,2048]{1,0:T(8,128)(2,1)S(1)}, bf16[8,2048]{1,0:T(8,128)(2,1)}, u32[]{:S(2)}) copy-start(bf16[8,2048]{1,0:T(8,128)(2,1)} %param.17) | copy-start | bytes 98308
  7.2 633.8 %copy-start.2 = (f32[2048]{0:T(1024)S(1)}, f32[2048]{0:T(1024)}, u32[]{:S(2)}) copy-start(f32[2048]{0:T(1024)} %param.18) | copy-start | bytes 24580
  7.2 706.2 %all-gather.6.cloned.1.call-start = ((), (), s32[]{:S(2)}) async-start(), calls=%async_computation.1 | async-start | bytes 1179648 | tf_op jit(solution)/shard_map/all_gather | solution.py:10
  689.4 70.6 %all-reduce.2.cloned.1.call-start = ((), (), s32[]{:S(2)}) async-start(), calls=%async_computation.2 | async-start | bytes 131072 | tf_op jit(solution)/shard_map/psum | solution.py:121
  708.9 17.0 %copy-start.3 = (bf16[8,512]{1,0:T(8,128)(2,1)}, bf16[8,512]{1,0:T(8,128)(2,1)S(1)}, u32[]{:S(2)}) copy-start(bf16[8,512]{1,0:T(8,128)(2,1)S(1)} %convolution_convert_fusion.1) | copy-start | bytes 24580
  711.5 49.8 %copy-start.4 = (f32[2048]{0:T(1024)S(1)}, f32[2048]{0:T(1024)}, u32[]{:S(2)}) copy-start(f32[2048]{0:T(1024)} %param.23) | copy-start | bytes 24580
  714.3 56.3 %copy-start.5 = (bf16[256,2048]{1,0:T(8,128)(2,1)S(1)}, bf16[256,2048]{1,0:T(8,128)(2,1)}, u32[]{:S(2)}) copy-start(bf16[256,2048]{1,0:T(8,128)(2,1)} %param.25) | copy-start | bytes 3145732
  725.9 180.7 %reduce-scatter.2.cloned.1.call-start = ((), (), s32[]{:S(2)}) async-start(), calls=%async_computation.3 | async-start | bytes 540672 | tf_op jit(solution)/shard_map/reduce_scatter | solution.py:133
Sparse Core Ops, SparseCore 0:
  689.6 23.7 all-gather.5
  726.1 33.9 all-reduce.1
  773.7 132.8 reduce-scatter.1
where the time goes:
time: 924 us; the launch traced here: 914 us
  other arithmetic  625 us (68%)
  waiting for transfers between devices  169 us (18%)
  local copies, waits for them, and re-layouts  51.2 us (6%)
  blocking collectives  36.7 us (4%)
  matrix products  17.6 us (2%)
  between operations  13.9 us (2%)
    select_n x14, other arithmetic, body(): slots = jnp.searchsorted(bounds, positions, side='right')  562 us
    reduce_scatter x1, waiting for transfers between devices, body(): lax.psum_scatter(term, ('req', 'tp'), scatter_dimension=0, tiled=True)  133 us
    select_n x1, other arithmetic, body(): row_owner = jnp.take(stream_order, slots)  39.9 us
    psum x1, waiting for transfers between devices, body(): middle = residual + lax.psum(partial_middle, 'tp')  34.1 us
    gather x28, local copies, waits for them, and re-layouts, body(): slots = jnp.searchsorted(bounds, positions, side='right')  20 us
  transfers between devices with their start and end apart: 3, of which 3 were waited for; matrix products, arithmetic and copies ran while one was open for 1% of the time, Pallas kernels for 0%

commit v1 on v0

v1 whole, which is shorter than its diff:
```python
import functools

import jax
import jax.numpy as jnp
from jax import lax
from jax.experimental import pallas as pl
from jax.experimental.pallas import tpu as pltpu
from jax.sharding import PartitionSpec as P

HEAD_DIM = 128
STATS = 128
NONE = -1e30
CHUNK = 1024
MIB = 1 << 20
VMEM = pl.BlockSpec(memory_space=pltpu.VMEM)
ANY = pl.BlockSpec(memory_space=pl.ANY)
F32 = jnp.float32
BF16 = jnp.bfloat16


def layer_norm(values, gain_vector):
    center = jnp.mean(values, axis=-1, keepdims=True)
    shifted = values - center
    spread = jnp.mean(shifted * shifted, axis=-1, keepdims=True)
    return shifted * lax.rsqrt(spread + 1e-05) * gain_vector


def dot(a, b):
    return jnp.dot(a, b, preferred_element_type=F32)


def stream_ranges(lens_row, order_row):
    n = lens_row.shape[1]
    down = lax.broadcasted_iota(jnp.int32, (n, n), 0)
    across = lax.broadcasted_iota(jnp.int32, (n, n), 1)
    lens = lens_row.astype(F32)
    eye = down == across
    lens_col = jnp.sum(jnp.where(eye, lens, 0.0), axis=1, keepdims=True)
    holds = order_row == down
    slot_len = jnp.sum(jnp.where(holds, lens_col, 0.0), axis=0, keepdims=True)
    slot_len_col = jnp.sum(jnp.where(eye, slot_len, 0.0), axis=1, keepdims=True)
    before = jnp.sum(jnp.where(down < across, slot_len_col, 0.0), axis=0, keepdims=True)
    first = jnp.sum(jnp.where(holds, before, 0.0), axis=1, keepdims=True)
    return first.astype(jnp.int32), (first + lens_col).astype(jnp.int32)


def attention_kernel(
    tokens_ref,
    gain_ref,
    lens_ref,
    order_ref,
    wq_hbm,
    wk_hbm,
    wv_hbm,
    keys_hbm,
    values_hbm,
    send_ref,
    new_keys_ref,
    new_values_ref,
    self_ref,
    wq,
    wk,
    wv,
    keys,
    values,
    scores,
    own,
    sems,
):
    requests = tokens_ref.shape[0]
    rows, head_width = keys.shape
    heads = head_width // HEAD_DIM
    chunks = rows // CHUNK
    parts, own_rows, _ = send_ref.shape
    me = lax.axis_index("req")

    def piece(ref, c):
        return ref.at[pl.ds(c * CHUNK, CHUNK)]

    copies = [pltpu.make_async_copy(wq_hbm, wq, sems.at[0])]
    copies += [
        pltpu.make_async_copy(piece(keys_hbm, c), piece(keys, c), sems.at[1 + c])
        for c in range(chunks)
    ]
    copies += [
        pltpu.make_async_copy(piece(values_hbm, c), piece(values, c), sems.at[1 + chunks + c])
        for c in range(chunks)
    ]
    copies.append(pltpu.make_async_copy(wk_hbm, wk, sems.at[1 + 2 * chunks]))
    copies.append(pltpu.make_async_copy(wv_hbm, wv, sems.at[2 + 2 * chunks]))
    for copy in copies:
        copy.start()
    normed = layer_norm(tokens_ref[...].astype(F32), gain_ref[...]).astype(BF16)
    first, last = stream_ranges(lens_ref[...], order_ref[...])
    first, last = first - me * rows, last - me * rows
    copies[0].wait()
    queries = (dot(normed, wq[...]) * HEAD_DIM ** (-0.5)).astype(BF16)

    lane_max = [jnp.full((requests, 128), NONE, F32)] * heads
    for c in range(chunks):
        copies[1 + c].wait()
        place = c * CHUNK + lax.broadcasted_iota(jnp.int32, (requests, CHUNK), 1)
        member = (place >= first) & (place < last)
        for h in range(heads):
            cols = slice(h * HEAD_DIM, (h + 1) * HEAD_DIM)
            score = lax.dot_general(
                queries[:, cols],
                keys[c * CHUNK : (c + 1) * CHUNK, cols],
                (((1,), (1,)), ((), ())),
                preferred_element_type=F32,
            )
            score = jnp.where(member, score, NONE)
            scores[h, :, c * CHUNK : (c + 1) * CHUNK] = score
            for t in range(CHUNK // 128):
                lane_max[h] = jnp.maximum(lane_max[h], score[:, t * 128 : (t + 1) * 128])

    peak = [jnp.max(lane_max[h], axis=1, keepdims=True) for h in range(heads)]
    mass = [jnp.zeros((requests, 128), F32)] * heads
    partial = [jnp.zeros((requests, HEAD_DIM), F32)] * heads
    for c in range(chunks):
        copies[1 + chunks + c].wait()
        for h in range(heads):
            cols = slice(h * HEAD_DIM, (h + 1) * HEAD_DIM)
            expo = jnp.exp(scores[h, :, c * CHUNK : (c + 1) * CHUNK] - peak[h])
            for t in range(CHUNK // 128):
                mass[h] = mass[h] + expo[:, t * 128 : (t + 1) * 128]
            partial[h] = partial[h] + dot(
                expo.astype(BF16), values[c * CHUNK : (c + 1) * CHUNK, cols]
            )
    lane = lax.broadcasted_iota(jnp.int32, (requests, STATS), 1)
    stats = jnp.zeros((requests, STATS), F32)
    for h in range(heads):
        stats = jnp.where(lane == h, peak[h], stats)
        stats = jnp.where(lane == heads + h, jnp.sum(mass[h], axis=1, keepdims=True), stats)
    for d in range(parts):
        r = slice(d * own_rows, (d + 1) * own_rows)
        for h in range(heads):
            send_ref[d, :, h * HEAD_DIM : (h + 1) * HEAD_DIM] = partial[h][r]
        send_ref[d, :, head_width : head_width + STATS] = stats[r]

    copies[1 + 2 * chunks].wait()
    own[0] = queries.astype(F32)
    own[1] = dot(normed, wk[...])
    copies[2 + 2 * chunks].wait()
    own[2] = dot(normed, wv[...])
    mine = pl.ds(pl.multiple_of(me * own_rows, own_rows), own_rows)
    new_keys = own[1, mine].astype(BF16)
    new_keys_ref[...] = new_keys
    new_values_ref[...] = own[2, mine].astype(BF16)
    product = own[0, mine] * new_keys.astype(F32)
    lane = lax.broadcasted_iota(jnp.int32, (own_rows, STATS), 1)
    self_score = jnp.zeros((own_rows, STATS), F32)
    for h in range(heads):
        one = jnp.sum(product[:, h * HEAD_DIM : (h + 1) * HEAD_DIM], axis=1, keepdims=True)
        self_score = jnp.where(lane == h, one, self_score)
    self_ref[...] = self_score


def attend(tokens, gain, lens, order, wq, wk, wv, keys, values, parts):
    requests, width = tokens.shape
    rows, head_width = keys.shape
    own_rows = requests // parts
    chunks = rows // CHUNK
    return pl.pallas_call(
        attention_kernel,
        out_shape=(
            jax.ShapeDtypeStruct((parts, own_rows, head_width + STATS), F32),
            jax.ShapeDtypeStruct((own_rows, head_width), BF16),
            jax.ShapeDtypeStruct((own_rows, head_width), BF16),
            jax.ShapeDtypeStruct((own_rows, STATS), F32),
        ),
        in_specs=[VMEM] * 4 + [ANY] * 5,
        out_specs=(VMEM,) * 4,
        scratch_shapes=[pltpu.VMEM((width, head_width), BF16)] * 3
        + [pltpu.VMEM((rows, head_width), BF16)] * 2
        + [
            pltpu.VMEM((head_width // HEAD_DIM, requests, rows), F32),
            pltpu.VMEM((3, requests, head_width), F32),
            pltpu.SemaphoreType.DMA((3 + 2 * chunks,)),
        ],
        compiler_params=pltpu.CompilerParams(vmem_limit_bytes=52 * MIB),
        name="attention",
    )(tokens, gain, lens, order, wq, wk, wv, keys, values)


def merge_kernel(recv_ref, self_ref, new_values_ref, wo_ref, out_ref):
    head_width = wo_ref.shape[0]
    heads = head_width // HEAD_DIM
    attended = []
    for h in range(heads):
        cols = slice(h * HEAD_DIM, (h + 1) * HEAD_DIM)
        peak = recv_ref[:, :, head_width + h : head_width + h + 1]
        mass = recv_ref[:, :, head_width + heads + h : head_width + heads + h + 1]
        self_score = self_ref[:, h : h + 1]
        top = jnp.maximum(jnp.max(peak, axis=0), self_score)
        scale = jnp.exp(peak - top[None])
        self_weight = jnp.exp(self_score - top)
        total = self_weight + jnp.sum(scale * mass, axis=0)
        summed = self_weight * new_values_ref[:, cols].astype(F32) + jnp.sum(
            scale * recv_ref[:, :, cols], axis=0
        )
        attended.append((summed / total).astype(BF16))
    out_ref[...] = dot(jnp.concatenate(attended, axis=1), wo_ref[...])


def merge(recv, self_score, new_values, wo):
    return pl.pallas_call(
        merge_kernel,
        out_shape=jax.ShapeDtypeStruct((recv.shape[1], wo.shape[1]), F32),
        in_specs=[VMEM] * 4,
        out_specs=VMEM,
        compiler_params=pltpu.CompilerParams(vmem_limit_bytes=16 * MIB),
        name="merge",
    )(recv, self_score, new_values, wo)


def middle_kernel(parts_ref, tokens_ref, gain_ref, normed_ref, columns_ref, mid):
    tp_count = parts_ref.shape[0]
    column_width = columns_ref.shape[1]
    total = parts_ref[0].astype(F32)
    for k in range(1, tp_count):
        total = total + parts_ref[k].astype(F32)
    middle = tokens_ref[...].astype(F32) + total
    mid[...] = middle
    normed_ref[...] = layer_norm(middle, gain_ref[...]).astype(BF16)
    offset = pl.multiple_of(lax.axis_index("tp") * column_width, column_width)
    columns_ref[...] = mid[:, pl.ds(offset, column_width)]


def middle(parts, tokens, gain):
    own_rows, width = tokens.shape
    return pl.pallas_call(
        middle_kernel,
        out_shape=(
            jax.ShapeDtypeStruct((own_rows, width), BF16),
            jax.ShapeDtypeStruct((own_rows, width // parts.shape[0]), F32),
        ),
        in_specs=[VMEM] * 3,
        out_specs=(VMEM,) * 2,
        scratch_shapes=[pltpu.VMEM((own_rows, width), F32)],
        compiler_params=pltpu.CompilerParams(vmem_limit_bytes=16 * MIB),
        name="middle",
    )(parts, tokens, gain)


def mlp_kernel(normed_ref, up_ref, down_ref, out_ref):
    blocks, own_rows, column_width = out_ref.shape
    req_count = normed_ref.shape[0] // own_rows
    tp_count = blocks // req_count
    up = dot(normed_ref[...], up_ref[...])
    activation = (0.5 * up * (1.0 + lax.erf(up * 0.5**0.5))).astype(BF16)
    for t in range(tp_count):
        term = dot(activation, down_ref[:, t * column_width : (t + 1) * column_width])
        for a in range(req_count):
            out_ref[a * tp_count + t] = term[a * own_rows : (a + 1) * own_rows].astype(
                out_ref.dtype
            )


def mlp(normed, up, down, req_count, tp_count):
    requests, width = normed.shape
    return pl.pallas_call(
        mlp_kernel,
        out_shape=jax.ShapeDtypeStruct(
            (req_count * tp_count, requests // req_count, width // tp_count), BF16
        ),
        in_specs=[VMEM] * 3,
        out_specs=VMEM,
        compiler_params=pltpu.CompilerParams(vmem_limit_bytes=16 * MIB),
        name="mlp",
    )(normed, up, down)


def finish_kernel(recv_ref, columns_ref, out_ref):
    total = recv_ref[0].astype(F32)
    for k in range(1, recv_ref.shape[0]):
        total = total + recv_ref[k].astype(F32)
    out_ref[...] = (columns_ref[...] + total).astype(BF16)


def finish(recv, columns):
    return pl.pallas_call(
        finish_kernel,
        out_shape=jax.ShapeDtypeStruct(columns.shape, BF16),
        in_specs=[VMEM] * 2,
        out_specs=VMEM,
        compiler_params=pltpu.CompilerParams(vmem_limit_bytes=16 * MIB),
        name="finish",
    )(recv, columns)


def body(
    tokens,
    first_gain,
    query_weight,
    key_weight,
    value_weight,
    out_weight,
    second_gain,
    up_weight,
    down_weight,
    cache_keys,
    cache_values,
    lengths,
    stream_order,
):
    req_count = lax.axis_size("req")
    tp_count = lax.axis_size("tp")
    all_tokens = lax.all_gather(tokens, "req", axis=0, tiled=True)
    send, new_keys, new_values, self_score = attend(
        all_tokens,
        first_gain[None],
        lengths[None],
        stream_order[None],
        query_weight,
        key_weight,
        value_weight,
        cache_keys,
        cache_values,
        req_count,
    )
    recv = lax.all_to_all(send, "req", split_axis=0, concat_axis=0, tiled=True)
    part = merge(recv, self_score, new_values, out_weight)
    parts = lax.all_gather(part, "tp", axis=0)
    normed, columns = middle(parts, tokens, second_gain[None])
    all_normed = lax.all_gather(normed, "req", axis=0, tiled=True)
    term = mlp(all_normed, up_weight, down_weight, req_count, tp_count)
    terms = lax.all_to_all(term, ("req", "tp"), split_axis=0, concat_axis=0, tiled=True)
    hidden = finish(terms, columns)
    return (hidden, new_keys, new_values)


def solution(mesh):
    return jax.shard_map(
        body,
        mesh=mesh,
        in_specs=(
            P("req", None),
            P(),
            P(None, "tp"),
            P(None, "tp"),
            P(None, "tp"),
            P("tp", None),
            P(),
            P(None, ("req", "tp")),
            P(("req", "tp"), None),
            P("req", "tp"),
            P("req", "tp"),
            P(),
            P(),
        ),
        out_specs=(P("req", "tp"), P("req", "tp"), P("req", "tp")),
        check_vma=False,
    )
```

time: 924 us -> 70.8 us (0.08)
  other arithmetic: 625 us -> 0 us
  waiting for transfers between devices: 169 us -> 0 us
  local copies, waits for them, and re-layouts: 51.2 us -> 2.73 us
  blocking collectives: 36.7 us -> 57.3 us
  matrix products: 17.6 us -> 0 us
  between operations: 13.9 us -> 0.68 us
  Pallas kernels: 0 us -> 9.77 us
    select_n x16 -> x0, other arithmetic: 603 us -> none  [the longest x14 562 us: body(): slots = jnp.searchsorted(bounds, positions, side='right')]
    reduce_scatter x1 -> x0, waiting for transfers between devices: 133 us -> none  [body(): lax.psum_scatter(term, ('req', 'tp'), scatter_dimension=0, tiled=True)]
    psum x1 -> x0, waiting for transfers between devices: 34.1 us -> none  [body(): middle = residual + lax.psum(partial_middle, 'tp')]
    gather x33 -> x0, local copies, waits for them, and re-layouts: 29.2 us -> none  [the longest x28 20 us: body(): slots = jnp.searchsorted(bounds, positions, side='right')]
    all_to_all x0 -> x2, blocking collectives: none -> 23.6 us  [the longest x1 15.1 us: body(): lax.all_to_all(term, ('req', 'tp'), split_axis=0, concat_axis=0, tiled=True)]
    dot_general x8 -> x0, matrix products: 17.6 us -> none  [the longest x1 3.27 us: body(): jnp.dot(select, every_query, preferred_element_type=jnp.float32)]
    unnamed x3 -> x0, other arithmetic: 10.4 us -> none
    pallas_call x0 -> x5, Pallas kernels: none -> 9.77 us  [the longest x1 7.6 us: attend(): pl.pallas_call(attention_kernel, out_shape=(jax.ShapeDtypeStruct((parts,...]
  transfers between devices with their start and end apart: 3 -> 0, of which waited for: 3 -> 0; matrix products, arithmetic and copies ran while one was open for 1% -> 0% of each run, Pallas kernels for 0% -> 0%
where the time goes in v1:
time: 70.8 us; the launch traced here: 70.4 us
  blocking collectives  57.3 us (81%)
  Pallas kernels  9.77 us (14%)
  local copies, waits for them, and re-layouts  2.73 us (4%)
    all_to_all x1, blocking collectives, body(): lax.all_to_all(term, ('req', 'tp'), split_axis=0, concat_axis=0, tiled=True)  15.1 us
    all_gather x1, blocking collectives, body(): parts = lax.all_gather(part, 'tp', axis=0)  14.1 us
    all_gather x1, blocking collectives, body(): all_tokens = lax.all_gather(tokens, 'req', axis=0, tiled=True)  11 us
    all_gather x1, blocking collectives, body(): all_normed = lax.all_gather(normed, 'req', axis=0, tiled=True)  8.57 us
    all_to_all x1, blocking collectives, body(): recv = lax.all_to_all(send, 'req', split_axis=0, concat_axis=0, tiled=True)  8.56 us
    pallas_call x1, Pallas kernels, attend(): pl.pallas_call(attention_kernel, out_shape=(jax.ShapeDtypeStruct((parts,...  7.6 us
    unnamed x18, local copies, waits for them, and re-layouts  2.73 us

profile of v1, /device:TPU:0, one launch (start us, length us, event | category | flops | bytes accessed | tf_op | source)
XLA Modules:
  0.0 70.4 jit_solution(17832427539967526792)
XLA Ops:
  0.6 11.0 %all_gather.12.tokens_ref = bf16[64,2048]{1,0:T(8,128)(2,1)S(1)} all-gather(bf16[8,2048]{1,0:T(8,128)(2,1)} %tokens_ref.1), channel_id=1, replica_groups=mesh['req'=8,'tp'=4] {'req'}, dimensions={0}, use_global_device_ids=true | all-gather | bytes 294912 | tf_op jit(solution)/shard_map/all_gather | solution.py:309
  11.6 0.0 copy-start.4
  11.6 0.7 copy-done.4
  12.3 0.0 copy-start.7
  12.3 0.7 copy-done.7
  13.0 0.7 copy-done.8
  13.6 7.6 %attention.1 = (f32[8,8,640]{2,1,0:T(8,128)S(1)}, bf16[8,512]{1,0:T(8,128)(2,1)}, bf16[8,512]{1,0:T(8,128)(2,1)}, f32[8,128]{1,0:T(8,128)S(1)}) custom-call(bf16[64,2048]{1,0:T(8,128)(2,1)S(1)} %all_gather.12.tokens_ref, f32[1,2048]{1,0:T(1,128)S(1)} %bitcast.6, s32[1,64]{1,0:T(1,128)S(1)} %bitcast.8, s32[1,64]{1,0:T(1,128)S(1)} %bitcast.9, ...), custom_call_target="tpu_custom_call" | custom-call | tf_op jit(solution)/shard_map/attention/pallas_call | solution.py:164
  21.2 0.0 copy-start.3
  21.2 0.0 copy-start.1
  21.3 0.0 copy-start.2
  21.3 8.6 %all_to_all.10.recv_ref = f32[8,8,640]{2,1,0:T(8,128)S(1)} all-to-all(f32[8,8,640]{2,1,0:T(8,128)S(1)} %get-tuple-element.9), channel_id=1, replica_groups=mesh['req'=8,'tp'=4] {'req'}, dimensions={0} | all-to-all | bytes 327680 | tf_op jit(solution)/shard_map/all_to_all | solution.py:322
  29.8 0.0 copy-done
  29.8 0.7 copy-done.5
  30.5 0.5 merge.1
  31.0 14.1 %all-gather = f32[32,2048]{1,0:T(8,128)S(1)} all-gather(f32[8,2048]{1,0:T(8,128)S(1)} %merge.1), channel_id=2, replica_groups=mesh['req'=8,'tp'=4] {'tp'}, dimensions={0}, use_global_device_ids=true | all-gather | bytes 327680 | tf_op jit(solution)/shard_map/all_gather | solution.py:324
  45.1 0.0 copy-done.6
  45.1 0.0 copy-done.3
  45.1 0.2 middle.1
  45.3 8.6 %all_gather.15.normed_ref = bf16[64,2048]{1,0:T(8,128)(2,1)S(1)} all-gather(bf16[8,2048]{1,0:T(8,128)(2,1)S(1)} %get-tuple-element.12), channel_id=1, replica_groups=mesh['req'=8,'tp'=4] {'req'}, dimensions={0}, use_global_device_ids=true | all-gather | bytes 294912 | tf_op jit(solution)/shard_map/all_gather | solution.py:326
  53.9 0.0 copy-done.1
  53.9 0.0 copy-done.2
  53.9 0.8 %mlp.1 = bf16[32,8,512]{2,1,0:T(8,128)(2,1)S(1)} custom-call(bf16[64,2048]{1,0:T(8,128)(2,1)S(1)} %all_gather.15.normed_ref, bf16[2048,256]{1,0:T(8,128)(2,1)S(1)} %copy-done.1, bf16[256,2048]{1,0:T(8,128)(2,1)S(1)} %copy-done.2), custom_call_target="tpu_custom_call" | custom-call | tf_op jit(solution)/shard_map/mlp/pallas_call | solution.py:262
  54.7 15.1 %all_to_all.11.recv_ref = bf16[32,8,512]{2,1,0:T(8,128)(2,1)S(1)} all-to-all(bf16[32,8,512]{2,1,0:T(8,128)(2,1)S(1)} %mlp.1), channel_id=1, replica_groups=mesh['req'=8,'tp'=4] {'req','tp'}, dimensions={0} | all-to-all | bytes 524288 | tf_op jit(solution)/shard_map/all_to_all | solution.py:328
  69.8 0.6 finish.1
  (4 shorter events, 0.0 us)
Async XLA Ops:
  11.6 0.7 copy-start.4
  12.3 0.7 copy-start.7
  13.0 0.7 copy-start.8
  13.6 16.2 %copy-start = (bf16[512,2048]{1,0:T(8,128)(2,1)S(1)}, bf16[512,2048]{1,0:T(8,128)(2,1)}, u32[]{:S(2)}) copy-start(bf16[512,2048]{1,0:T(8,128)(2,1)} %wo_ref.1) | copy-start | bytes 6291460
  13.6 31.5 %copy-start.6 = (f32[2048]{0:T(1024)S(1)}, f32[2048]{0:T(1024)}, u32[]{:S(2)}) copy-start(f32[2048]{0:T(1024)} %param.19) | copy-start | bytes 24580
  21.2 23.9 %copy-start.3 = (bf16[8,2048]{1,0:T(8,128)(2,1)S(1)}, bf16[8,2048]{1,0:T(8,128)(2,1)}, u32[]{:S(2)}) copy-start(bf16[8,2048]{1,0:T(8,128)(2,1)} %tokens_ref.1) | copy-start | bytes 98308
  21.2 32.7 %copy-start.1 = (bf16[2048,256]{1,0:T(8,128)(2,1)S(1)}, bf16[2048,256]{1,0:T(8,128)(2,1)}, u32[]{:S(2)}) copy-start(bf16[2048,256]{1,0:T(8,128)(2,1)} %up_ref.1) | copy-start | bytes 3145732
  21.3 32.7 %copy-start.2 = (bf16[256,2048]{1,0:T(8,128)(2,1)S(1)}, bf16[256,2048]{1,0:T(8,128)(2,1)}, u32[]{:S(2)}) copy-start(bf16[256,2048]{1,0:T(8,128)(2,1)} %down_ref.1) | copy-start | bytes 3145732
  29.8 0.7 copy-start.5

commit v2 on v1

v2 whole, which is shorter than its diff:
```python
import functools

import jax
import jax.numpy as jnp
from jax import lax
from jax.experimental import pallas as pl
from jax.experimental.pallas import tpu as pltpu
from jax.sharding import PartitionSpec as P

HEAD_DIM = 128
STATS = 128
NONE = -1e30
CHUNK = 1024
MIB = 1 << 20
LIMIT = 8
VMEM = pl.BlockSpec(memory_space=pltpu.VMEM)
ANY = pl.BlockSpec(memory_space=pl.ANY)
F32 = jnp.float32
BF16 = jnp.bfloat16


def layer_norm(values, gain_vector):
    center = jnp.mean(values, axis=-1, keepdims=True)
    shifted = values - center
    spread = jnp.mean(shifted * shifted, axis=-1, keepdims=True)
    return shifted * lax.rsqrt(spread + 1e-05) * gain_vector


def dot(a, b):
    return jnp.dot(a, b, preferred_element_type=F32)


def stream_ranges(lens_row, order_row):
    n = lens_row.shape[1]
    down = lax.broadcasted_iota(jnp.int32, (n, n), 0)
    across = lax.broadcasted_iota(jnp.int32, (n, n), 1)
    lens = lens_row.astype(F32)
    eye = down == across
    lens_col = jnp.sum(jnp.where(eye, lens, 0.0), axis=1, keepdims=True)
    holds = order_row == down
    slot_len = jnp.sum(jnp.where(holds, lens_col, 0.0), axis=0, keepdims=True)
    slot_len_col = jnp.sum(jnp.where(eye, slot_len, 0.0), axis=1, keepdims=True)
    before = jnp.sum(jnp.where(down < across, slot_len_col, 0.0), axis=0, keepdims=True)
    first = jnp.sum(jnp.where(holds, before, 0.0), axis=1, keepdims=True)
    return first.astype(jnp.int32), (first + lens_col).astype(jnp.int32)


def swap(x, axis, offset):
    n = lax.axis_size(axis)
    return lax.ppermute(x, axis, [(i, i ^ offset) for i in range(n)])


def exchange_order(n):
    return list(range(0, n, 2)) + list(range(1, n, 2))


def gather_far(x):
    return [swap(x, "req", m) for m in range(2, lax.axis_size("req"), 2)]


def gather_near(x, far):
    return [x[None]] + [part[None] for part in far] + [swap(jnp.stack([x] + far), "req", 1)]


def scatter_req(groups):
    n = lax.axis_size("req")
    got = [groups[0]] + [swap(groups[c], "req", 2 * c) for c in range(1, n // 2)]
    return got + [swap(jnp.stack([part[1] for part in got]), "req", 1)]


def landed_blocks(n):
    return [(c, 0) for c in range(n // 2)] + [(n // 2, c) for c in range(n // 2)]


def stacked(refs):
    blocks = [ref[k].astype(F32) for ref in refs for k in range(ref.shape[0])]
    return jnp.concatenate(blocks, axis=0)


def load_kernel(*refs):
    n = 8
    sources, targets = refs[:n], refs[n : 2 * n - 2]
    bounds_ref, lens, order, sems = refs[2 * n - 2 :]
    targets = (lens, order) + targets
    copies = [
        pltpu.make_async_copy(source, target, sems.at[k])
        for k, (source, target) in enumerate(zip(sources, targets))
    ]
    for copy in copies:
        copy.start()
    copies[0].wait()
    copies[1].wait()
    first, last = stream_ranges(lens[...], order[...])
    bounds_ref[0] = jnp.broadcast_to(first, bounds_ref.shape[1:])
    bounds_ref[1] = jnp.broadcast_to(last, bounds_ref.shape[1:])
    for copy in copies[2:]:
        copy.wait()


def load(lens, order, *arrays):
    sources = [pltpu.with_memory_space_constraint(x, pltpu.HBM) for x in (lens, order) + arrays]
    return pl.pallas_call(
        load_kernel,
        out_shape=[pltpu.VMEM(x.shape, x.dtype) for x in arrays]
        + [pltpu.VMEM((2, lens.shape[1], 128), jnp.int32)],
        in_specs=[ANY] * len(sources),
        out_specs=[VMEM] * (len(arrays) + 1),
        scratch_shapes=[
            pltpu.VMEM(lens.shape, jnp.int32),
            pltpu.VMEM(order.shape, jnp.int32),
            pltpu.SemaphoreType.DMA((len(sources),)),
        ],
        compiler_params=pltpu.CompilerParams(vmem_limit_bytes=LIMIT * MIB),
        cost_estimate=pl.CostEstimate(
            flops=0, bytes_accessed=2 * sum(x.size for x in arrays), transcendentals=0
        ),
        name="load",
    )(*sources)


def attention_kernel(req_count, n_tokens, *refs):
    token_refs, refs = refs[:n_tokens], refs[n_tokens:]
    gain_ref, bounds, wq, wk, wv, keys, values_hbm = refs[:7]
    groups = req_count // 2
    send_refs, refs = refs[7 : 7 + groups], refs[7 + groups :]
    new_keys_ref, new_values_ref, self_ref, values, scores, sems = refs
    rows, head_width = keys.shape
    heads = head_width // HEAD_DIM
    chunks = rows // CHUNK
    own_rows = new_keys_ref.shape[0]
    requests = own_rows * req_count
    me = lax.axis_index("req")

    copies = []
    for c in range(chunks):
        part = pl.ds(c * CHUNK, CHUNK)
        copies.append(pltpu.make_async_copy(values_hbm.at[part], values.at[part], sems.at[c]))
    for copy in copies:
        copy.start()
    normed = layer_norm(stacked(token_refs), gain_ref[...]).astype(BF16)
    owners = [
        pl.ds(pl.multiple_of((me ^ offset) * own_rows, own_rows), own_rows)
        for offset in exchange_order(req_count)
    ]
    first = jnp.concatenate([bounds[0, owner][:, :1] for owner in owners], axis=0) - me * rows
    last = jnp.concatenate([bounds[1, owner][:, :1] for owner in owners], axis=0) - me * rows
    queries = (dot(normed, wq[...]) * HEAD_DIM ** (-0.5)).astype(BF16)

    lane_max = [jnp.full((requests, 128), NONE, F32)] * heads
    for c in range(chunks):
        place = c * CHUNK + lax.broadcasted_iota(jnp.int32, (requests, CHUNK), 1)
        member = (place >= first) & (place < last)
        for h in range(heads):
            cols = slice(h * HEAD_DIM, (h + 1) * HEAD_DIM)
            score = lax.dot_general(
                queries[:, cols],
                keys[c * CHUNK : (c + 1) * CHUNK, cols],
                (((1,), (1,)), ((), ())),
                preferred_element_type=F32,
            )
            score = jnp.where(member, score, NONE)
            scores[h, :, c * CHUNK : (c + 1) * CHUNK] = score
            for t in range(CHUNK // 128):
                lane_max[h] = jnp.maximum(lane_max[h], score[:, t * 128 : (t + 1) * 128])

    peak = [jnp.max(lane_max[h], axis=1, keepdims=True) for h in range(heads)]
    mass = [jnp.zeros((requests, 128), F32)] * heads
    partial = [jnp.zeros((requests, HEAD_DIM), F32)] * heads
    for c in range(chunks):
        copies[c].wait()
        for h in range(heads):
            cols = slice(h * HEAD_DIM, (h + 1) * HEAD_DIM)
            expo = jnp.exp(scores[h, :, c * CHUNK : (c + 1) * CHUNK] - peak[h])
            for t in range(CHUNK // 128):
                mass[h] = mass[h] + expo[:, t * 128 : (t + 1) * 128]
            partial[h] = partial[h] + dot(
                expo.astype(BF16), values[c * CHUNK : (c + 1) * CHUNK, cols]
            )
    lane = lax.broadcasted_iota(jnp.int32, (requests, STATS), 1)
    stats = jnp.zeros((requests, STATS), F32)
    for h in range(heads):
        stats = jnp.where(lane == h, peak[h], stats)
        stats = jnp.where(lane == heads + h, jnp.sum(mass[h], axis=1, keepdims=True), stats)
    for c, ref in enumerate(send_refs):
        for k, block in enumerate((c, groups + c)):
            r = slice(block * own_rows, (block + 1) * own_rows)
            for h in range(heads):
                ref[k, :, h * HEAD_DIM : (h + 1) * HEAD_DIM] = partial[h][r]
            ref[k, :, head_width : head_width + STATS] = stats[r]

    mine = normed[: max(own_rows, 16)]
    new_keys = dot(mine, wk[...])[:own_rows].astype(BF16)
    new_values = dot(mine, wv[...])[:own_rows].astype(BF16)
    new_keys_ref[...] = new_keys
    new_values_ref[...] = new_values
    product = queries[: max(own_rows, 16)].astype(F32)[:own_rows] * new_keys.astype(F32)
    lane = lax.broadcasted_iota(jnp.int32, (own_rows, STATS), 1)
    self_score = jnp.zeros((own_rows, STATS), F32)
    for h in range(heads):
        one = jnp.sum(product[:, h * HEAD_DIM : (h + 1) * HEAD_DIM], axis=1, keepdims=True)
        self_score = jnp.where(lane == h, one, self_score)
    self_ref[:, :head_width] = new_values.astype(F32)
    self_ref[:, head_width:] = self_score


def attend(tokens, gain, bounds, wq, wk, wv, keys, values):
    req_count = lax.axis_size("req")
    own_rows, width = tokens[0].shape[1:]
    requests = own_rows * req_count
    rows, head_width = keys.shape
    heads = head_width // HEAD_DIM
    groups = req_count // 2
    *sends, new_keys, new_values, self_part = pl.pallas_call(
        functools.partial(attention_kernel, req_count, len(tokens)),
        out_shape=[jax.ShapeDtypeStruct((2, own_rows, head_width + STATS), F32)] * groups
        + [jax.ShapeDtypeStruct((own_rows, head_width), BF16)] * 2
        + [jax.ShapeDtypeStruct((own_rows, head_width + STATS), F32)],
        in_specs=[VMEM] * (len(tokens) + 6) + [ANY],
        out_specs=[VMEM] * (groups + 3),
        scratch_shapes=[
            pltpu.VMEM((rows, head_width), BF16),
            pltpu.VMEM((heads, requests, rows), F32),
            pltpu.SemaphoreType.DMA((rows // CHUNK,)),
        ],
        compiler_params=pltpu.CompilerParams(vmem_limit_bytes=heads * requests * rows * 4 + (4 + LIMIT) * MIB),
        name="attention",
    )(
        *tokens,
        gain,
        bounds,
        wq,
        wk,
        wv,
        keys,
        pltpu.with_memory_space_constraint(values, pltpu.HBM),
    )
    return sends, new_keys, new_values, self_part


def merge_kernel(places, n_landed, *refs):
    landed, (self_ref, wo_ref, part_ref, sent_ref) = refs[:n_landed], refs[n_landed:]
    head_width = wo_ref.shape[0]
    heads = head_width // HEAD_DIM
    attended = []
    for h in range(heads):
        cols = slice(h * HEAD_DIM, (h + 1) * HEAD_DIM)
        at_peak = slice(head_width + h, head_width + h + 1)
        at_mass = slice(head_width + heads + h, head_width + heads + h + 1)
        self_score = self_ref[:, at_peak]
        peaks = [landed[a][k, :, at_peak] for a, k in places]
        top = functools.reduce(jnp.maximum, peaks, self_score)
        total = jnp.exp(self_score - top)
        summed = total * self_ref[:, cols]
        for (a, k), peak in zip(places, peaks):
            scale = jnp.exp(peak - top)
            total = total + scale * landed[a][k, :, at_mass]
            summed = summed + scale * landed[a][k, :, cols]
        attended.append((summed / total).astype(BF16))
    part = dot(jnp.concatenate(attended, axis=1), wo_ref[...])
    part_ref[...] = part
    sent_ref[...] = part.astype(BF16)


def merge(landed, self_part, wo):
    shape = (self_part.shape[0], wo.shape[1])
    return pl.pallas_call(
        functools.partial(merge_kernel, landed_blocks(lax.axis_size("req")), len(landed)),
        out_shape=(jax.ShapeDtypeStruct(shape, F32), jax.ShapeDtypeStruct(shape, BF16)),
        in_specs=[VMEM] * (len(landed) + 2),
        out_specs=(VMEM,) * 2,
        compiler_params=pltpu.CompilerParams(vmem_limit_bytes=16 * MIB),
        name="merge",
    )(*landed, self_part, wo)


def middle_kernel(*refs):
    part_ref, *others, tokens_ref, gain_ref, normed_ref, columns_ref, mid = refs
    column_width = columns_ref.shape[1]
    total = part_ref[...]
    for other in others:
        total = total + other[...].astype(F32)
    middle = tokens_ref[...].astype(F32) + total
    mid[...] = middle
    normed_ref[...] = layer_norm(middle, gain_ref[...]).astype(BF16)
    offset = pl.multiple_of(lax.axis_index("tp") * column_width, column_width)
    columns_ref[...] = mid[:, pl.ds(offset, column_width)]


def middle(part, others, tokens, gain):
    own_rows, width = tokens.shape
    return pl.pallas_call(
        middle_kernel,
        out_shape=(
            jax.ShapeDtypeStruct((own_rows, width), BF16),
            jax.ShapeDtypeStruct((own_rows, width // (1 + len(others))), F32),
        ),
        in_specs=[VMEM] * (3 + len(others)),
        out_specs=(VMEM,) * 2,
        scratch_shapes=[pltpu.VMEM((own_rows, width), F32)],
        compiler_params=pltpu.CompilerParams(vmem_limit_bytes=16 * MIB),
        name="middle",
    )(part, *others, tokens, gain)


def mlp_kernel(req_count, *refs):
    *normed_refs, up_ref, down_ref, out_ref = refs
    blocks, own_rows, column_width = out_ref.shape
    tp_count = blocks // req_count
    me = lax.axis_index("req")
    up = dot(stacked(normed_refs).astype(BF16), up_ref[...])
    activation = (0.5 * up * (1.0 + lax.erf(up * 0.5**0.5))).astype(BF16)
    for t in range(tp_count):
        term = dot(activation, down_ref[:, t * column_width : (t + 1) * column_width])
        for k, offset in enumerate(exchange_order(req_count)):
            out_ref[(me ^ offset) * tp_count + t] = term[
                k * own_rows : (k + 1) * own_rows
            ].astype(BF16)


def mlp(normed, up, down):
    req_count, tp_count = lax.axis_size("req"), lax.axis_size("tp")
    own_rows, width = normed[0].shape[1:]
    return pl.pallas_call(
        functools.partial(mlp_kernel, req_count),
        out_shape=jax.ShapeDtypeStruct(
            (req_count * tp_count, own_rows, width // tp_count), BF16
        ),
        in_specs=[VMEM] * (len(normed) + 2),
        out_specs=VMEM,
        compiler_params=pltpu.CompilerParams(vmem_limit_bytes=16 * MIB),
        name="mlp",
    )(*normed, up, down)


def finish_kernel(recv_ref, columns_ref, out_ref):
    total = recv_ref[0].astype(F32)
    for k in range(1, recv_ref.shape[0]):
        total = total + recv_ref[k].astype(F32)
    out_ref[...] = (columns_ref[...] + total).astype(BF16)


def finish(recv, columns):
    return pl.pallas_call(
        finish_kernel,
        out_shape=jax.ShapeDtypeStruct(columns.shape, BF16),
        in_specs=[VMEM] * 2,
        out_specs=VMEM,
        compiler_params=pltpu.CompilerParams(vmem_limit_bytes=16 * MIB),
        name="finish",
    )(recv, columns)


def body(
    tokens,
    first_gain,
    query_weight,
    key_weight,
    value_weight,
    out_weight,
    second_gain,
    up_weight,
    down_weight,
    cache_keys,
    cache_values,
    lengths,
    stream_order,
):
    far = gather_far(tokens)
    tokens, gain, wq, wk, wv, keys, bounds = load(
        lengths[None],
        stream_order[None],
        tokens,
        first_gain[None],
        query_weight,
        key_weight,
        value_weight,
        cache_keys,
    )
    sends, new_keys, new_values, self_part = attend(
        gather_near(tokens, far), gain, bounds, wq, wk, wv, keys, cache_values
    )
    part, sent = merge(scatter_req(sends), self_part, out_weight)
    others = [swap(sent, "tp", m) for m in range(1, lax.axis_size("tp"))]
    normed, columns = middle(part, others, tokens, second_gain[None])
    term = mlp(gather_near(normed, gather_far(normed)), up_weight, down_weight)
    terms = lax.all_to_all(term, ("req", "tp"), split_axis=0, concat_axis=0, tiled=True)
    hidden = finish(terms, columns)
    return (hidden, new_keys, new_values)


def solution(mesh):
    return jax.shard_map(
        body,
        mesh=mesh,
        in_specs=(
            P("req", None),
            P(),
            P(None, "tp"),
            P(None, "tp"),
            P(None, "tp"),
            P("tp", None),
            P(),
            P(None, ("req", "tp")),
            P(("req", "tp"), None),
            P("req", "tp"),
            P("req", "tp"),
            P(),
            P(),
        ),
        out_specs=(P("req", "tp"), P("req", "tp"), P("req", "tp")),
        check_vma=False,
    )
```

time: 70.8 us -> 57.2 us (0.81)
  blocking collectives: 57.3 us -> 13.3 us
  starting transfers between devices: 0 us -> 16.3 us
  waiting for transfers between devices: 0 us -> 15.3 us
  local copies, waits for them, and re-layouts: 2.73 us -> 0.03 us
  Pallas kernels: 9.77 us -> 11.3 us
    all_gather x3 -> x0, blocking collectives: 33.6 us -> none  [the longest x1 14.1 us: body(): parts = lax.all_gather(part, 'tp', axis=0)]
    ppermute x0 -> x15, starting transfers between devices: none -> 16.3 us  [swap(): return lax.ppermute(x, axis, [(i, i ^ offset) for i in range(n)])]
    ppermute x0 -> x15, waiting for transfers between devices: none -> 15.3 us  [swap(): return lax.ppermute(x, axis, [(i, i ^ offset) for i in range(n)])]
    all_to_all x1 -> x0, blocking collectives: 8.56 us -> none  [body(): recv = lax.all_to_all(send, 'req', split_axis=0, concat_axis=0, tiled=True)]
    unnamed x18 -> x8, local copies, waits for them, and re-layouts: 2.73 us -> 0.02 us
    all_to_all x1, blocking collectives: 15.1 us -> 13.3 us  [body(): lax.all_to_all(term, ('req', 'tp'), split_axis=0, concat_axis=0, tiled=True)]
    pallas_call x3 -> x4, Pallas kernels: 8.91 us -> 10.5 us  [the longest x1 4.97 us: attend(): pl.pallas_call(functools.partial(attention_kernel, req_count, len(tokens)...]
  transfers between devices with their start and end apart: 0 -> 15, of which waited for: 0 -> 10; matrix products, arithmetic and copies ran while one was open for 0% -> 0% of each run, Pallas kernels for 0% -> 7%
where the time goes in v2:
time: 57.2 us; the launch traced here: 57 us
  starting transfers between devices  16.3 us (28%)
  waiting for transfers between devices  15.3 us (27%)
  blocking collectives  13.3 us (23%)
  Pallas kernels  11.3 us (20%)
  between operations  0.76 us (1%)
    ppermute x15, starting transfers between devices, swap(): return lax.ppermute(x, axis, [(i, i ^ offset) for i in range(n)])  16.3 us
    ppermute x15, waiting for transfers between devices, swap(): return lax.ppermute(x, axis, [(i, i ^ offset) for i in range(n)])  15.3 us
    all_to_all x1, blocking collectives, body(): lax.all_to_all(term, ('req', 'tp'), split_axis=0, concat_axis=0, tiled=True)  13.3 us
    pallas_call x1, Pallas kernels, attend(): pl.pallas_call(functools.partial(attention_kernel, req_count, len(tokens)...  4.97 us
    pallas_call x1, Pallas kernels, load(): pl.pallas_call(load_kernel, out_shape=[pltpu.VMEM(x.shape, x.dtype) for x...  4.19 us
  transfers between devices with their start and end apart: 15, of which 10 were waited for; matrix products, arithmetic and copies ran while one was open for 0% of the time, Pallas kernels for 7%

profile of v2, /device:TPU:0, one launch (start us, length us, event | category | flops | bytes accessed | tf_op | source)
XLA Modules:
  0.0 57.0 jit_solution(10313022064729938120)
XLA Ops:
  0.6 3.0 %collective-permute-start = (bf16[8,2048]{1,0:T(8,128)(2,1)}, bf16[8,2048]{1,0:T(8,128)(2,1)S(1)}, u32[]{:S(2)}, u32[]{:S(2)}) collective-permute-start(bf16[8,2048]{1,0:T(8,128)(2,1)} %refs_2_.1), channel_id=1, source_target_pairs={{0,8},{4,12},{8,0},{12,4},{16,24},{20,28},{24,16},{28,20},{1,9},{5... | collective-permute-start | bytes 98312 | tf_op jit(solution)/shard_map/ppermute | solution.py:50
  3.6 1.5 %collective-permute-start.2 = (bf16[8,2048]{1,0:T(8,128)(2,1)}, bf16[8,2048]{1,0:T(8,128)(2,1)S(1)}, u32[]{:S(2)}, u32[]{:S(2)}) collective-permute-start(bf16[8,2048]{1,0:T(8,128)(2,1)} %refs_2_.1), channel_id=1, source_target_pairs={{0,24},{4,28},{8,16},{12,20},{16,8},{20,12},{24,0},{28,4},{1,25},{... | collective-permute-start | bytes 98312 | tf_op jit(solution)/shard_map/ppermute | solution.py:50
  5.2 4.2 %load.1 = (bf16[8,2048]{1,0:T(8,128)(2,1)S(1)}, f32[1,2048]{1,0:T(1,128)S(1)}, bf16[2048,512]{1,0:T(8,128)(2,1)S(1)}, bf16[2048,512]{1,0:T(8,128)(2,1)S(1)}, bf1...) custom-call(s32[1,64]{1,0:T(1,128)} %bitcast.30, s32[1,64]{1,0:T(1,128)} %bitcast.31, ...), custom_call_target="tpu_custom_call" | custom-call | bytes 10522624 | tf_op jit(solution)/shard_map/load/pallas_call | solution.py:102
  9.5 1.3 %collective-permute-done.3.refs_4_ = bf16[4,8,2048]{2,1,0:T(8,128)(2,1)S(1)} collective-permute-done((bf16[4,8,2048]{2,1,0:T(8,128)(2,1)S(1)}, bf16[4,8,2048]{2,1,0:T(8,128)(2,1)S(1)}, u32[]{:S(2)}, u32[]{:S(2)}) %collective-permute-start.3) | collective-permute-done | bytes 131104 | tf_op jit(solution)/shard_map/ppermute | solution.py:50
  10.9 5.0 %attention.1 = (f32[2,8,640]{2,1,0:T(8,128)S(1)}, f32[2,8,640]{2,1,0:T(8,128)S(1)}, f32[2,8,640]{2,1,0:T(8,128)S(1)}, f32[2,8,640]{2,1,0:T(8,128)S(1)}, bf16[8,5...) custom-call(bf16[1,8,2048]{2,1,0:T(8,128)(2,1)S(1)} %bitcast.13, bf16[1,8,2048]{2,1,0:T(8,128)(2,1)S(1)} %bitcast.15, ...), custom_call_target="tpu_custom_call" | custom-call | tf_op jit(solution)/shard_map/attention/pallas_call | solution.py:213
  15.9 2.0 %collective-permute-start.4 = (f32[2,8,640]{2,1,0:T(8,128)S(1)}, f32[2,8,640]{2,1,0:T(8,128)S(1)}, u32[]{:S(2)}, u32[]{:S(2)}) collective-permute-start(f32[2,8,640]{2,1,0:T(8,128)S(1)} %get-tuple-element.29), channel_id=1, source_target_pairs={{0,8},{4,12},{8,0},{12,4},{16,24},{20,28},{24,16},{28,20},{1,9},{5... | collective-permute-start | bytes 122888 | tf_op jit(solution)/shard_map/ppermute | solution.py:50
  17.9 1.5 %collective-permute-start.5 = (f32[2,8,640]{2,1,0:T(8,128)S(1)}, f32[2,8,640]{2,1,0:T(8,128)S(1)}, u32[]{:S(2)}, u32[]{:S(2)}) collective-permute-start(f32[2,8,640]{2,1,0:T(8,128)S(1)} %get-tuple-element.30), channel_id=1, source_target_pairs={{0,16},{4,20},{8,24},{12,28},{16,0},{20,4},{24,8},{28,12},{1,17},{... | collective-permute-start | bytes 122888 | tf_op jit(solution)/shard_map/ppermute | solution.py:50
  19.9 2.0 %collective-permute-done.5.refs_2_ = f32[2,8,640]{2,1,0:T(8,128)S(1)} collective-permute-done((f32[2,8,640]{2,1,0:T(8,128)S(1)}, f32[2,8,640]{2,1,0:T(8,128)S(1)}, u32[]{:S(2)}, u32[]{:S(2)}) %collective-permute-start.5) | collective-permute-done | bytes 40992 | tf_op jit(solution)/shard_map/ppermute | solution.py:50
  21.9 2.4 %collective-permute-done.6.refs_3_ = f32[2,8,640]{2,1,0:T(8,128)S(1)} collective-permute-done((f32[2,8,640]{2,1,0:T(8,128)S(1)}, f32[2,8,640]{2,1,0:T(8,128)S(1)}, u32[]{:S(2)}, u32[]{:S(2)}) %collective-permute-start.6) | collective-permute-done | bytes 40992 | tf_op jit(solution)/shard_map/ppermute | solution.py:50
  24.4 1.3 %collective-permute-done.7.refs_4_ = f32[4,8,640]{2,1,0:T(8,128)S(1)} collective-permute-done((f32[4,8,640]{2,1,0:T(8,128)S(1)}, f32[4,8,640]{2,1,0:T(8,128)S(1)}, u32[]{:S(2)}, u32[]{:S(2)}) %collective-permute-start.7) | collective-permute-done | bytes 81952 | tf_op jit(solution)/shard_map/ppermute | solution.py:50
  25.7 0.5 merge.1
  26.2 3.6 %collective-permute-start.10 = (bf16[8,2048]{1,0:T(8,128)(2,1)S(1)}, bf16[8,2048]{1,0:T(8,128)(2,1)S(1)}, u32[]{:S(2)}, u32[]{:S(2)}) collective-permute-start(bf16[8,2048]{1,0:T(8,128)(2,1)S(1)} %get-tuple-element.34), channel_id=1, source_target_pairs={{0,3},{1,2},{2,1},{3,0},{4,7},{5,6},{6,5},{7,4},{8,11},{9,10},{10,... | collective-permute-start | bytes 98312 | tf_op jit(solution)/shard_map/ppermute | solution.py:50
  29.8 0.8 %collective-permute-start.8 = (bf16[8,2048]{1,0:T(8,128)(2,1)S(1)}, bf16[8,2048]{1,0:T(8,128)(2,1)S(1)}, u32[]{:S(2)}, u32[]{:S(2)}) collective-permute-start(bf16[8,2048]{1,0:T(8,128)(2,1)S(1)} %get-tuple-element.34), channel_id=1, source_target_pairs={{0,1},{1,0},{2,3},{3,2},{4,5},{5,4},{6,7},{7,6},{8,9},{9,8},{10,11... | collective-permute-start | bytes 98312 | tf_op jit(solution)/shard_map/ppermute | solution.py:50
  30.6 1.3 %collective-permute-done.10.refs_3_ = bf16[8,2048]{1,0:T(8,128)(2,1)S(1)} collective-permute-done((bf16[8,2048]{1,0:T(8,128)(2,1)S(1)}, bf16[8,2048]{1,0:T(8,128)(2,1)S(1)}, u32[]{:S(2)}, u32[]{:S(2)}) %collective-permute-start.10) | collective-permute-done | bytes 32800 | tf_op jit(solution)/shard_map/ppermute | solution.py:50
  31.9 2.7 %collective-permute-done.9.refs_2_ = bf16[8,2048]{1,0:T(8,128)(2,1)S(1)} collective-permute-done((bf16[8,2048]{1,0:T(8,128)(2,1)S(1)}, bf16[8,2048]{1,0:T(8,128)(2,1)S(1)}, u32[]{:S(2)}, u32[]{:S(2)}) %collective-permute-start.9) | collective-permute-done | bytes 32800 | tf_op jit(solution)/shard_map/ppermute | solution.py:50
  34.8 0.5 collective-permute-start.13
  35.4 1.5 %collective-permute-start.12 = (bf16[8,2048]{1,0:T(8,128)(2,1)S(1)}, bf16[8,2048]{1,0:T(8,128)(2,1)S(1)}, u32[]{:S(2)}, u32[]{:S(2)}) collective-permute-start(bf16[8,2048]{1,0:T(8,128)(2,1)S(1)} %get-tuple-element.35), channel_id=1, source_target_pairs={{0,16},{4,20},{8,24},{12,28},{16,0},{20,4},{24,8},{28,12},{1,17},{... | collective-permute-start | bytes 98312 | tf_op jit(solution)/shard_map/ppermute | solution.py:50
  36.9 1.5 %collective-permute-start.11 = (bf16[8,2048]{1,0:T(8,128)(2,1)S(1)}, bf16[8,2048]{1,0:T(8,128)(2,1)S(1)}, u32[]{:S(2)}, u32[]{:S(2)}) collective-permute-start(bf16[8,2048]{1,0:T(8,128)(2,1)S(1)} %get-tuple-element.35), channel_id=1, source_target_pairs={{0,8},{4,12},{8,0},{12,4},{16,24},{20,28},{24,16},{28,20},{1,9},{5... | collective-permute-start | bytes 98312 | tf_op jit(solution)/shard_map/ppermute | solution.py:50
  38.4 1.3 %collective-permute-done.13 = bf16[8,2048]{1,0:T(8,128)(2,1)S(1)} collective-permute-done((bf16[8,2048]{1,0:T(8,128)(2,1)S(1)}, bf16[8,2048]{1,0:T(8,128)(2,1)S(1)}, u32[]{:S(2)}, u32[]{:S(2)}) %collective-permute-start.13) | collective-permute-done | bytes 32800 | tf_op jit(solution)/shard_map/ppermute | solution.py:50
  39.7 1.1 %collective-permute-done.11 = bf16[8,2048]{1,0:T(8,128)(2,1)S(1)} collective-permute-done((bf16[8,2048]{1,0:T(8,128)(2,1)S(1)}, bf16[8,2048]{1,0:T(8,128)(2,1)S(1)}, u32[]{:S(2)}, u32[]{:S(2)}) %collective-permute-start.11) | collective-permute-done | bytes 32800 | tf_op jit(solution)/shard_map/ppermute | solution.py:50
  40.9 1.3 %collective-permute-done.14.refs_4_ = bf16[4,8,2048]{2,1,0:T(8,128)(2,1)S(1)} collective-permute-done((bf16[4,8,2048]{2,1,0:T(8,128)(2,1)S(1)}, bf16[4,8,2048]{2,1,0:T(8,128)(2,1)S(1)}, u32[]{:S(2)}, u32[]{:S(2)}) %collective-permute-start.14) | collective-permute-done | bytes 131104 | tf_op jit(solution)/shard_map/ppermute | solution.py:50
  42.2 0.8 %mlp.1 = bf16[32,8,512]{2,1,0:T(8,128)(2,1)S(1)} custom-call(bf16[1,8,2048]{2,1,0:T(8,128)(2,1)S(1)} %bitcast.19, bf16[1,8,2048]{2,1,0:T(8,128)(2,1)S(1)} %bitcast.27, bf16[1,8,2048]{2,1,0:T(8,128)(2,1)S(1)} %bitcast.25, bf16[1,8,2048]{2,1,0:T(8,128)(2,1)S(1)} %bitcast.23, bf16[4,8,2048]{2,1,0:T(8,128)(2,1)S(1)} %collective-permute-done.14.refs_4_, ...), custom_call_target="tpu_custom_call" | custom-call | tf_op jit(solution)/shard_map/mlp/pallas_call | solution.py:323
  43.1 13.3 %all_to_all.5.recv_ref = bf16[32,8,512]{2,1,0:T(8,128)(2,1)S(1)} all-to-all(bf16[32,8,512]{2,1,0:T(8,128)(2,1)S(1)} %mlp.1), channel_id=1, replica_groups=mesh['req'=8,'tp'=4] {'req','tp'}, dimensions={0} | all-to-all | bytes 524288 | tf_op jit(solution)/shard_map/all_to_all | solution.py:386
  56.4 0.6 %finish.1 = bf16[8,512]{1,0:T(8,128)(2,1)} custom-call(bf16[32,8,512]{2,1,0:T(8,128)(2,1)S(1)} %all_to_all.5.recv_ref, f32[8,512]{1,0:T(8,128)S(1)} %get-tuple-element.36.columns_ref), custom_call_target="tpu_custom_call" | custom-call | tf_op jit(solution)/shard_map/finish/pallas_call | solution.py:343
  (28 shorter events, 1.1 us)
Async XLA Ops:
  0.6 8.7 %collective-permute-start = (bf16[8,2048]{1,0:T(8,128)(2,1)}, bf16[8,2048]{1,0:T(8,128)(2,1)S(1)}, u32[]{:S(2)}, u32[]{:S(2)}) collective-permute-start(bf16[8,2048]{1,0:T(8,128)(2,1)} %refs_2_.1), channel_id=1, source_target_pairs={{0,8},{4,12},{8,0},{12,4},{16,24},{20,28},{24,16},{28,20},{1,9},{5... | collective-permute-start | bytes 98312 | tf_op jit(solution)/shard_map/ppermute | solution.py:50
  3.6 5.8 %collective-permute-start.2 = (bf16[8,2048]{1,0:T(8,128)(2,1)}, bf16[8,2048]{1,0:T(8,128)(2,1)S(1)}, u32[]{:S(2)}, u32[]{:S(2)}) collective-permute-start(bf16[8,2048]{1,0:T(8,128)(2,1)} %refs_2_.1), channel_id=1, source_target_pairs={{0,24},{4,28},{8,16},{12,20},{16,8},{20,12},{24,0},{28,4},{1,25},{... | collective-permute-start | bytes 98312 | tf_op jit(solution)/shard_map/ppermute | solution.py:50
  5.1 4.3 %collective-permute-start.1 = (bf16[8,2048]{1,0:T(8,128)(2,1)}, bf16[8,2048]{1,0:T(8,128)(2,1)S(1)}, u32[]{:S(2)}, u32[]{:S(2)}) collective-permute-start(bf16[8,2048]{1,0:T(8,128)(2,1)} %refs_2_.1), channel_id=1, source_target_pairs={{0,16},{4,20},{8,24},{12,28},{16,0},{20,4},{24,8},{28,12},{1,17},{... | collective-permute-start | bytes 98312 | tf_op jit(solution)/shard_map/ppermute | solution.py:50
  9.4 1.4 %collective-permute-start.3 = (bf16[4,8,2048]{2,1,0:T(8,128)(2,1)S(1)}, bf16[4,8,2048]{2,1,0:T(8,128)(2,1)S(1)}, u32[]{:S(2)}, u32[]{:S(2)}) collective-permute-start(bf16[4,8,2048]{2,1,0:T(8,128)(2,1)S(1)} %pad_maximum_fusion), channel_id=1, source_target_pairs={{0,4},{4,0},{8,12},{12,8},{16,20},{20,16},{24,28},{28,24},{1,5},{5... | collective-permute-start | bytes 393224 | tf_op jit(solution)/shard_map/ppermute | solution.py:50
  10.9 14.8 %copy-start = (bf16[512,2048]{1,0:T(8,128)(2,1)S(1)}, bf16[512,2048]{1,0:T(8,128)(2,1)}, u32[]{:S(2)}) copy-start(bf16[512,2048]{1,0:T(8,128)(2,1)} %refs_6_.4) | copy-start | bytes 6291460
  15.8 18.8 %copy-start.3 = (f32[2048]{0:T(1024)S(1)}, f32[2048]{0:T(1024)}, u32[]{:S(2)}) copy-start(f32[2048]{0:T(1024)} %param.19) | copy-start | bytes 24580
  15.8 26.4 %copy-start.1 = (bf16[2048,256]{1,0:T(8,128)(2,1)S(1)}, bf16[2048,256]{1,0:T(8,128)(2,1)}, u32[]{:S(2)}) copy-start(bf16[2048,256]{1,0:T(8,128)(2,1)} %refs_5_.3) | copy-start | bytes 3145732
  15.9 26.4 %copy-start.2 = (bf16[256,2048]{1,0:T(8,128)(2,1)S(1)}, bf16[256,2048]{1,0:T(8,128)(2,1)}, u32[]{:S(2)}) copy-start(bf16[256,2048]{1,0:T(8,128)(2,1)} %refs_6_.5) | copy-start | bytes 3145732
  15.9 4.1 %collective-permute-start.4 = (f32[2,8,640]{2,1,0:T(8,128)S(1)}, f32[2,8,640]{2,1,0:T(8,128)S(1)}, u32[]{:S(2)}, u32[]{:S(2)}) collective-permute-start(f32[2,8,640]{2,1,0:T(8,128)S(1)} %get-tuple-element.29), channel_id=1, source_target_pairs={{0,8},{4,12},{8,0},{12,4},{16,24},{20,28},{24,16},{28,20},{1,9},{5... | collective-permute-start | bytes 122888 | tf_op jit(solution)/shard_map/ppermute | solution.py:50
  17.9 4.0 %collective-permute-start.5 = (f32[2,8,640]{2,1,0:T(8,128)S(1)}, f32[2,8,640]{2,1,0:T(8,128)S(1)}, u32[]{:S(2)}, u32[]{:S(2)}) collective-permute-start(f32[2,8,640]{2,1,0:T(8,128)S(1)} %get-tuple-element.30), channel_id=1, source_target_pairs={{0,16},{4,20},{8,24},{12,28},{16,0},{20,4},{24,8},{28,12},{1,17},{... | collective-permute-start | bytes 122888 | tf_op jit(solution)/shard_map/ppermute | solution.py:50
  19.4 4.9 %collective-permute-start.6 = (f32[2,8,640]{2,1,0:T(8,128)S(1)}, f32[2,8,640]{2,1,0:T(8,128)S(1)}, u32[]{:S(2)}, u32[]{:S(2)}) collective-permute-start(f32[2,8,640]{2,1,0:T(8,128)S(1)} %get-tuple-element.31), channel_id=1, source_target_pairs={{0,24},{4,28},{8,16},{12,20},{16,8},{20,12},{24,0},{28,4},{1,25},{... | collective-permute-start | bytes 122888 | tf_op jit(solution)/shard_map/ppermute | solution.py:50
  24.3 1.3 %collective-permute-start.7 = (f32[4,8,640]{2,1,0:T(8,128)S(1)}, f32[4,8,640]{2,1,0:T(8,128)S(1)}, u32[]{:S(2)}, u32[]{:S(2)}) collective-permute-start(f32[4,8,640]{2,1,0:T(8,128)S(1)} %pad_maximum_fusion.2), channel_id=1, source_target_pairs={{0,4},{4,0},{8,12},{12,8},{16,20},{20,16},{24,28},{28,24},{1,5},{5... | collective-permute-start | bytes 245768 | tf_op jit(solution)/shard_map/ppermute | solution.py:50
  26.2 5.7 %collective-permute-start.10 = (bf16[8,2048]{1,0:T(8,128)(2,1)S(1)}, bf16[8,2048]{1,0:T(8,128)(2,1)S(1)}, u32[]{:S(2)}, u32[]{:S(2)}) collective-permute-start(bf16[8,2048]{1,0:T(8,128)(2,1)S(1)} %get-tuple-element.34), channel_id=1, source_target_pairs={{0,3},{1,2},{2,1},{3,0},{4,7},{5,6},{6,5},{7,4},{8,11},{9,10},{10,... | collective-permute-start | bytes 98312 | tf_op jit(solution)/shard_map/ppermute | solution.py:50
  29.8 4.8 %collective-permute-start.9 = (bf16[8,2048]{1,0:T(8,128)(2,1)S(1)}, bf16[8,2048]{1,0:T(8,128)(2,1)S(1)}, u32[]{:S(2)}, u32[]{:S(2)}) collective-permute-start(bf16[8,2048]{1,0:T(8,128)(2,1)S(1)} %get-tuple-element.34), channel_id=1, source_target_pairs={{0,2},{1,3},{2,0},{3,1},{4,6},{5,7},{6,4},{7,5},{8,10},{9,11},{10,... | collective-permute-start | bytes 98312 | tf_op jit(solution)/shard_map/ppermute | solution.py:50
  29.8 4.8 %collective-permute-start.8 = (bf16[8,2048]{1,0:T(8,128)(2,1)S(1)}, bf16[8,2048]{1,0:T(8,128)(2,1)S(1)}, u32[]{:S(2)}, u32[]{:S(2)}) collective-permute-start(bf16[8,2048]{1,0:T(8,128)(2,1)S(1)} %get-tuple-element.34), channel_id=1, source_target_pairs={{0,1},{1,0},{2,3},{3,2},{4,5},{5,4},{6,7},{7,6},{8,9},{9,8},{10,11... | collective-permute-start | bytes 98312 | tf_op jit(solution)/shard_map/ppermute | solution.py:50
  34.8 4.9 %collective-permute-start.13 = (bf16[8,2048]{1,0:T(8,128)(2,1)S(1)}, bf16[8,2048]{1,0:T(8,128)(2,1)S(1)}, u32[]{:S(2)}, u32[]{:S(2)}) collective-permute-start(bf16[8,2048]{1,0:T(8,128)(2,1)S(1)} %get-tuple-element.35), channel_id=1, source_target_pairs={{0,24},{4,28},{8,16},{12,20},{16,8},{20,12},{24,0},{28,4},{1,25},{... | collective-permute-start | bytes 98312 | tf_op jit(solution)/shard_map/ppermute | solution.py:50
  35.4 4.3 %collective-permute-start.12 = (bf16[8,2048]{1,0:T(8,128)(2,1)S(1)}, bf16[8,2048]{1,0:T(8,128)(2,1)S(1)}, u32[]{:S(2)}, u32[]{:S(2)}) collective-permute-start(bf16[8,2048]{1,0:T(8,128)(2,1)S(1)} %get-tuple-element.35), channel_id=1, source_target_pairs={{0,16},{4,20},{8,24},{12,28},{16,0},{20,4},{24,8},{28,12},{1,17},{... | collective-permute-start | bytes 98312 | tf_op jit(solution)/shard_map/ppermute | solution.py:50
  36.9 3.9 %collective-permute-start.11 = (bf16[8,2048]{1,0:T(8,128)(2,1)S(1)}, bf16[8,2048]{1,0:T(8,128)(2,1)S(1)}, u32[]{:S(2)}, u32[]{:S(2)}) collective-permute-start(bf16[8,2048]{1,0:T(8,128)(2,1)S(1)} %get-tuple-element.35), channel_id=1, source_target_pairs={{0,8},{4,12},{8,0},{12,4},{16,24},{20,28},{24,16},{28,20},{1,9},{5... | collective-permute-start | bytes 98312 | tf_op jit(solution)/shard_map/ppermute | solution.py:50
  40.8 1.4 %collective-permute-start.14 = (bf16[4,8,2048]{2,1,0:T(8,128)(2,1)S(1)}, bf16[4,8,2048]{2,1,0:T(8,128)(2,1)S(1)}, u32[]{:S(2)}, u32[]{:S(2)}) collective-permute-start(bf16[4,8,2048]{2,1,0:T(8,128)(2,1)S(1)} %pad_maximum_fusion.1), channel_id=1, source_target_pairs={{0,4},{4,0},{8,12},{12,8},{16,20},{20,16},{24,28},{28,24},{1,5},{5... | collective-permute-start | bytes 393224 | tf_op jit(solution)/shard_map/ppermute | solution.py:50

commit v3 on v2

--- a/solution.py
+++ b/solution.py
@@ -62,14 +62,24 @@
     return [x[None]] + [part[None] for part in far] + [swap(jnp.stack([x] + far), "req", 1)]
 
 
-def scatter_req(groups):
-    n = lax.axis_size("req")
-    got = [groups[0]] + [swap(groups[c], "req", 2 * c) for c in range(1, n // 2)]
-    return got + [swap(jnp.stack([part[1] for part in got]), "req", 1)]
+def scatter_far(groups):
+    return [groups[0]] + [swap(groups[c], "req", 2 * c) for c in range(1, len(groups))]
+
+
+def scatter_near(near, far):
+    return swap(jnp.stack([near] + [part[1] for part in far]), "req", 1)
 
 
 def landed_blocks(n):
     return [(c, 0) for c in range(n // 2)] + [(n // 2, c) for c in range(n // 2)]
+
+
+def split_three(x):
+    parts = []
+    for _ in range(3):
+        parts.append(x.astype(BF16).astype(F32))
+        x = x - parts[-1]
+    return parts
 
 
 def stacked(refs):
@@ -77,13 +87,12 @@
     return jnp.concatenate(blocks, axis=0)
 
 
-def load_kernel(*refs):
-    n = 8
+def load_kernel(n, *refs):
     sources, targets = refs[:n], refs[n : 2 * n - 2]
     bounds_ref, lens, order, sems = refs[2 * n - 2 :]
     targets = (lens, order) + targets
     copies = [
-        pltpu.make_async_copy(source, target, sems.at[k])
+        pltpu.make_async_copy(source.at[pl.ds(0, target.shape[0])], target, sems.at[k])
         for k, (source, target) in enumerate(zip(sources, targets))
     ]
     for copy in copies:
@@ -97,11 +106,13 @@
         copy.wait()
 
 
-def load(lens, order, *arrays):
+def load(lens, order, *arrays, last_rows):
     sources = [pltpu.with_memory_space_constraint(x, pltpu.HBM) for x in (lens, order) + arrays]
-    return pl.pallas_call(
-        load_kernel,
-        out_shape=[pltpu.VMEM(x.shape, x.dtype) for x in arrays]
+    last = arrays[-1]
+    return pl.pallas_call(
+        functools.partial(load_kernel, len(sources)),
+        out_shape=[pltpu.VMEM(x.shape, x.dtype) for x in arrays[:-1]]
+        + [pltpu.VMEM((last_rows, last.shape[1]), last.dtype)]
         + [pltpu.VMEM((2, lens.shape[1], 128), jnp.int32)],
         in_specs=[ANY] * len(sources),
         out_specs=[VMEM] * (len(arrays) + 1),
@@ -120,21 +131,30 @@
 
 def attention_kernel(req_count, n_tokens, *refs):
     token_refs, refs = refs[:n_tokens], refs[n_tokens:]
-    gain_ref, bounds, wq, wk, wv, keys, values_hbm = refs[:7]
+    gain_ref, bounds, wq, first_keys, keys_hbm, values_hbm = refs[:6]
     groups = req_count // 2
-    send_refs, refs = refs[7 : 7 + groups], refs[7 + groups :]
-    new_keys_ref, new_values_ref, self_ref, values, scores, sems = refs
-    rows, head_width = keys.shape
+    send_refs, refs = refs[6 : 6 + groups], refs[6 + groups :]
+    own_normed_ref, own_queries_ref, last_keys, values, scores, sems = refs
+    rows, head_width = values.shape
+    held = first_keys.shape[0]
     heads = head_width // HEAD_DIM
     chunks = rows // CHUNK
-    own_rows = new_keys_ref.shape[0]
+    own_rows = own_normed_ref.shape[0] // 2
     requests = own_rows * req_count
     me = lax.axis_index("req")
 
     copies = []
+    for c in range(held // CHUNK, chunks):
+        there, here = pl.ds(c * CHUNK, CHUNK), pl.ds(c * CHUNK - held, CHUNK)
+        copies.append(
+            pltpu.make_async_copy(keys_hbm.at[there], last_keys.at[here], sems.at[len(copies)])
+        )
+    late = len(copies)
     for c in range(chunks):
         part = pl.ds(c * CHUNK, CHUNK)
-        copies.append(pltpu.make_async_copy(values_hbm.at[part], values.at[part], sems.at[c]))
+        copies.append(
+            pltpu.make_async_copy(values_hbm.at[part], values.at[part], sems.at[len(copies)])
+        )
     for copy in copies:
         copy.start()
     normed = layer_norm(stacked(token_refs), gain_ref[...]).astype(BF16)
@@ -148,13 +168,17 @@
 
     lane_max = [jnp.full((requests, 128), NONE, F32)] * heads
     for c in range(chunks):
+        keys, at = first_keys, c * CHUNK
+        if at >= held:
+            copies[(at - held) // CHUNK].wait()
+            keys, at = last_keys, at - held
         place = c * CHUNK + lax.broadcasted_iota(jnp.int32, (requests, CHUNK), 1)
         member = (place >= first) & (place < last)
         for h in range(heads):
             cols = slice(h * HEAD_DIM, (h + 1) * HEAD_DIM)
             score = lax.dot_general(
                 queries[:, cols],
-                keys[c * CHUNK : (c + 1) * CHUNK, cols],
+                keys[at : at + CHUNK, cols],
                 (((1,), (1,)), ((), ())),
                 preferred_element_type=F32,
             )
@@ -167,7 +191,7 @@
     mass = [jnp.zeros((requests, 128), F32)] * heads
     partial = [jnp.zeros((requests, HEAD_DIM), F32)] * heads
     for c in range(chunks):
-        copies[c].wait()
+        copies[late + c].wait()
         for h in range(heads):
             cols = slice(h * HEAD_DIM, (h + 1) * HEAD_DIM)
             expo = jnp.exp(scores[h, :, c * CHUNK : (c + 1) * CHUNK] - peak[h])
@@ -179,62 +203,89 @@
     lane = lax.broadcasted_iota(jnp.int32, (requests, STATS), 1)
     stats = jnp.zeros((requests, STATS), F32)
     for h in range(heads):
-        stats = jnp.where(lane == h, peak[h], stats)
-        stats = jnp.where(lane == heads + h, jnp.sum(mass[h], axis=1, keepdims=True), stats)
+        both = (peak[h], jnp.sum(mass[h], axis=1, keepdims=True))
+        for kind, number in enumerate(both):
+            for k, piece in enumerate(split_three(number)):
+                stats = jnp.where(lane == (kind * heads + h) * 3 + k, piece, stats)
     for c, ref in enumerate(send_refs):
         for k, block in enumerate((c, groups + c)):
             r = slice(block * own_rows, (block + 1) * own_rows)
             for h in range(heads):
-                ref[k, :, h * HEAD_DIM : (h + 1) * HEAD_DIM] = partial[h][r]
-            ref[k, :, head_width : head_width + STATS] = stats[r]
-
-    mine = normed[: max(own_rows, 16)]
-    new_keys = dot(mine, wk[...])[:own_rows].astype(BF16)
-    new_values = dot(mine, wv[...])[:own_rows].astype(BF16)
-    new_keys_ref[...] = new_keys
-    new_values_ref[...] = new_values
-    product = queries[: max(own_rows, 16)].astype(F32)[:own_rows] * new_keys.astype(F32)
-    lane = lax.broadcasted_iota(jnp.int32, (own_rows, STATS), 1)
-    self_score = jnp.zeros((own_rows, STATS), F32)
-    for h in range(heads):
-        one = jnp.sum(product[:, h * HEAD_DIM : (h + 1) * HEAD_DIM], axis=1, keepdims=True)
-        self_score = jnp.where(lane == h, one, self_score)
-    self_ref[:, :head_width] = new_values.astype(F32)
-    self_ref[:, head_width:] = self_score
-
-
-def attend(tokens, gain, bounds, wq, wk, wv, keys, values):
+                ref[k, :, h * HEAD_DIM : (h + 1) * HEAD_DIM] = partial[h][r].astype(BF16)
+            ref[k, :, head_width : head_width + STATS] = stats[r].astype(BF16)
+    own_normed_ref[...] = normed[: 2 * own_rows]
+    own_queries_ref[...] = queries[: 2 * own_rows].astype(F32)
+
+
+def attend(tokens, gain, bounds, wq, first_keys, keys, values):
     req_count = lax.axis_size("req")
     own_rows, width = tokens[0].shape[1:]
     requests = own_rows * req_count
     rows, head_width = keys.shape
     heads = head_width // HEAD_DIM
     groups = req_count // 2
-    *sends, new_keys, new_values, self_part = pl.pallas_call(
+    scratch = heads * requests * rows * 4 + 4 * rows * head_width
+    *sends, own_normed, own_queries = pl.pallas_call(
         functools.partial(attention_kernel, req_count, len(tokens)),
-        out_shape=[jax.ShapeDtypeStruct((2, own_rows, head_width + STATS), F32)] * groups
-        + [jax.ShapeDtypeStruct((own_rows, head_width), BF16)] * 2
-        + [jax.ShapeDtypeStruct((own_rows, head_width + STATS), F32)],
-        in_specs=[VMEM] * (len(tokens) + 6) + [ANY],
-        out_specs=[VMEM] * (groups + 3),
+        out_shape=[jax.ShapeDtypeStruct((2, own_rows, head_width + STATS), BF16)] * groups
+        + [
+            jax.ShapeDtypeStruct((2 * own_rows, width), BF16),
+            jax.ShapeDtypeStruct((2 * own_rows, head_width), F32),
+        ],
+        in_specs=[VMEM] * (len(tokens) + 4) + [ANY] * 2,
+        out_specs=[VMEM] * (groups + 2),
         scratch_shapes=[
+            pltpu.VMEM((rows - first_keys.shape[0], head_width), BF16),
             pltpu.VMEM((rows, head_width), BF16),
             pltpu.VMEM((heads, requests, rows), F32),
-            pltpu.SemaphoreType.DMA((rows // CHUNK,)),
+            pltpu.SemaphoreType.DMA((2 * rows // CHUNK,)),
         ],
-        compiler_params=pltpu.CompilerParams(vmem_limit_bytes=heads * requests * rows * 4 + (4 + LIMIT) * MIB),
+        compiler_params=pltpu.CompilerParams(vmem_limit_bytes=scratch + LIMIT * MIB),
         name="attention",
     )(
         *tokens,
         gain,
         bounds,
         wq,
-        wk,
-        wv,
-        keys,
+        first_keys,
+        pltpu.with_memory_space_constraint(keys, pltpu.HBM),
         pltpu.with_memory_space_constraint(values, pltpu.HBM),
     )
-    return sends, new_keys, new_values, self_part
+    return sends, own_normed, own_queries
+
+
+def own_kernel(normed_ref, queries_ref, wk, wv, group_ref, new_keys_ref, new_values_ref, self_ref, near_ref):
+    own_rows, head_width = new_keys_ref.shape
+    new_keys = dot(normed_ref[...], wk[...])[:own_rows].astype(BF16)
+    new_values = dot(normed_ref[...], wv[...])[:own_rows].astype(BF16)
+    new_keys_ref[...] = new_keys
+    new_values_ref[...] = new_values
+    product = queries_ref[:own_rows] * new_keys.astype(F32)
+    lane = lax.broadcasted_iota(jnp.int32, (own_rows, STATS), 1)
+    self_score = jnp.zeros((own_rows, STATS), F32)
+    for h in range(head_width // HEAD_DIM):
+        one = jnp.sum(product[:, h * HEAD_DIM : (h + 1) * HEAD_DIM], axis=1, keepdims=True)
+        self_score = jnp.where(lane == h, one, self_score)
+    self_ref[:, :head_width] = new_values.astype(F32)
+    self_ref[:, head_width:] = self_score
+    near_ref[...] = group_ref[1]
+
+
+def own_part(normed, queries, wk, wv, group):
+    own_rows, head_width = normed.shape[0] // 2, wk.shape[1]
+    return pl.pallas_call(
+        own_kernel,
+        out_shape=[
+            jax.ShapeDtypeStruct((own_rows, head_width), BF16),
+            jax.ShapeDtypeStruct((own_rows, head_width), BF16),
+            jax.ShapeDtypeStruct((own_rows, head_width + STATS), F32),
+            jax.ShapeDtypeStruct(group.shape[1:], BF16),
+        ],
+        in_specs=[VMEM] * 5,
+        out_specs=[VMEM] * 4,
+        compiler_params=pltpu.CompilerParams(vmem_limit_bytes=LIMIT * MIB),
+        name="own",
+    )(normed, queries, wk, wv, group)
 
 
 def merge_kernel(places, n_landed, *refs):
@@ -244,17 +295,23 @@
     attended = []
     for h in range(heads):
         cols = slice(h * HEAD_DIM, (h + 1) * HEAD_DIM)
-        at_peak = slice(head_width + h, head_width + h + 1)
-        at_mass = slice(head_width + heads + h, head_width + heads + h + 1)
-        self_score = self_ref[:, at_peak]
-        peaks = [landed[a][k, :, at_peak] for a, k in places]
+        self_score = self_ref[:, head_width + h : head_width + h + 1]
+
+        def stat(a, k, kind):
+            at = head_width + (kind * heads + h) * 3
+            hi, mid, lo = (
+                landed[a][k, :, at + j : at + j + 1].astype(F32) for j in range(3)
+            )
+            return hi + mid + lo
+
+        peaks = [stat(a, k, 0) for a, k in places]
         top = functools.reduce(jnp.maximum, peaks, self_score)
         total = jnp.exp(self_score - top)
         summed = total * self_ref[:, cols]
         for (a, k), peak in zip(places, peaks):
             scale = jnp.exp(peak - top)
-            total = total + scale * landed[a][k, :, at_mass]
-            summed = summed + scale * landed[a][k, :, cols]
+            total = total + scale * stat(a, k, 1)
+            summed = summed + scale * landed[a][k, :, cols].astype(F32)
         attended.append((summed / total).astype(BF16))
     part = dot(jnp.concatenate(attended, axis=1), wo_ref[...])
     part_ref[...] = part
@@ -302,34 +359,37 @@
     )(part, *others, tokens, gain)
 
 
-def mlp_kernel(req_count, *refs):
-    *normed_refs, up_ref, down_ref, out_ref = refs
-    blocks, own_rows, column_width = out_ref.shape
-    tp_count = blocks // req_count
+def mlp_kernel(req_count, tp_count, n_normed, *refs):
+    normed_refs, (up_ref, down_ref, up_peer_ref, down_peer_ref, out_ref) = refs[:n_normed], refs[n_normed:]
+    own_rows, column_width = out_ref.shape[1:]
     me = lax.axis_index("req")
-    up = dot(stacked(normed_refs).astype(BF16), up_ref[...])
-    activation = (0.5 * up * (1.0 + lax.erf(up * 0.5**0.5))).astype(BF16)
+    normed = stacked(normed_refs).astype(BF16)
+    activations = []
+    for ref in (up_ref, up_peer_ref):
+        up = dot(normed, ref[...])
+        activations.append((0.5 * up * (1.0 + lax.erf(up * 0.5**0.5))).astype(BF16))
     for t in range(tp_count):
-        term = dot(activation, down_ref[:, t * column_width : (t + 1) * column_width])
-        for k, offset in enumerate(exchange_order(req_count)):
-            out_ref[(me ^ offset) * tp_count + t] = term[
-                k * own_rows : (k + 1) * own_rows
+        cols = slice(t * column_width, (t + 1) * column_width)
+        term = dot(activations[0], down_ref[:, cols]) + dot(activations[1], down_peer_ref[:, cols])
+        for c in range(req_count // 2):
+            out_ref[((me ^ (2 * c)) // 2) * tp_count + t] = term[
+                c * own_rows : (c + 1) * own_rows
             ].astype(BF16)
 
 
-def mlp(normed, up, down):
+def mlp(normed, *weights):
     req_count, tp_count = lax.axis_size("req"), lax.axis_size("tp")
     own_rows, width = normed[0].shape[1:]
     return pl.pallas_call(
-        functools.partial(mlp_kernel, req_count),
+        functools.partial(mlp_kernel, req_count, tp_count, len(normed)),
         out_shape=jax.ShapeDtypeStruct(
-            (req_count * tp_count, own_rows, width // tp_count), BF16
+            (req_count * tp_count // 2, own_rows, width // tp_count), BF16
         ),
-        in_specs=[VMEM] * (len(normed) + 2),
+        in_specs=[VMEM] * (len(normed) + len(weights)),
         out_specs=VMEM,
         compiler_params=pltpu.CompilerParams(vmem_limit_bytes=16 * MIB),
         name="mlp",
-    )(*normed, up, down)
+    )(*normed, *weights)
 
 
 def finish_kernel(recv_ref, columns_ref, out_ref):
@@ -365,25 +425,44 @@
     lengths,
     stream_order,
 ):
+    req_count = lax.axis_size("req")
+    tp_count = lax.axis_size("tp")
+    up_peer, down_peer = swap(up_weight, "req", 1), swap(down_weight, "req", 1)
     far = gather_far(tokens)
-    tokens, gain, wq, wk, wv, keys, bounds = load(
+    tokens, gain, wq, first_keys, bounds = load(
         lengths[None],
         stream_order[None],
         tokens,
         first_gain[None],
         query_weight,
-        key_weight,
-        value_weight,
         cache_keys,
-    )
-    sends, new_keys, new_values, self_part = attend(
-        gather_near(tokens, far), gain, bounds, wq, wk, wv, keys, cache_values
-    )
-    part, sent = merge(scatter_req(sends), self_part, out_weight)
-    others = [swap(sent, "tp", m) for m in range(1, lax.axis_size("tp"))]
+        last_rows=cache_keys.shape[0] // 2,
+    )
+    sends, own_normed, own_queries = attend(
+        gather_near(tokens, far), gain, bounds, wq, first_keys, cache_keys, cache_values
+    )
+    new_keys, new_values, self_part, near = own_part(
+        own_normed, own_queries, key_weight, value_weight, sends[0]
+    )
+    landed = scatter_far(sends)
+    landed.append(scatter_near(near, landed[1:]))
+    part, sent = merge(landed, self_part, out_weight)
+    others = [swap(sent, "tp", m) for m in range(1, tp_count)]
     normed, columns = middle(part, others, tokens, second_gain[None])
-    term = mlp(gather_near(normed, gather_far(normed)), up_weight, down_weight)
-    terms = lax.all_to_all(term, ("req", "tp"), split_axis=0, concat_axis=0, tiled=True)
+    all_normed = [part[None] for part in [normed] + gather_far(normed)]
+    term = mlp(all_normed, up_weight, down_weight, up_peer, down_peer)
+    same_core = [
+        [i * tp_count + t for i in range(core, req_count, 2) for t in range(tp_count)]
+        for core in range(2)
+    ]
+    terms = lax.all_to_all(
+        term,
+        ("req", "tp"),
+        split_axis=0,
+        concat_axis=0,
+        tiled=True,
+        axis_index_groups=same_core,
+    )
     hidden = finish(terms, columns)
     return (hidden, new_keys, new_values)
 

time: 57.2 us -> 53.5 us (0.935)
  blocking collectives: 13.3 us -> 10.5 us
  Pallas kernels: 11.3 us -> 10.5 us
    all_to_all x1, blocking collectives: 13.3 us -> 10.5 us  [body(): lax.all_to_all(term, ('req', 'tp'), split_axis=0, concat_axis=0, tiled=Tr...]
    pallas_call x2 -> x3, Pallas kernels: 5 us -> 4.5 us  [the longest x1 2.34 us: load(): pl.pallas_call(functools.partial(load_kernel, len(sources)), out_shape=[p...]
    ppermute x15 -> x16, starting transfers between devices: 16.3 us -> 16.7 us  [swap(): return lax.ppermute(x, axis, [(i, i ^ offset) for i in range(n)])]
    ppermute x15 -> x16, waiting for transfers between devices: 15.3 us -> 14.8 us  [swap(): return lax.ppermute(x, axis, [(i, i ^ offset) for i in range(n)])]
  transfers between devices with their start and end apart: 15 -> 16, of which waited for: 10 -> 11; matrix products, arithmetic and copies ran while one was open for 0% -> 0% of each run, Pallas kernels for 7% -> 17%
where the time goes in v3:
time: 53.5 us; the launch traced here: 53.3 us
  starting transfers between devices  16.7 us (31%)
  waiting for transfers between devices  14.8 us (28%)
  Pallas kernels  10.5 us (20%)
  blocking collectives  10.5 us (20%)
  between operations  0.74 us (1%)
    ppermute x16, starting transfers between devices, swap(): return lax.ppermute(x, axis, [(i, i ^ offset) for i in range(n)])  16.7 us
    ppermute x16, waiting for transfers between devices, swap(): return lax.ppermute(x, axis, [(i, i ^ offset) for i in range(n)])  14.8 us
    all_to_all x1, blocking collectives, body(): lax.all_to_all(term, ('req', 'tp'), split_axis=0, concat_axis=0, tiled=Tr...  10.5 us
    pallas_call x1, Pallas kernels, attend(): pl.pallas_call(functools.partial(attention_kernel, req_count, len(tokens)...  4.41 us
    pallas_call x1, Pallas kernels, load(): pl.pallas_call(functools.partial(load_kernel, len(sources)), out_shape=[p...  2.34 us
    pallas_call x1, Pallas kernels, own_part(): pl.pallas_call(own_kernel, out_shape=[jax.ShapeDtypeStruct((own_rows, hea...  1.26 us
  transfers between devices with their start and end apart: 16, of which 11 were waited for; matrix products, arithmetic and copies ran while one was open for 0% of the time, Pallas kernels for 17%

profile of v3, /device:TPU:0, one launch (start us, length us, event | category | flops | bytes accessed | tf_op | source)
XLA Modules:
  0.0 53.3 jit_solution(2736766567670549312)
XLA Ops:
  1.2 2.9 %collective-permute-start = (bf16[8,2048]{1,0:T(8,128)(2,1)}, bf16[8,2048]{1,0:T(8,128)(2,1)S(1)}, u32[]{:S(2)}, u32[]{:S(2)}) collective-permute-start(bf16[8,2048]{1,0:T(8,128)(2,1)} %refs_2_.1), channel_id=1, source_target_pairs={{0,8},{4,12},{8,0},{12,4},{16,24},{20,28},{24,16},{28,20},{1,9},{5... | collective-permute-start | bytes 98312 | tf_op jit(solution)/shard_map/ppermute | solution.py:50
  4.1 1.5 %collective-permute-start.1 = (bf16[8,2048]{1,0:T(8,128)(2,1)}, bf16[8,2048]{1,0:T(8,128)(2,1)S(1)}, u32[]{:S(2)}, u32[]{:S(2)}) collective-permute-start(bf16[8,2048]{1,0:T(8,128)(2,1)} %refs_2_.1), channel_id=1, source_target_pairs={{0,16},{4,20},{8,24},{12,28},{16,0},{20,4},{24,8},{28,12},{1,17},{... | collective-permute-start | bytes 98312 | tf_op jit(solution)/shard_map/ppermute | solution.py:50
  5.7 2.3 %load.1 = (bf16[8,2048]{1,0:T(8,128)(2,1)S(1)}, f32[1,2048]{1,0:T(1,128)S(1)}, bf16[2048,512]{1,0:T(8,128)(2,1)S(1)}, bf16[2048,512]{1,0:T(8,128)(2,1)S(1)}, s32[2,64,128]{2,1,0:T(8,128)S(1)}) custom-call(s32[1,64]{1,0:T(1,128)} %bitcast.28, s32[1,64]{1,0:T(1,128)} %bitcast.29, bf16[8,2048]{1,0:T(8,128)(2,1)} %refs_2_.1, f32[1,2048]{1,0:T(1,128)} %bitcast.27, ...), custom_call_target="tpu_custom_call" | custom-call | bytes 6328320 | tf_op jit(solution)/shard_map/load/pallas_call | solution.py:112
  8.3 2.4 %collective-permute-done.2 = bf16[8,2048]{1,0:T(8,128)(2,1)S(1)} collective-permute-done((bf16[8,2048]{1,0:T(8,128)(2,1)}, bf16[8,2048]{1,0:T(8,128)(2,1)S(1)}, u32[]{:S(2)}, u32[]{:S(2)}) %collective-permute-start.2) | collective-permute-done | bytes 32800 | tf_op jit(solution)/shard_map/ppermute | solution.py:50
  10.8 1.3 %collective-permute-done.3.refs_4_ = bf16[4,8,2048]{2,1,0:T(8,128)(2,1)S(1)} collective-permute-done((bf16[4,8,2048]{2,1,0:T(8,128)(2,1)S(1)}, bf16[4,8,2048]{2,1,0:T(8,128)(2,1)S(1)}, u32[]{:S(2)}, u32[]{:S(2)}) %collective-permute-start.3) | collective-permute-done | bytes 131104 | tf_op jit(solution)/shard_map/ppermute | solution.py:50
  12.1 4.4 %attention.1 = (bf16[2,8,640]{2,1,0:T(8,128)(2,1)S(1)}, bf16[2,8,640]{2,1,0:T(8,128)(2,1)S(1)}, bf16[2,8,640]{2,1,0:T(8,128)(2,1)S(1)}, bf16[2,8,640]{2,1,0:T(8,...) custom-call(bf16[1,8,2048]{2,1,0:T(8,128)(2,1)S(1)} %bitcast.14, bf16[1,8,2048]{2,1,0:T(8,128)(2,1)S(1)} %bitcast.16, ...), custom_call_target="tpu_custom_call" | custom-call | tf_op jit(solution)/shard_map/attention/pallas_call | solution.py:228
  17.5 2.6 %collective-permute-start.6 = (bf16[2,8,640]{2,1,0:T(8,128)(2,1)S(1)}, bf16[2,8,640]{2,1,0:T(8,128)(2,1)S(1)}, u32[]{:S(2)}, u32[]{:S(2)}) collective-permute-start(bf16[2,8,640]{2,1,0:T(8,128)(2,1)S(1)} %get-tuple-element.30), channel_id=1, source_target_pairs={{0,24},{4,28},{8,16},{12,20},{16,8},{20,12},{24,0},{28,4},{1,25},{... | collective-permute-start | bytes 61448 | tf_op jit(solution)/shard_map/ppermute | solution.py:50
  20.1 1.3 %own.1 = (bf16[8,512]{1,0:T(8,128)(2,1)}, bf16[8,512]{1,0:T(8,128)(2,1)}, f32[8,640]{1,0:T(8,128)S(1)}, bf16[8,640]{1,0:T(8,128)(2,1)S(1)}) custom-call(bf16[16,2048]{1,0:T(8,128)(2,1)S(1)} %get-tuple-element.31.normed_ref, f32[16,512]{1,0:T(8,128)S(1)} %get-tuple-element.32.queries_ref, bf16[2048,512]{1,0:T(8,128)(2,1)S(1)} %copy-done, ...), custom_call_target="tpu_custom_call" | custom-call | tf_op jit(solution)/shard_map/own/pallas_call | solution.py:276
  21.4 0.7 %collective-permute-done.6.refs_3_ = bf16[2,8,640]{2,1,0:T(8,128)(2,1)S(1)} collective-permute-done((bf16[2,8,640]{2,1,0:T(8,128)(2,1)S(1)}, bf16[2,8,640]{2,1,0:T(8,128)(2,1)S(1)}, u32[]{:S(2)}, u32[]{:S(2)}) %collective-permute-start.6) | collective-permute-done | bytes 20512 | tf_op jit(solution)/shard_map/ppermute | solution.py:50
  22.2 1.2 %collective-permute-done.7.refs_4_ = bf16[4,8,640]{2,1,0:T(8,128)(2,1)S(1)} collective-permute-done((bf16[4,8,640]{2,1,0:T(8,128)(2,1)S(1)}, bf16[4,8,640]{2,1,0:T(8,128)(2,1)S(1)}, u32[]{:S(2)}, u32[]{:S(2)}) %collective-permute-start.7) | collective-permute-done | bytes 40992 | tf_op jit(solution)/shard_map/ppermute | solution.py:50
  23.4 0.7 %merge.1 = (f32[8,2048]{1,0:T(8,128)S(1)}, bf16[8,2048]{1,0:T(8,128)(2,1)S(1)}) custom-call(bf16[2,8,640]{2,1,0:T(8,128)(2,1)S(1)} %get-tuple-element.27.group_ref.refs_0_, bf16[2,8,640]{2,1,0:T(8,128)(2,1)S(1)} %collective-permute-done.4.refs_1_, bf16[2,8,640]{2,1,0:T(8,128)(2,1)S(1)} %collective-permute-done.5.refs_2_, ...), custom_call_target="tpu_custom_call" | custom-call | tf_op jit(solution)/shard_map/merge/pallas_call | solution.py:323
  24.2 3.8 %collective-permute-start.10 = (bf16[8,2048]{1,0:T(8,128)(2,1)S(1)}, bf16[8,2048]{1,0:T(8,128)(2,1)S(1)}, u32[]{:S(2)}, u32[]{:S(2)}) collective-permute-start(bf16[8,2048]{1,0:T(8,128)(2,1)S(1)} %get-tuple-element.36), channel_id=1, source_target_pairs={{0,3},{1,2},{2,1},{3,0},{4,7},{5,6},{6,5},{7,4},{8,11},{9,10},{10,... | collective-permute-start | bytes 98312 | tf_op jit(solution)/shard_map/ppermute | solution.py:50
  28.0 0.6 %collective-permute-start.9 = (bf16[8,2048]{1,0:T(8,128)(2,1)S(1)}, bf16[8,2048]{1,0:T(8,128)(2,1)S(1)}, u32[]{:S(2)}, u32[]{:S(2)}) collective-permute-start(bf16[8,2048]{1,0:T(8,128)(2,1)S(1)} %get-tuple-element.36), channel_id=1, source_target_pairs={{0,2},{1,3},{2,0},{3,1},{4,6},{5,7},{6,4},{7,5},{8,10},{9,11},{10,... | collective-permute-start | bytes 98312 | tf_op jit(solution)/shard_map/ppermute | solution.py:50
  28.6 1.5 %collective-permute-done.10.refs_3_ = bf16[8,2048]{1,0:T(8,128)(2,1)S(1)} collective-permute-done((bf16[8,2048]{1,0:T(8,128)(2,1)S(1)}, bf16[8,2048]{1,0:T(8,128)(2,1)S(1)}, u32[]{:S(2)}, u32[]{:S(2)}) %collective-permute-start.10) | collective-permute-done | bytes 32800 | tf_op jit(solution)/shard_map/ppermute | solution.py:50
  30.0 2.0 %collective-permute-done.8.refs_1_ = bf16[8,2048]{1,0:T(8,128)(2,1)S(1)} collective-permute-done((bf16[8,2048]{1,0:T(8,128)(2,1)S(1)}, bf16[8,2048]{1,0:T(8,128)(2,1)S(1)}, u32[]{:S(2)}, u32[]{:S(2)}) %collective-permute-start.8) | collective-permute-done | bytes 32800 | tf_op jit(solution)/shard_map/ppermute | solution.py:50
  32.1 1.1 %collective-permute-done.9.refs_2_ = bf16[8,2048]{1,0:T(8,128)(2,1)S(1)} collective-permute-done((bf16[8,2048]{1,0:T(8,128)(2,1)S(1)}, bf16[8,2048]{1,0:T(8,128)(2,1)S(1)}, u32[]{:S(2)}, u32[]{:S(2)}) %collective-permute-start.9) | collective-permute-done | bytes 32800 | tf_op jit(solution)/shard_map/ppermute | solution.py:50
  33.4 1.6 %collective-permute-start.11 = (bf16[8,2048]{1,0:T(8,128)(2,1)S(1)}, bf16[8,2048]{1,0:T(8,128)(2,1)S(1)}, u32[]{:S(2)}, u32[]{:S(2)}) collective-permute-start(bf16[8,2048]{1,0:T(8,128)(2,1)S(1)} %get-tuple-element.37), channel_id=1, source_target_pairs={{0,8},{4,12},{8,0},{12,4},{16,24},{20,28},{24,16},{28,20},{1,9},{5... | collective-permute-start | bytes 98312 | tf_op jit(solution)/shard_map/ppermute | solution.py:50
  34.9 1.5 %collective-permute-start.12 = (bf16[8,2048]{1,0:T(8,128)(2,1)S(1)}, bf16[8,2048]{1,0:T(8,128)(2,1)S(1)}, u32[]{:S(2)}, u32[]{:S(2)}) collective-permute-start(bf16[8,2048]{1,0:T(8,128)(2,1)S(1)} %get-tuple-element.37), channel_id=1, source_target_pairs={{0,16},{4,20},{8,24},{12,28},{16,0},{20,4},{24,8},{28,12},{1,17},{... | collective-permute-start | bytes 98312 | tf_op jit(solution)/shard_map/ppermute | solution.py:50
  36.9 0.6 %collective-permute-done.11 = bf16[8,2048]{1,0:T(8,128)(2,1)S(1)} collective-permute-done((bf16[8,2048]{1,0:T(8,128)(2,1)S(1)}, bf16[8,2048]{1,0:T(8,128)(2,1)S(1)}, u32[]{:S(2)}, u32[]{:S(2)}) %collective-permute-start.11) | collective-permute-done | bytes 32800 | tf_op jit(solution)/shard_map/ppermute | solution.py:50
  37.5 1.3 %collective-permute-done.12 = bf16[8,2048]{1,0:T(8,128)(2,1)S(1)} collective-permute-done((bf16[8,2048]{1,0:T(8,128)(2,1)S(1)}, bf16[8,2048]{1,0:T(8,128)(2,1)S(1)}, u32[]{:S(2)}, u32[]{:S(2)}) %collective-permute-start.12) | collective-permute-done | bytes 32800 | tf_op jit(solution)/shard_map/ppermute | solution.py:50
  38.8 2.4 %collective-permute-done.13 = bf16[8,2048]{1,0:T(8,128)(2,1)S(1)} collective-permute-done((bf16[8,2048]{1,0:T(8,128)(2,1)S(1)}, bf16[8,2048]{1,0:T(8,128)(2,1)S(1)}, u32[]{:S(2)}, u32[]{:S(2)}) %collective-permute-start.13) | collective-permute-done | bytes 32800 | tf_op jit(solution)/shard_map/ppermute | solution.py:50
  41.3 0.9 %mlp.1 = bf16[16,8,512]{2,1,0:T(8,128)(2,1)S(1)} custom-call(bf16[1,8,2048]{2,1,0:T(8,128)(2,1)S(1)} %bitcast.21, bf16[1,8,2048]{2,1,0:T(8,128)(2,1)S(1)} %bitcast.22, bf16[1,8,2048]{2,1,0:T(8,128)(2,1)S(1)} %bitcast.23, bf16[1,8,2048]{2,1,0:T(8,128)(2,1)S(1)} %bitcast.24, bf16[2048,256]{1,0:T(8,128)(2,1)S(1)} %copy-done.3, bf16[256,2048]{1,0:T(8,128)(2,1)S(1)} %copy-done.4, ...), custom_call_target="tpu_custom_call" | custom-call | tf_op jit(solution)/shard_map/mlp/pallas_call | solution.py:383
  42.2 10.5 %all_to_all.5.recv_ref = bf16[16,8,512]{2,1,0:T(8,128)(2,1)S(1)} all-to-all(bf16[16,8,512]{2,1,0:T(8,128)(2,1)S(1)} %mlp.1), channel_id=1, replica_groups={{0,1,2,3,8,9,10,11,16,17,18,19,24,25,26,27},{4,5,6,7,12,13,14,15,20,21,..., dimensions={0} | all-to-all | bytes 262144 | tf_op jit(solution)/shard_map/all_to_all | solution.py:458
  52.7 0.6 %finish.1 = bf16[8,512]{1,0:T(8,128)(2,1)} custom-call(bf16[16,8,512]{2,1,0:T(8,128)(2,1)S(1)} %all_to_all.5.recv_ref, f32[8,512]{1,0:T(8,128)S(1)} %get-tuple-element.38.columns_ref), custom_call_target="tpu_custom_call" | custom-call | tf_op jit(solution)/shard_map/finish/pallas_call | solution.py:403
  (33 shorter events, 2.7 us)
Async XLA Ops:
  0.6 40.6 %collective-permute-start.14 = (bf16[2048,256]{1,0:T(8,128)(2,1)}, bf16[2048,256]{1,0:T(8,128)(2,1)S(1)}, u32[]{:S(2)}, u32[]{:S(2)}) collective-permute-start(bf16[2048,256]{1,0:T(8,128)(2,1)} %refs_4_.3), channel_id=1, source_target_pairs={{0,4},{4,0},{8,12},{12,8},{16,20},{20,16},{24,28},{28,24},{1,5},{5... | collective-permute-start | bytes 3145736 | tf_op jit(solution)/shard_map/ppermute | solution.py:50
  1.1 40.1 %collective-permute-start.15 = (bf16[256,2048]{1,0:T(8,128)(2,1)}, bf16[256,2048]{1,0:T(8,128)(2,1)S(1)}, u32[]{:S(2)}, u32[]{:S(2)}) collective-permute-start(bf16[256,2048]{1,0:T(8,128)(2,1)} %refs_5_.3), channel_id=1, source_target_pairs={{0,4},{4,0},{8,12},{12,8},{16,20},{20,16},{24,28},{28,24},{1,5},{5... | collective-permute-start | bytes 3145736 | tf_op jit(solution)/shard_map/ppermute | solution.py:50
  1.2 6.8 %collective-permute-start = (bf16[8,2048]{1,0:T(8,128)(2,1)}, bf16[8,2048]{1,0:T(8,128)(2,1)S(1)}, u32[]{:S(2)}, u32[]{:S(2)}) collective-permute-start(bf16[8,2048]{1,0:T(8,128)(2,1)} %refs_2_.1), channel_id=1, source_target_pairs={{0,8},{4,12},{8,0},{12,4},{16,24},{20,28},{24,16},{28,20},{1,9},{5... | collective-permute-start | bytes 98312 | tf_op jit(solution)/shard_map/ppermute | solution.py:50
  4.1 4.1 %collective-permute-start.1 = (bf16[8,2048]{1,0:T(8,128)(2,1)}, bf16[8,2048]{1,0:T(8,128)(2,1)S(1)}, u32[]{:S(2)}, u32[]{:S(2)}) collective-permute-start(bf16[8,2048]{1,0:T(8,128)(2,1)} %refs_2_.1), channel_id=1, source_target_pairs={{0,16},{4,20},{8,24},{12,28},{16,0},{20,4},{24,8},{28,12},{1,17},{... | collective-permute-start | bytes 98312 | tf_op jit(solution)/shard_map/ppermute | solution.py:50
  5.7 5.0 %collective-permute-start.2 = (bf16[8,2048]{1,0:T(8,128)(2,1)}, bf16[8,2048]{1,0:T(8,128)(2,1)S(1)}, u32[]{:S(2)}, u32[]{:S(2)}) collective-permute-start(bf16[8,2048]{1,0:T(8,128)(2,1)} %refs_2_.1), channel_id=1, source_target_pairs={{0,24},{4,28},{8,16},{12,20},{16,8},{20,12},{24,0},{28,4},{1,25},{... | collective-permute-start | bytes 98312 | tf_op jit(solution)/shard_map/ppermute | solution.py:50
  10.7 1.4 %collective-permute-start.3 = (bf16[4,8,2048]{2,1,0:T(8,128)(2,1)S(1)}, bf16[4,8,2048]{2,1,0:T(8,128)(2,1)S(1)}, u32[]{:S(2)}, u32[]{:S(2)}) collective-permute-start(bf16[4,8,2048]{2,1,0:T(8,128)(2,1)S(1)} %pad_maximum_fusion), channel_id=1, source_target_pairs={{0,4},{4,0},{8,12},{12,8},{16,20},{20,16},{24,28},{28,24},{1,5},{5... | collective-permute-start | bytes 393224 | tf_op jit(solution)/shard_map/ppermute | solution.py:50
  12.1 8.0 %copy-start = (bf16[2048,512]{1,0:T(8,128)(2,1)S(1)}, bf16[2048,512]{1,0:T(8,128)(2,1)}, u32[]{:S(2)}) copy-start(bf16[2048,512]{1,0:T(8,128)(2,1)} %wk.1) | copy-start | bytes 6291460
  12.1 8.0 %copy-start.1 = (bf16[2048,512]{1,0:T(8,128)(2,1)S(1)}, bf16[2048,512]{1,0:T(8,128)(2,1)}, u32[]{:S(2)}) copy-start(bf16[2048,512]{1,0:T(8,128)(2,1)} %wv.1) | copy-start | bytes 6291460
  16.6 4.8 %collective-permute-start.4 = (bf16[2,8,640]{2,1,0:T(8,128)(2,1)S(1)}, bf16[2,8,640]{2,1,0:T(8,128)(2,1)S(1)}, u32[]{:S(2)}, u32[]{:S(2)}) collective-permute-start(bf16[2,8,640]{2,1,0:T(8,128)(2,1)S(1)} %get-tuple-element.28), channel_id=1, source_target_pairs={{0,8},{4,12},{8,0},{12,4},{16,24},{20,28},{24,16},{28,20},{1,9},{5... | collective-permute-start | bytes 61448 | tf_op jit(solution)/shard_map/ppermute | solution.py:50
  17.1 4.3 %collective-permute-start.5 = (bf16[2,8,640]{2,1,0:T(8,128)(2,1)S(1)}, bf16[2,8,640]{2,1,0:T(8,128)(2,1)S(1)}, u32[]{:S(2)}, u32[]{:S(2)}) collective-permute-start(bf16[2,8,640]{2,1,0:T(8,128)(2,1)S(1)} %get-tuple-element.29), channel_id=1, source_target_pairs={{0,16},{4,20},{8,24},{12,28},{16,0},{20,4},{24,8},{28,12},{1,17},{... | collective-permute-start | bytes 61448 | tf_op jit(solution)/shard_map/ppermute | solution.py:50
  17.5 4.7 %collective-permute-start.6 = (bf16[2,8,640]{2,1,0:T(8,128)(2,1)S(1)}, bf16[2,8,640]{2,1,0:T(8,128)(2,1)S(1)}, u32[]{:S(2)}, u32[]{:S(2)}) collective-permute-start(bf16[2,8,640]{2,1,0:T(8,128)(2,1)S(1)} %get-tuple-element.30), channel_id=1, source_target_pairs={{0,24},{4,28},{8,16},{12,20},{16,8},{20,12},{24,0},{28,4},{1,25},{... | collective-permute-start | bytes 61448 | tf_op jit(solution)/shard_map/ppermute | solution.py:50
  20.1 3.3 %copy-start.2 = (bf16[512,2048]{1,0:T(8,128)(2,1)S(1)}, bf16[512,2048]{1,0:T(8,128)(2,1)}, u32[]{:S(2)}) copy-start(bf16[512,2048]{1,0:T(8,128)(2,1)} %refs_6_.1) | copy-start | bytes 6291460
  21.4 11.8 %copy-start.5 = (f32[2048]{0:T(1024)S(1)}, f32[2048]{0:T(1024)}, u32[]{:S(2)}) copy-start(f32[2048]{0:T(1024)} %param.19) | copy-start | bytes 24580
  21.4 19.9 %copy-start.3 = (bf16[2048,256]{1,0:T(8,128)(2,1)S(1)}, bf16[2048,256]{1,0:T(8,128)(2,1)}, u32[]{:S(2)}) copy-start(bf16[2048,256]{1,0:T(8,128)(2,1)} %refs_4_.3) | copy-start | bytes 3145732
  21.4 19.9 %copy-start.4 = (bf16[256,2048]{1,0:T(8,128)(2,1)S(1)}, bf16[256,2048]{1,0:T(8,128)(2,1)}, u32[]{:S(2)}) copy-start(bf16[256,2048]{1,0:T(8,128)(2,1)} %refs_5_.3) | copy-start | bytes 3145732
  22.2 1.3 %collective-permute-start.7 = (bf16[4,8,640]{2,1,0:T(8,128)(2,1)S(1)}, bf16[4,8,640]{2,1,0:T(8,128)(2,1)S(1)}, u32[]{:S(2)}, u32[]{:S(2)}) collective-permute-start(bf16[4,8,640]{2,1,0:T(8,128)(2,1)S(1)} %pad_maximum_fusion.1), channel_id=1, source_target_pairs={{0,4},{4,0},{8,12},{12,8},{16,20},{20,16},{24,28},{28,24},{1,5},{5... | collective-permute-start | bytes 122888 | tf_op jit(solution)/shard_map/ppermute | solution.py:50
  24.2 5.9 %collective-permute-start.10 = (bf16[8,2048]{1,0:T(8,128)(2,1)S(1)}, bf16[8,2048]{1,0:T(8,128)(2,1)S(1)}, u32[]{:S(2)}, u32[]{:S(2)}) collective-permute-start(bf16[8,2048]{1,0:T(8,128)(2,1)S(1)} %get-tuple-element.36), channel_id=1, source_target_pairs={{0,3},{1,2},{2,1},{3,0},{4,7},{5,6},{6,5},{7,4},{8,11},{9,10},{10,... | collective-permute-start | bytes 98312 | tf_op jit(solution)/shard_map/ppermute | solution.py:50
  28.0 4.1 %collective-permute-start.8 = (bf16[8,2048]{1,0:T(8,128)(2,1)S(1)}, bf16[8,2048]{1,0:T(8,128)(2,1)S(1)}, u32[]{:S(2)}, u32[]{:S(2)}) collective-permute-start(bf16[8,2048]{1,0:T(8,128)(2,1)S(1)} %get-tuple-element.36), channel_id=1, source_target_pairs={{0,1},{1,0},{2,3},{3,2},{4,5},{5,4},{6,7},{7,6},{8,9},{9,8},{10,11... | collective-permute-start | bytes 98312 | tf_op jit(solution)/shard_map/ppermute | solution.py:50
  28.0 5.2 %collective-permute-start.9 = (bf16[8,2048]{1,0:T(8,128)(2,1)S(1)}, bf16[8,2048]{1,0:T(8,128)(2,1)S(1)}, u32[]{:S(2)}, u32[]{:S(2)}) collective-permute-start(bf16[8,2048]{1,0:T(8,128)(2,1)S(1)} %get-tuple-element.36), channel_id=1, source_target_pairs={{0,2},{1,3},{2,0},{3,1},{4,6},{5,7},{6,4},{7,5},{8,10},{9,11},{10,... | collective-permute-start | bytes 98312 | tf_op jit(solution)/shard_map/ppermute | solution.py:50
  33.4 4.2 %collective-permute-start.11 = (bf16[8,2048]{1,0:T(8,128)(2,1)S(1)}, bf16[8,2048]{1,0:T(8,128)(2,1)S(1)}, u32[]{:S(2)}, u32[]{:S(2)}) collective-permute-start(bf16[8,2048]{1,0:T(8,128)(2,1)S(1)} %get-tuple-element.37), channel_id=1, source_target_pairs={{0,8},{4,12},{8,0},{12,4},{16,24},{20,28},{24,16},{28,20},{1,9},{5... | collective-permute-start | bytes 98312 | tf_op jit(solution)/shard_map/ppermute | solution.py:50
  34.9 3.9 %collective-permute-start.12 = (bf16[8,2048]{1,0:T(8,128)(2,1)S(1)}, bf16[8,2048]{1,0:T(8,128)(2,1)S(1)}, u32[]{:S(2)}, u32[]{:S(2)}) collective-permute-start(bf16[8,2048]{1,0:T(8,128)(2,1)S(1)} %get-tuple-element.37), channel_id=1, source_target_pairs={{0,16},{4,20},{8,24},{12,28},{16,0},{20,4},{24,8},{28,12},{1,17},{... | collective-permute-start | bytes 98312 | tf_op jit(solution)/shard_map/ppermute | solution.py:50
  36.4 4.8 %collective-permute-start.13 = (bf16[8,2048]{1,0:T(8,128)(2,1)S(1)}, bf16[8,2048]{1,0:T(8,128)(2,1)S(1)}, u32[]{:S(2)}, u32[]{:S(2)}) collective-permute-start(bf16[8,2048]{1,0:T(8,128)(2,1)S(1)} %get-tuple-element.37), channel_id=1, source_target_pairs={{0,24},{4,28},{8,16},{12,20},{16,8},{20,12},{24,0},{28,4},{1,25},{... | collective-permute-start | bytes 98312 | tf_op jit(solution)/shard_map/ppermute | solution.py:50

commit v4 on v3

--- a/solution.py
+++ b/solution.py
@@ -50,12 +50,17 @@
     return lax.ppermute(x, axis, [(i, i ^ offset) for i in range(n)])
 
 
+def far_offsets(n):
+    return list(range(n - 2, 0, -2))
+
+
 def exchange_order(n):
-    return list(range(0, n, 2)) + list(range(1, n, 2))
+    same = [0] + far_offsets(n)
+    return same + [offset + 1 for offset in same]
 
 
 def gather_far(x):
-    return [swap(x, "req", m) for m in range(2, lax.axis_size("req"), 2)]
+    return [swap(x, "req", m) for m in far_offsets(lax.axis_size("req"))]
 
 
 def gather_near(x, far):
@@ -63,7 +68,8 @@
 
 
 def scatter_far(groups):
-    return [groups[0]] + [swap(groups[c], "req", 2 * c) for c in range(1, len(groups))]
+    offsets = far_offsets(lax.axis_size("req"))
+    return groups[:1] + [swap(group, "req", m) for group, m in zip(groups[1:], offsets)]
 
 
 def scatter_near(near, far):
@@ -371,8 +377,8 @@
     for t in range(tp_count):
         cols = slice(t * column_width, (t + 1) * column_width)
         term = dot(activations[0], down_ref[:, cols]) + dot(activations[1], down_peer_ref[:, cols])
-        for c in range(req_count // 2):
-            out_ref[((me ^ (2 * c)) // 2) * tp_count + t] = term[
+        for c, offset in enumerate([0] + far_offsets(req_count)):
+            out_ref[((me ^ offset) // 2) * tp_count + t] = term[
                 c * own_rows : (c + 1) * own_rows
             ].astype(BF16)
 

time: 53.5 us -> 52.6 us (0.983)
  waiting for transfers between devices: 14.8 us -> 13 us
  blocking collectives: 10.5 us -> 11.4 us
    ppermute x16, waiting for transfers between devices: 14.8 us -> 13 us  [swap(): return lax.ppermute(x, axis, [(i, i ^ offset) for i in range(n)])]
    all_to_all x1, blocking collectives: 10.5 us -> 11.4 us  [body(): lax.all_to_all(term, ('req', 'tp'), split_axis=0, concat_axis=0, tiled=Tr...]
  transfers between devices with their start and end apart: 16 -> 16, of which waited for: 11 -> 12; matrix products, arithmetic and copies ran while one was open for 0% -> 0% of each run, Pallas kernels for 17% -> 17%
where the time goes in v4:
time: 52.6 us; the launch traced here: 52.4 us
  starting transfers between devices  16.7 us (32%)
  waiting for transfers between devices  13 us (25%)
  blocking collectives  11.4 us (22%)
  Pallas kernels  10.5 us (20%)
  between operations  0.72 us (1%)
    ppermute x16, starting transfers between devices, swap(): return lax.ppermute(x, axis, [(i, i ^ offset) for i in range(n)])  16.7 us
    ppermute x16, waiting for transfers between devices, swap(): return lax.ppermute(x, axis, [(i, i ^ offset) for i in range(n)])  13 us
    all_to_all x1, blocking collectives, body(): lax.all_to_all(term, ('req', 'tp'), split_axis=0, concat_axis=0, tiled=Tr...  11.4 us
    pallas_call x1, Pallas kernels, attend(): pl.pallas_call(functools.partial(attention_kernel, req_count, len(tokens)...  4.4 us
    pallas_call x1, Pallas kernels, load(): pl.pallas_call(functools.partial(load_kernel, len(sources)), out_shape=[p...  2.34 us
    pallas_call x1, Pallas kernels, own_part(): pl.pallas_call(own_kernel, out_shape=[jax.ShapeDtypeStruct((own_rows, hea...  1.26 us
  transfers between devices with their start and end apart: 16, of which 12 were waited for; matrix products, arithmetic and copies ran while one was open for 0% of the time, Pallas kernels for 17%

profile of v4, /device:TPU:0, one launch (start us, length us, event | category | flops | bytes accessed | tf_op | source)
XLA Modules:
  0.0 52.4 jit_solution(14920976903076592341)
XLA Ops:
  0.6 0.5 collective-permute-start.14
  1.2 3.9 %collective-permute-start = (bf16[8,2048]{1,0:T(8,128)(2,1)}, bf16[8,2048]{1,0:T(8,128)(2,1)S(1)}, u32[]{:S(2)}, u32[]{:S(2)}) collective-permute-start(bf16[8,2048]{1,0:T(8,128)(2,1)} %refs_2_.1), channel_id=1, source_target_pairs={{0,24},{4,28},{8,16},{12,20},{16,8},{20,12},{24,0},{28,4},{1,25},{... | collective-permute-start | bytes 98312 | tf_op jit(solution)/shard_map/ppermute | solution.py:50
  5.7 2.3 %load.1 = (bf16[8,2048]{1,0:T(8,128)(2,1)S(1)}, f32[1,2048]{1,0:T(1,128)S(1)}, bf16[2048,512]{1,0:T(8,128)(2,1)S(1)}, bf16[2048,512]{1,0:T(8,128)(2,1)S(1)}, s32[2,64,128]{2,1,0:T(8,128)S(1)}) custom-call(s32[1,64]{1,0:T(1,128)} %bitcast.28, s32[1,64]{1,0:T(1,128)} %bitcast.29, bf16[8,2048]{1,0:T(8,128)(2,1)} %refs_2_.1, f32[1,2048]{1,0:T(1,128)} %bitcast.27, ...), custom_call_target="tpu_custom_call" | custom-call | bytes 6328320 | tf_op jit(solution)/shard_map/load/pallas_call | solution.py:118
  8.0 1.2 %collective-permute-done.1 = bf16[8,2048]{1,0:T(8,128)(2,1)S(1)} collective-permute-done((bf16[8,2048]{1,0:T(8,128)(2,1)}, bf16[8,2048]{1,0:T(8,128)(2,1)S(1)}, u32[]{:S(2)}, u32[]{:S(2)}) %collective-permute-start.1) | collective-permute-done | bytes 32800 | tf_op jit(solution)/shard_map/ppermute | solution.py:50
  9.8 1.3 %collective-permute-done.3.refs_4_ = bf16[4,8,2048]{2,1,0:T(8,128)(2,1)S(1)} collective-permute-done((bf16[4,8,2048]{2,1,0:T(8,128)(2,1)S(1)}, bf16[4,8,2048]{2,1,0:T(8,128)(2,1)S(1)}, u32[]{:S(2)}, u32[]{:S(2)}) %collective-permute-start.3) | collective-permute-done | bytes 131104 | tf_op jit(solution)/shard_map/ppermute | solution.py:50
  11.2 4.4 %attention.1 = (bf16[2,8,640]{2,1,0:T(8,128)(2,1)S(1)}, bf16[2,8,640]{2,1,0:T(8,128)(2,1)S(1)}, bf16[2,8,640]{2,1,0:T(8,128)(2,1)S(1)}, bf16[2,8,640]{2,1,0:T(8,...) custom-call(bf16[1,8,2048]{2,1,0:T(8,128)(2,1)S(1)} %bitcast.14, bf16[1,8,2048]{2,1,0:T(8,128)(2,1)S(1)} %bitcast.16, ...), custom_call_target="tpu_custom_call" | custom-call | tf_op jit(solution)/shard_map/attention/pallas_call | solution.py:234
  15.6 1.6 %collective-permute-start.4 = (bf16[2,8,640]{2,1,0:T(8,128)(2,1)S(1)}, bf16[2,8,640]{2,1,0:T(8,128)(2,1)S(1)}, u32[]{:S(2)}, u32[]{:S(2)}) collective-permute-start(bf16[2,8,640]{2,1,0:T(8,128)(2,1)S(1)} %get-tuple-element.28), channel_id=1, source_target_pairs={{0,24},{4,28},{8,16},{12,20},{16,8},{20,12},{24,0},{28,4},{1,25},{... | collective-permute-start | bytes 61448 | tf_op jit(solution)/shard_map/ppermute | solution.py:50
  17.4 1.7 %collective-permute-start.6 = (bf16[2,8,640]{2,1,0:T(8,128)(2,1)S(1)}, bf16[2,8,640]{2,1,0:T(8,128)(2,1)S(1)}, u32[]{:S(2)}, u32[]{:S(2)}) collective-permute-start(bf16[2,8,640]{2,1,0:T(8,128)(2,1)S(1)} %get-tuple-element.30), channel_id=1, source_target_pairs={{0,8},{4,12},{8,0},{12,4},{16,24},{20,28},{24,16},{28,20},{1,9},{5... | collective-permute-start | bytes 61448 | tf_op jit(solution)/shard_map/ppermute | solution.py:50
  19.1 1.3 %own.1 = (bf16[8,512]{1,0:T(8,128)(2,1)}, bf16[8,512]{1,0:T(8,128)(2,1)}, f32[8,640]{1,0:T(8,128)S(1)}, bf16[8,640]{1,0:T(8,128)(2,1)S(1)}) custom-call(bf16[16,2048]{1,0:T(8,128)(2,1)S(1)} %get-tuple-element.31.normed_ref, f32[16,512]{1,0:T(8,128)S(1)} %get-tuple-element.32.queries_ref, bf16[2048,512]{1,0:T(8,128)(2,1)S(1)} %copy-done, ...), custom_call_target="tpu_custom_call" | custom-call | tf_op jit(solution)/shard_map/own/pallas_call | solution.py:282
  21.3 1.2 %collective-permute-done.7.refs_4_ = bf16[4,8,640]{2,1,0:T(8,128)(2,1)S(1)} collective-permute-done((bf16[4,8,640]{2,1,0:T(8,128)(2,1)S(1)}, bf16[4,8,640]{2,1,0:T(8,128)(2,1)S(1)}, u32[]{:S(2)}, u32[]{:S(2)}) %collective-permute-start.7) | collective-permute-done | bytes 40992 | tf_op jit(solution)/shard_map/ppermute | solution.py:50
  22.5 0.7 %merge.1 = (f32[8,2048]{1,0:T(8,128)S(1)}, bf16[8,2048]{1,0:T(8,128)(2,1)S(1)}) custom-call(bf16[2,8,640]{2,1,0:T(8,128)(2,1)S(1)} %get-tuple-element.27.group_ref.refs_0_, bf16[2,8,640]{2,1,0:T(8,128)(2,1)S(1)} %collective-permute-done.4.refs_1_, bf16[2,8,640]{2,1,0:T(8,128)(2,1)S(1)} %collective-permute-done.5.refs_2_, ...), custom_call_target="tpu_custom_call" | custom-call | tf_op jit(solution)/shard_map/merge/pallas_call | solution.py:329
  23.2 3.9 %collective-permute-start.10 = (bf16[8,2048]{1,0:T(8,128)(2,1)S(1)}, bf16[8,2048]{1,0:T(8,128)(2,1)S(1)}, u32[]{:S(2)}, u32[]{:S(2)}) collective-permute-start(bf16[8,2048]{1,0:T(8,128)(2,1)S(1)} %get-tuple-element.36), channel_id=1, source_target_pairs={{0,3},{1,2},{2,1},{3,0},{4,7},{5,6},{6,5},{7,4},{8,11},{9,10},{10,... | collective-permute-start | bytes 98312 | tf_op jit(solution)/shard_map/ppermute | solution.py:50
  27.1 0.6 %collective-permute-start.9 = (bf16[8,2048]{1,0:T(8,128)(2,1)S(1)}, bf16[8,2048]{1,0:T(8,128)(2,1)S(1)}, u32[]{:S(2)}, u32[]{:S(2)}) collective-permute-start(bf16[8,2048]{1,0:T(8,128)(2,1)S(1)} %get-tuple-element.36), channel_id=1, source_target_pairs={{0,2},{1,3},{2,0},{3,1},{4,6},{5,7},{6,4},{7,5},{8,10},{9,11},{10,... | collective-permute-start | bytes 98312 | tf_op jit(solution)/shard_map/ppermute | solution.py:50
  27.7 1.5 %collective-permute-done.10.refs_3_ = bf16[8,2048]{1,0:T(8,128)(2,1)S(1)} collective-permute-done((bf16[8,2048]{1,0:T(8,128)(2,1)S(1)}, bf16[8,2048]{1,0:T(8,128)(2,1)S(1)}, u32[]{:S(2)}, u32[]{:S(2)}) %collective-permute-start.10) | collective-permute-done | bytes 32800 | tf_op jit(solution)/shard_map/ppermute | solution.py:50
  29.1 2.0 %collective-permute-done.8.refs_1_ = bf16[8,2048]{1,0:T(8,128)(2,1)S(1)} collective-permute-done((bf16[8,2048]{1,0:T(8,128)(2,1)S(1)}, bf16[8,2048]{1,0:T(8,128)(2,1)S(1)}, u32[]{:S(2)}, u32[]{:S(2)}) %collective-permute-start.8) | collective-permute-done | bytes 32800 | tf_op jit(solution)/shard_map/ppermute | solution.py:50
  31.2 1.1 %collective-permute-done.9.refs_2_ = bf16[8,2048]{1,0:T(8,128)(2,1)S(1)} collective-permute-done((bf16[8,2048]{1,0:T(8,128)(2,1)S(1)}, bf16[8,2048]{1,0:T(8,128)(2,1)S(1)}, u32[]{:S(2)}, u32[]{:S(2)}) %collective-permute-start.9) | collective-permute-done | bytes 32800 | tf_op jit(solution)/shard_map/ppermute | solution.py:50
  32.5 2.5 %collective-permute-start.11 = (bf16[8,2048]{1,0:T(8,128)(2,1)S(1)}, bf16[8,2048]{1,0:T(8,128)(2,1)S(1)}, u32[]{:S(2)}, u32[]{:S(2)}) collective-permute-start(bf16[8,2048]{1,0:T(8,128)(2,1)S(1)} %get-tuple-element.37), channel_id=1, source_target_pairs={{0,24},{4,28},{8,16},{12,20},{16,8},{20,12},{24,0},{28,4},{1,25},{... | collective-permute-start | bytes 98312 | tf_op jit(solution)/shard_map/ppermute | solution.py:50
  35.0 0.5 collective-permute-start.12
  35.5 0.5 %collective-permute-start.13 = (bf16[8,2048]{1,0:T(8,128)(2,1)S(1)}, bf16[8,2048]{1,0:T(8,128)(2,1)S(1)}, u32[]{:S(2)}, u32[]{:S(2)}) collective-permute-start(bf16[8,2048]{1,0:T(8,128)(2,1)S(1)} %get-tuple-element.37), channel_id=1, source_target_pairs={{0,8},{4,12},{8,0},{12,4},{16,24},{20,28},{24,16},{28,20},{1,9},{5... | collective-permute-start | bytes 98312 | tf_op jit(solution)/shard_map/ppermute | solution.py:50
  36.0 1.5 %collective-permute-done.11 = bf16[8,2048]{1,0:T(8,128)(2,1)S(1)} collective-permute-done((bf16[8,2048]{1,0:T(8,128)(2,1)S(1)}, bf16[8,2048]{1,0:T(8,128)(2,1)S(1)}, u32[]{:S(2)}, u32[]{:S(2)}) %collective-permute-start.11) | collective-permute-done | bytes 32800 | tf_op jit(solution)/shard_map/ppermute | solution.py:50
  37.6 1.3 %collective-permute-done.12 = bf16[8,2048]{1,0:T(8,128)(2,1)S(1)} collective-permute-done((bf16[8,2048]{1,0:T(8,128)(2,1)S(1)}, bf16[8,2048]{1,0:T(8,128)(2,1)S(1)}, u32[]{:S(2)}, u32[]{:S(2)}) %collective-permute-start.12) | collective-permute-done | bytes 32800 | tf_op jit(solution)/shard_map/ppermute | solution.py:50
  39.4 0.9 %mlp.1 = bf16[16,8,512]{2,1,0:T(8,128)(2,1)S(1)} custom-call(bf16[1,8,2048]{2,1,0:T(8,128)(2,1)S(1)} %bitcast.21, bf16[1,8,2048]{2,1,0:T(8,128)(2,1)S(1)} %bitcast.22, bf16[1,8,2048]{2,1,0:T(8,128)(2,1)S(1)} %bitcast.23, bf16[1,8,2048]{2,1,0:T(8,128)(2,1)S(1)} %bitcast.24, bf16[2048,256]{1,0:T(8,128)(2,1)S(1)} %copy-done.3, bf16[256,2048]{1,0:T(8,128)(2,1)S(1)} %copy-done.4, ...), custom_call_target="tpu_custom_call" | custom-call | tf_op jit(solution)/shard_map/mlp/pallas_call | solution.py:389
  40.3 11.4 %all_to_all.5.recv_ref = bf16[16,8,512]{2,1,0:T(8,128)(2,1)S(1)} all-to-all(bf16[16,8,512]{2,1,0:T(8,128)(2,1)S(1)} %mlp.1), channel_id=1, replica_groups={{0,1,2,3,8,9,10,11,16,17,18,19,24,25,26,27},{4,5,6,7,12,13,14,15,20,21,..., dimensions={0} | all-to-all | bytes 262144 | tf_op jit(solution)/shard_map/all_to_all | solution.py:464
  51.8 0.6 %finish.1 = bf16[8,512]{1,0:T(8,128)(2,1)} custom-call(bf16[16,8,512]{2,1,0:T(8,128)(2,1)S(1)} %all_to_all.5.recv_ref, f32[8,512]{1,0:T(8,128)S(1)} %get-tuple-element.38.columns_ref), custom_call_target="tpu_custom_call" | custom-call | tf_op jit(solution)/shard_map/finish/pallas_call | solution.py:409
  (33 shorter events, 3.1 us)
Async XLA Ops:
  0.6 38.8 %collective-permute-start.14 = (bf16[2048,256]{1,0:T(8,128)(2,1)}, bf16[2048,256]{1,0:T(8,128)(2,1)S(1)}, u32[]{:S(2)}, u32[]{:S(2)}) collective-permute-start(bf16[2048,256]{1,0:T(8,128)(2,1)} %refs_4_.3), channel_id=1, source_target_pairs={{0,4},{4,0},{8,12},{12,8},{16,20},{20,16},{24,28},{28,24},{1,5},{5... | collective-permute-start | bytes 3145736 | tf_op jit(solution)/shard_map/ppermute | solution.py:50
  1.1 38.3 %collective-permute-start.15 = (bf16[256,2048]{1,0:T(8,128)(2,1)}, bf16[256,2048]{1,0:T(8,128)(2,1)S(1)}, u32[]{:S(2)}, u32[]{:S(2)}) collective-permute-start(bf16[256,2048]{1,0:T(8,128)(2,1)} %refs_5_.3), channel_id=1, source_target_pairs={{0,4},{4,0},{8,12},{12,8},{16,20},{20,16},{24,28},{28,24},{1,5},{5... | collective-permute-start | bytes 3145736 | tf_op jit(solution)/shard_map/ppermute | solution.py:50
  1.2 6.8 %collective-permute-start = (bf16[8,2048]{1,0:T(8,128)(2,1)}, bf16[8,2048]{1,0:T(8,128)(2,1)S(1)}, u32[]{:S(2)}, u32[]{:S(2)}) collective-permute-start(bf16[8,2048]{1,0:T(8,128)(2,1)} %refs_2_.1), channel_id=1, source_target_pairs={{0,24},{4,28},{8,16},{12,20},{16,8},{20,12},{24,0},{28,4},{1,25},{... | collective-permute-start | bytes 98312 | tf_op jit(solution)/shard_map/ppermute | solution.py:50
  5.1 4.1 %collective-permute-start.1 = (bf16[8,2048]{1,0:T(8,128)(2,1)}, bf16[8,2048]{1,0:T(8,128)(2,1)S(1)}, u32[]{:S(2)}, u32[]{:S(2)}) collective-permute-start(bf16[8,2048]{1,0:T(8,128)(2,1)} %refs_2_.1), channel_id=1, source_target_pairs={{0,16},{4,20},{8,24},{12,28},{16,0},{20,4},{24,8},{28,12},{1,17},{... | collective-permute-start | bytes 98312 | tf_op jit(solution)/shard_map/ppermute | solution.py:50
  5.6 4.1 %collective-permute-start.2 = (bf16[8,2048]{1,0:T(8,128)(2,1)}, bf16[8,2048]{1,0:T(8,128)(2,1)S(1)}, u32[]{:S(2)}, u32[]{:S(2)}) collective-permute-start(bf16[8,2048]{1,0:T(8,128)(2,1)} %refs_2_.1), channel_id=1, source_target_pairs={{0,8},{4,12},{8,0},{12,4},{16,24},{20,28},{24,16},{28,20},{1,9},{5... | collective-permute-start | bytes 98312 | tf_op jit(solution)/shard_map/ppermute | solution.py:50
  9.8 1.4 %collective-permute-start.3 = (bf16[4,8,2048]{2,1,0:T(8,128)(2,1)S(1)}, bf16[4,8,2048]{2,1,0:T(8,128)(2,1)S(1)}, u32[]{:S(2)}, u32[]{:S(2)}) collective-permute-start(bf16[4,8,2048]{2,1,0:T(8,128)(2,1)S(1)} %pad_maximum_fusion), channel_id=1, source_target_pairs={{0,4},{4,0},{8,12},{12,8},{16,20},{20,16},{24,28},{28,24},{1,5},{5... | collective-permute-start | bytes 393224 | tf_op jit(solution)/shard_map/ppermute | solution.py:50
  11.2 8.0 %copy-start = (bf16[2048,512]{1,0:T(8,128)(2,1)S(1)}, bf16[2048,512]{1,0:T(8,128)(2,1)}, u32[]{:S(2)}) copy-start(bf16[2048,512]{1,0:T(8,128)(2,1)} %wk.1) | copy-start | bytes 6291460
  11.2 8.0 %copy-start.1 = (bf16[2048,512]{1,0:T(8,128)(2,1)S(1)}, bf16[2048,512]{1,0:T(8,128)(2,1)}, u32[]{:S(2)}) copy-start(bf16[2048,512]{1,0:T(8,128)(2,1)} %wv.1) | copy-start | bytes 6291460
  15.6 4.8 %collective-permute-start.4 = (bf16[2,8,640]{2,1,0:T(8,128)(2,1)S(1)}, bf16[2,8,640]{2,1,0:T(8,128)(2,1)S(1)}, u32[]{:S(2)}, u32[]{:S(2)}) collective-permute-start(bf16[2,8,640]{2,1,0:T(8,128)(2,1)S(1)} %get-tuple-element.28), channel_id=1, source_target_pairs={{0,24},{4,28},{8,16},{12,20},{16,8},{20,12},{24,0},{28,4},{1,25},{... | collective-permute-start | bytes 61448 | tf_op jit(solution)/shard_map/ppermute | solution.py:50
  17.1 3.8 %collective-permute-start.5 = (bf16[2,8,640]{2,1,0:T(8,128)(2,1)S(1)}, bf16[2,8,640]{2,1,0:T(8,128)(2,1)S(1)}, u32[]{:S(2)}, u32[]{:S(2)}) collective-permute-start(bf16[2,8,640]{2,1,0:T(8,128)(2,1)S(1)} %get-tuple-element.29), channel_id=1, source_target_pairs={{0,16},{4,20},{8,24},{12,28},{16,0},{20,4},{24,8},{28,12},{1,17},{... | collective-permute-start | bytes 61448 | tf_op jit(solution)/shard_map/ppermute | solution.py:50
  17.4 3.8 %collective-permute-start.6 = (bf16[2,8,640]{2,1,0:T(8,128)(2,1)S(1)}, bf16[2,8,640]{2,1,0:T(8,128)(2,1)S(1)}, u32[]{:S(2)}, u32[]{:S(2)}) collective-permute-start(bf16[2,8,640]{2,1,0:T(8,128)(2,1)S(1)} %get-tuple-element.30), channel_id=1, source_target_pairs={{0,8},{4,12},{8,0},{12,4},{16,24},{20,28},{24,16},{28,20},{1,9},{5... | collective-permute-start | bytes 61448 | tf_op jit(solution)/shard_map/ppermute | solution.py:50
  19.1 3.3 %copy-start.2 = (bf16[512,2048]{1,0:T(8,128)(2,1)S(1)}, bf16[512,2048]{1,0:T(8,128)(2,1)}, u32[]{:S(2)}) copy-start(bf16[512,2048]{1,0:T(8,128)(2,1)} %refs_6_.1) | copy-start | bytes 6291460
  20.4 11.8 %copy-start.5 = (f32[2048]{0:T(1024)S(1)}, f32[2048]{0:T(1024)}, u32[]{:S(2)}) copy-start(f32[2048]{0:T(1024)} %param.19) | copy-start | bytes 24580
  20.4 19.0 %copy-start.3 = (bf16[2048,256]{1,0:T(8,128)(2,1)S(1)}, bf16[2048,256]{1,0:T(8,128)(2,1)}, u32[]{:S(2)}) copy-start(bf16[2048,256]{1,0:T(8,128)(2,1)} %refs_4_.3) | copy-start | bytes 3145732
  20.4 19.0 %copy-start.4 = (bf16[256,2048]{1,0:T(8,128)(2,1)S(1)}, bf16[256,2048]{1,0:T(8,128)(2,1)}, u32[]{:S(2)}) copy-start(bf16[256,2048]{1,0:T(8,128)(2,1)} %refs_5_.3) | copy-start | bytes 3145732
  21.2 1.3 %collective-permute-start.7 = (bf16[4,8,640]{2,1,0:T(8,128)(2,1)S(1)}, bf16[4,8,640]{2,1,0:T(8,128)(2,1)S(1)}, u32[]{:S(2)}, u32[]{:S(2)}) collective-permute-start(bf16[4,8,640]{2,1,0:T(8,128)(2,1)S(1)} %pad_maximum_fusion.1), channel_id=1, source_target_pairs={{0,4},{4,0},{8,12},{12,8},{16,20},{20,16},{24,28},{28,24},{1,5},{5... | collective-permute-start | bytes 122888 | tf_op jit(solution)/shard_map/ppermute | solution.py:50
  23.2 5.9 %collective-permute-start.10 = (bf16[8,2048]{1,0:T(8,128)(2,1)S(1)}, bf16[8,2048]{1,0:T(8,128)(2,1)S(1)}, u32[]{:S(2)}, u32[]{:S(2)}) collective-permute-start(bf16[8,2048]{1,0:T(8,128)(2,1)S(1)} %get-tuple-element.36), channel_id=1, source_target_pairs={{0,3},{1,2},{2,1},{3,0},{4,7},{5,6},{6,5},{7,4},{8,11},{9,10},{10,... | collective-permute-start | bytes 98312 | tf_op jit(solution)/shard_map/ppermute | solution.py:50
  27.1 4.1 %collective-permute-start.8 = (bf16[8,2048]{1,0:T(8,128)(2,1)S(1)}, bf16[8,2048]{1,0:T(8,128)(2,1)S(1)}, u32[]{:S(2)}, u32[]{:S(2)}) collective-permute-start(bf16[8,2048]{1,0:T(8,128)(2,1)S(1)} %get-tuple-element.36), channel_id=1, source_target_pairs={{0,1},{1,0},{2,3},{3,2},{4,5},{5,4},{6,7},{7,6},{8,9},{9,8},{10,11... | collective-permute-start | bytes 98312 | tf_op jit(solution)/shard_map/ppermute | solution.py:50
  27.1 5.2 %collective-permute-start.9 = (bf16[8,2048]{1,0:T(8,128)(2,1)S(1)}, bf16[8,2048]{1,0:T(8,128)(2,1)S(1)}, u32[]{:S(2)}, u32[]{:S(2)}) collective-permute-start(bf16[8,2048]{1,0:T(8,128)(2,1)S(1)} %get-tuple-element.36), channel_id=1, source_target_pairs={{0,2},{1,3},{2,0},{3,1},{4,6},{5,7},{6,4},{7,5},{8,10},{9,11},{10,... | collective-permute-start | bytes 98312 | tf_op jit(solution)/shard_map/ppermute | solution.py:50
  32.5 5.1 %collective-permute-start.11 = (bf16[8,2048]{1,0:T(8,128)(2,1)S(1)}, bf16[8,2048]{1,0:T(8,128)(2,1)S(1)}, u32[]{:S(2)}, u32[]{:S(2)}) collective-permute-start(bf16[8,2048]{1,0:T(8,128)(2,1)S(1)} %get-tuple-element.37), channel_id=1, source_target_pairs={{0,24},{4,28},{8,16},{12,20},{16,8},{20,12},{24,0},{28,4},{1,25},{... | collective-permute-start | bytes 98312 | tf_op jit(solution)/shard_map/ppermute | solution.py:50
  35.0 3.9 %collective-permute-start.12 = (bf16[8,2048]{1,0:T(8,128)(2,1)S(1)}, bf16[8,2048]{1,0:T(8,128)(2,1)S(1)}, u32[]{:S(2)}, u32[]{:S(2)}) collective-permute-start(bf16[8,2048]{1,0:T(8,128)(2,1)S(1)} %get-tuple-element.37), channel_id=1, source_target_pairs={{0,16},{4,20},{8,24},{12,28},{16,0},{20,4},{24,8},{28,12},{1,17},{... | collective-permute-start | bytes 98312 | tf_op jit(solution)/shard_map/ppermute | solution.py:50
  35.5 3.9 %collective-permute-start.13 = (bf16[8,2048]{1,0:T(8,128)(2,1)S(1)}, bf16[8,2048]{1,0:T(8,128)(2,1)S(1)}, u32[]{:S(2)}, u32[]{:S(2)}) collective-permute-start(bf16[8,2048]{1,0:T(8,128)(2,1)S(1)} %get-tuple-element.37), channel_id=1, source_target_pairs={{0,8},{4,12},{8,0},{12,4},{16,24},{20,28},{24,16},{28,20},{1,9},{5... | collective-permute-start | bytes 98312 | tf_op jit(solution)/shard_map/ppermute | solution.py:50

commit v5 on v4

--- a/solution.py
+++ b/solution.py
@@ -43,6 +43,14 @@
     before = jnp.sum(jnp.where(down < across, slot_len_col, 0.0), axis=0, keepdims=True)
     first = jnp.sum(jnp.where(holds, before, 0.0), axis=1, keepdims=True)
     return first.astype(jnp.int32), (first + lens_col).astype(jnp.int32)
+
+
+TERM_ORDER = (14, 12, 4, 5, 15, 8, 11, 10, 1, 7, 6, 13, 3, 0, 9, 2)
+
+
+def term_order(req_count, tp_count):
+    n = req_count * tp_count // 2
+    return TERM_ORDER if n == len(TERM_ORDER) else tuple(range(n))
 
 
 def swap(x, axis, offset):
@@ -172,7 +180,18 @@
     last = jnp.concatenate([bounds[1, owner][:, :1] for owner in owners], axis=0) - me * rows
     queries = (dot(normed, wq[...]) * HEAD_DIM ** (-0.5)).astype(BF16)
 
-    lane_max = [jnp.full((requests, 128), NONE, F32)] * heads
+    pairs = heads // 2
+    two = 2 * requests
+    wide = 2 * HEAD_DIM
+    zero = jnp.zeros((requests, HEAD_DIM), BF16)
+    paired = []
+    for p in range(pairs):
+        left = queries[:, p * wide : p * wide + HEAD_DIM]
+        right = queries[:, p * wide + HEAD_DIM : (p + 1) * wide]
+        upper = jnp.concatenate([left, zero], axis=1)
+        lower = jnp.concatenate([zero, right], axis=1)
+        paired.append(jnp.concatenate([upper, lower], axis=0))
+    lane_max = [jnp.full((two, 128), NONE, F32)] * pairs
     for c in range(chunks):
         keys, at = first_keys, c * CHUNK
         if at >= held:
@@ -180,39 +199,50 @@
             keys, at = last_keys, at - held
         place = c * CHUNK + lax.broadcasted_iota(jnp.int32, (requests, CHUNK), 1)
         member = (place >= first) & (place < last)
-        for h in range(heads):
-            cols = slice(h * HEAD_DIM, (h + 1) * HEAD_DIM)
+        for p in range(pairs):
             score = lax.dot_general(
-                queries[:, cols],
-                keys[at : at + CHUNK, cols],
+                paired[p],
+                keys[at : at + CHUNK, p * wide : (p + 1) * wide],
                 (((1,), (1,)), ((), ())),
                 preferred_element_type=F32,
             )
-            score = jnp.where(member, score, NONE)
-            scores[h, :, c * CHUNK : (c + 1) * CHUNK] = score
+            score = jnp.concatenate(
+                [
+                    jnp.where(member, score[:requests], NONE),
+                    jnp.where(member, score[requests:], NONE),
+                ],
+                axis=0,
+            )
+            scores[p, :, c * CHUNK : (c + 1) * CHUNK] = score
             for t in range(CHUNK // 128):
-                lane_max[h] = jnp.maximum(lane_max[h], score[:, t * 128 : (t + 1) * 128])
-
-    peak = [jnp.max(lane_max[h], axis=1, keepdims=True) for h in range(heads)]
-    mass = [jnp.zeros((requests, 128), F32)] * heads
-    partial = [jnp.zeros((requests, HEAD_DIM), F32)] * heads
+                lane_max[p] = jnp.maximum(lane_max[p], score[:, t * 128 : (t + 1) * 128])
+
+    tops = [jnp.max(lane_max[p], axis=1, keepdims=True) for p in range(pairs)]
+    sums = [jnp.zeros((two, 128), F32)] * pairs
+    outs = [jnp.zeros((two, wide), F32)] * pairs
     for c in range(chunks):
         copies[late + c].wait()
-        for h in range(heads):
-            cols = slice(h * HEAD_DIM, (h + 1) * HEAD_DIM)
-            expo = jnp.exp(scores[h, :, c * CHUNK : (c + 1) * CHUNK] - peak[h])
+        for p in range(pairs):
+            expo = jnp.exp(scores[p, :, c * CHUNK : (c + 1) * CHUNK] - tops[p])
             for t in range(CHUNK // 128):
-                mass[h] = mass[h] + expo[:, t * 128 : (t + 1) * 128]
-            partial[h] = partial[h] + dot(
-                expo.astype(BF16), values[c * CHUNK : (c + 1) * CHUNK, cols]
+                sums[p] = sums[p] + expo[:, t * 128 : (t + 1) * 128]
+            outs[p] = outs[p] + dot(
+                expo.astype(BF16),
+                values[c * CHUNK : (c + 1) * CHUNK, p * wide : (p + 1) * wide],
             )
+    peak, mass, partial = [], [], []
+    for h in range(heads):
+        p, r = h // 2, slice(h % 2 * requests, (h % 2 + 1) * requests)
+        peak.append(tops[p][r])
+        mass.append(sums[p][r])
+        partial.append(outs[p][r, h % 2 * HEAD_DIM : (h % 2 + 1) * HEAD_DIM])
     lane = lax.broadcasted_iota(jnp.int32, (requests, STATS), 1)
     stats = jnp.zeros((requests, STATS), F32)
     for h in range(heads):
         both = (peak[h], jnp.sum(mass[h], axis=1, keepdims=True))
         for kind, number in enumerate(both):
             for k, piece in enumerate(split_three(number)):
-                stats = jnp.where(lane == (kind * heads + h) * 3 + k, piece, stats)
+                stats = jnp.where(lane == (k * 2 + kind) * heads + h, piece, stats)
     for c, ref in enumerate(send_refs):
         for k, block in enumerate((c, groups + c)):
             r = slice(block * own_rows, (block + 1) * own_rows)
@@ -243,7 +273,7 @@
         scratch_shapes=[
             pltpu.VMEM((rows - first_keys.shape[0], head_width), BF16),
             pltpu.VMEM((rows, head_width), BF16),
-            pltpu.VMEM((heads, requests, rows), F32),
+            pltpu.VMEM((heads // 2, 2 * requests, rows), F32),
             pltpu.SemaphoreType.DMA((2 * rows // CHUNK,)),
         ],
         compiler_params=pltpu.CompilerParams(vmem_limit_bytes=scratch + LIMIT * MIB),
@@ -298,27 +328,28 @@
     landed, (self_ref, wo_ref, part_ref, sent_ref) = refs[:n_landed], refs[n_landed:]
     head_width = wo_ref.shape[0]
     heads = head_width // HEAD_DIM
+    self_scores = self_ref[:, head_width:]
+
+    def left(x, n):
+        return pltpu.roll(x, STATS - n, 1)
+
+    stats = []
+    for a, k in places:
+        pieces = landed[a][k, :, head_width:].astype(F32)
+        stats.append(pieces + left(pieces, 2 * heads) + left(pieces, 4 * heads))
+    top = functools.reduce(jnp.maximum, stats, self_scores)
+    self_weight = jnp.exp(self_scores - top)
+    scales = [jnp.exp(stat - top) for stat in stats]
+    total = self_weight
+    for stat, scale in zip(stats, scales):
+        total = total + scale * left(stat, heads)
     attended = []
     for h in range(heads):
         cols = slice(h * HEAD_DIM, (h + 1) * HEAD_DIM)
-        self_score = self_ref[:, head_width + h : head_width + h + 1]
-
-        def stat(a, k, kind):
-            at = head_width + (kind * heads + h) * 3
-            hi, mid, lo = (
-                landed[a][k, :, at + j : at + j + 1].astype(F32) for j in range(3)
-            )
-            return hi + mid + lo
-
-        peaks = [stat(a, k, 0) for a, k in places]
-        top = functools.reduce(jnp.maximum, peaks, self_score)
-        total = jnp.exp(self_score - top)
-        summed = total * self_ref[:, cols]
-        for (a, k), peak in zip(places, peaks):
-            scale = jnp.exp(peak - top)
-            total = total + scale * stat(a, k, 1)
-            summed = summed + scale * landed[a][k, :, cols].astype(F32)
-        attended.append((summed / total).astype(BF16))
+        summed = self_weight[:, h : h + 1] * self_ref[:, cols]
+        for (a, k), scale in zip(places, scales):
+            summed = summed + scale[:, h : h + 1] * landed[a][k, :, cols].astype(F32)
+        attended.append((summed / total[:, h : h + 1]).astype(BF16))
     part = dot(jnp.concatenate(attended, axis=1), wo_ref[...])
     part_ref[...] = part
     sent_ref[...] = part.astype(BF16)
@@ -370,6 +401,7 @@
     own_rows, column_width = out_ref.shape[1:]
     me = lax.axis_index("req")
     normed = stacked(normed_refs).astype(BF16)
+    order = term_order(req_count, tp_count)
     activations = []
     for ref in (up_ref, up_peer_ref):
         up = dot(normed, ref[...])
@@ -378,9 +410,10 @@
         cols = slice(t * column_width, (t + 1) * column_width)
         term = dot(activations[0], down_ref[:, cols]) + dot(activations[1], down_peer_ref[:, cols])
         for c, offset in enumerate([0] + far_offsets(req_count)):
-            out_ref[((me ^ offset) // 2) * tp_count + t] = term[
-                c * own_rows : (c + 1) * own_rows
-            ].astype(BF16)
+            chip, place = (me ^ offset) // 2, 0
+            for other in range(req_count // 2):
+                place = jnp.where(chip == other, order.index(other * tp_count + t), place)
+            out_ref[place] = term[c * own_rows : (c + 1) * own_rows].astype(BF16)
 
 
 def mlp(normed, *weights):
@@ -442,7 +475,7 @@
         first_gain[None],
         query_weight,
         cache_keys,
-        last_rows=cache_keys.shape[0] // 2,
+        last_rows=cache_keys.shape[0] * 3 // 4,
     )
     sends, own_normed, own_queries = attend(
         gather_near(tokens, far), gain, bounds, wq, first_keys, cache_keys, cache_values
@@ -457,8 +490,9 @@
     normed, columns = middle(part, others, tokens, second_gain[None])
     all_normed = [part[None] for part in [normed] + gather_far(normed)]
     term = mlp(all_normed, up_weight, down_weight, up_peer, down_peer)
+    order = term_order(req_count, tp_count)
     same_core = [
-        [i * tp_count + t for i in range(core, req_count, 2) for t in range(tp_count)]
+        [(2 * (k // tp_count) + core) * tp_count + k % tp_count for k in order]
         for core in range(2)
     ]
     terms = lax.all_to_all(

time: 52.6 us -> 50.6 us (0.962)
  blocking collectives: 11.4 us -> 10.1 us
    all_to_all x1, blocking collectives: 11.4 us -> 10.1 us  [body(): lax.all_to_all(term, ('req', 'tp'), split_axis=0, concat_axis=0, tiled=Tr...]
where the time goes in v5:
time: 50.6 us; the launch traced here: 50.4 us
  starting transfers between devices  16.7 us (33%)
  waiting for transfers between devices  12.7 us (25%)
  Pallas kernels  10.1 us (20%)
  blocking collectives  10.1 us (20%)
  between operations  0.73 us (1%)
    ppermute x16, starting transfers between devices, swap(): return lax.ppermute(x, axis, [(i, i ^ offset) for i in range(n)])  16.7 us
    ppermute x16, waiting for transfers between devices, swap(): return lax.ppermute(x, axis, [(i, i ^ offset) for i in range(n)])  12.7 us
    all_to_all x1, blocking collectives, body(): lax.all_to_all(term, ('req', 'tp'), split_axis=0, concat_axis=0, tiled=Tr...  10.1 us
    pallas_call x1, Pallas kernels, attend(): pl.pallas_call(functools.partial(attention_kernel, req_count, len(tokens)...  3.91 us
    pallas_call x1, Pallas kernels, load(): pl.pallas_call(functools.partial(load_kernel, len(sources)), out_shape=[p...  2.64 us
    pallas_call x1, Pallas kernels, own_part(): pl.pallas_call(own_kernel, out_shape=[jax.ShapeDtypeStruct((own_rows, hea...  1.26 us
  transfers between devices with their start and end apart: 16, of which 12 were waited for; matrix products, arithmetic and copies ran while one was open for 0% of the time, Pallas kernels for 17%

profile of v5, /device:TPU:0, one launch (start us, length us, event | category | flops | bytes accessed | tf_op | source)
XLA Modules:
  0.0 50.4 jit_solution(8058266839801943186)
XLA Ops:
  0.6 0.5 %collective-permute-start.14 = (bf16[2048,256]{1,0:T(8,128)(2,1)}, bf16[2048,256]{1,0:T(8,128)(2,1)S(1)}, u32[]{:S(2)}, u32[]{:S(2)}) collective-permute-start(bf16[2048,256]{1,0:T(8,128)(2,1)} %refs_4_.3), channel_id=1, source_target_pairs={{0,4},{4,0},{8,12},{12,8},{16,20},{20,16},{24,28},{28,24},{1,5},{5... | collective-permute-start | bytes 3145736 | tf_op jit(solution)/shard_map/ppermute | solution.py:58
  1.2 3.9 %collective-permute-start = (bf16[8,2048]{1,0:T(8,128)(2,1)}, bf16[8,2048]{1,0:T(8,128)(2,1)S(1)}, u32[]{:S(2)}, u32[]{:S(2)}) collective-permute-start(bf16[8,2048]{1,0:T(8,128)(2,1)} %refs_2_.1), channel_id=1, source_target_pairs={{0,24},{4,28},{8,16},{12,20},{16,8},{20,12},{24,0},{28,4},{1,25},{... | collective-permute-start | bytes 98312 | tf_op jit(solution)/shard_map/ppermute | solution.py:58
  5.7 2.6 %load.1 = (bf16[8,2048]{1,0:T(8,128)(2,1)S(1)}, f32[1,2048]{1,0:T(1,128)S(1)}, bf16[2048,512]{1,0:T(8,128)(2,1)S(1)}, bf16[3072,512]{1,0:T(8,128)(2,1)S(1)}, s32[2,64,128]{2,1,0:T(8,128)S(1)}) custom-call(s32[1,64]{1,0:T(1,128)} %bitcast.28, s32[1,64]{1,0:T(1,128)} %bitcast.29, bf16[8,2048]{1,0:T(8,128)(2,1)} %refs_2_.1, f32[1,2048]{1,0:T(1,128)} %bitcast.27, ...), custom_call_target="tpu_custom_call" | custom-call | bytes 6328320 | tf_op jit(solution)/shard_map/load/pallas_call | solution.py:126
  8.3 0.9 %collective-permute-done.1 = bf16[8,2048]{1,0:T(8,128)(2,1)S(1)} collective-permute-done((bf16[8,2048]{1,0:T(8,128)(2,1)}, bf16[8,2048]{1,0:T(8,128)(2,1)S(1)}, u32[]{:S(2)}, u32[]{:S(2)}) %collective-permute-start.1) | collective-permute-done | bytes 32800 | tf_op jit(solution)/shard_map/ppermute | solution.py:58
  9.8 1.3 %collective-permute-done.3.refs_4_ = bf16[4,8,2048]{2,1,0:T(8,128)(2,1)S(1)} collective-permute-done((bf16[4,8,2048]{2,1,0:T(8,128)(2,1)S(1)}, bf16[4,8,2048]{2,1,0:T(8,128)(2,1)S(1)}, u32[]{:S(2)}, u32[]{:S(2)}) %collective-permute-start.3) | collective-permute-done | bytes 131104 | tf_op jit(solution)/shard_map/ppermute | solution.py:58
  11.2 3.9 %attention.1 = (bf16[2,8,640]{2,1,0:T(8,128)(2,1)S(1)}, bf16[2,8,640]{2,1,0:T(8,128)(2,1)S(1)}, bf16[2,8,640]{2,1,0:T(8,128)(2,1)S(1)}, bf16[2,8,640]{2,1,0:T(8,...) custom-call(bf16[1,8,2048]{2,1,0:T(8,128)(2,1)S(1)} %bitcast.14, bf16[1,8,2048]{2,1,0:T(8,128)(2,1)S(1)} %bitcast.16, ...), custom_call_target="tpu_custom_call" | custom-call | tf_op jit(solution)/shard_map/attention/pallas_call | solution.py:264
  15.1 1.6 %collective-permute-start.4 = (bf16[2,8,640]{2,1,0:T(8,128)(2,1)S(1)}, bf16[2,8,640]{2,1,0:T(8,128)(2,1)S(1)}, u32[]{:S(2)}, u32[]{:S(2)}) collective-permute-start(bf16[2,8,640]{2,1,0:T(8,128)(2,1)S(1)} %get-tuple-element.28), channel_id=1, source_target_pairs={{0,24},{4,28},{8,16},{12,20},{16,8},{20,12},{24,0},{28,4},{1,25},{... | collective-permute-start | bytes 61448 | tf_op jit(solution)/shard_map/ppermute | solution.py:58
  17.2 1.4 %collective-permute-start.6 = (bf16[2,8,640]{2,1,0:T(8,128)(2,1)S(1)}, bf16[2,8,640]{2,1,0:T(8,128)(2,1)S(1)}, u32[]{:S(2)}, u32[]{:S(2)}) collective-permute-start(bf16[2,8,640]{2,1,0:T(8,128)(2,1)S(1)} %get-tuple-element.30), channel_id=1, source_target_pairs={{0,8},{4,12},{8,0},{12,4},{16,24},{20,28},{24,16},{28,20},{1,9},{5... | collective-permute-start | bytes 61448 | tf_op jit(solution)/shard_map/ppermute | solution.py:58
  18.7 1.3 %own.1 = (bf16[8,512]{1,0:T(8,128)(2,1)}, bf16[8,512]{1,0:T(8,128)(2,1)}, f32[8,640]{1,0:T(8,128)S(1)}, bf16[8,640]{1,0:T(8,128)(2,1)S(1)}) custom-call(bf16[16,2048]{1,0:T(8,128)(2,1)S(1)} %get-tuple-element.31.normed_ref, f32[16,512]{1,0:T(8,128)S(1)} %get-tuple-element.32.queries_ref, bf16[2048,512]{1,0:T(8,128)(2,1)S(1)} %copy-done, ...), custom_call_target="tpu_custom_call" | custom-call | tf_op jit(solution)/shard_map/own/pallas_call | solution.py:312
  19.9 0.6 %collective-permute-done.5.refs_2_ = bf16[2,8,640]{2,1,0:T(8,128)(2,1)S(1)} collective-permute-done((bf16[2,8,640]{2,1,0:T(8,128)(2,1)S(1)}, bf16[2,8,640]{2,1,0:T(8,128)(2,1)S(1)}, u32[]{:S(2)}, u32[]{:S(2)}) %collective-permute-start.5) | collective-permute-done | bytes 20512 | tf_op jit(solution)/shard_map/ppermute | solution.py:58
  21.1 1.2 %collective-permute-done.7.refs_4_ = bf16[4,8,640]{2,1,0:T(8,128)(2,1)S(1)} collective-permute-done((bf16[4,8,640]{2,1,0:T(8,128)(2,1)S(1)}, bf16[4,8,640]{2,1,0:T(8,128)(2,1)S(1)}, u32[]{:S(2)}, u32[]{:S(2)}) %collective-permute-start.7) | collective-permute-done | bytes 40992 | tf_op jit(solution)/shard_map/ppermute | solution.py:58
  22.3 0.6 %merge.1 = (f32[8,2048]{1,0:T(8,128)S(1)}, bf16[8,2048]{1,0:T(8,128)(2,1)S(1)}) custom-call(bf16[2,8,640]{2,1,0:T(8,128)(2,1)S(1)} %get-tuple-element.27.group_ref.refs_0_, bf16[2,8,640]{2,1,0:T(8,128)(2,1)S(1)} %collective-permute-done.4.refs_1_, bf16[2,8,640]{2,1,0:T(8,128)(2,1)S(1)} %collective-permute-done.5.refs_2_, ...), custom_call_target="tpu_custom_call" | custom-call | tf_op jit(solution)/shard_map/merge/pallas_call | solution.py:360
  22.9 3.6 %collective-permute-start.10 = (bf16[8,2048]{1,0:T(8,128)(2,1)S(1)}, bf16[8,2048]{1,0:T(8,128)(2,1)S(1)}, u32[]{:S(2)}, u32[]{:S(2)}) collective-permute-start(bf16[8,2048]{1,0:T(8,128)(2,1)S(1)} %get-tuple-element.36), channel_id=1, source_target_pairs={{0,3},{1,2},{2,1},{3,0},{4,7},{5,6},{6,5},{7,4},{8,11},{9,10},{10,... | collective-permute-start | bytes 98312 | tf_op jit(solution)/shard_map/ppermute | solution.py:58
  26.5 0.8 %collective-permute-start.9 = (bf16[8,2048]{1,0:T(8,128)(2,1)S(1)}, bf16[8,2048]{1,0:T(8,128)(2,1)S(1)}, u32[]{:S(2)}, u32[]{:S(2)}) collective-permute-start(bf16[8,2048]{1,0:T(8,128)(2,1)S(1)} %get-tuple-element.36), channel_id=1, source_target_pairs={{0,2},{1,3},{2,0},{3,1},{4,6},{5,7},{6,4},{7,5},{8,10},{9,11},{10,... | collective-permute-start | bytes 98312 | tf_op jit(solution)/shard_map/ppermute | solution.py:58
  27.3 1.3 %collective-permute-done.10.refs_3_ = bf16[8,2048]{1,0:T(8,128)(2,1)S(1)} collective-permute-done((bf16[8,2048]{1,0:T(8,128)(2,1)S(1)}, bf16[8,2048]{1,0:T(8,128)(2,1)S(1)}, u32[]{:S(2)}, u32[]{:S(2)}) %collective-permute-start.10) | collective-permute-done | bytes 32800 | tf_op jit(solution)/shard_map/ppermute | solution.py:58
  28.6 2.0 %collective-permute-done.8.refs_1_ = bf16[8,2048]{1,0:T(8,128)(2,1)S(1)} collective-permute-done((bf16[8,2048]{1,0:T(8,128)(2,1)S(1)}, bf16[8,2048]{1,0:T(8,128)(2,1)S(1)}, u32[]{:S(2)}, u32[]{:S(2)}) %collective-permute-start.8) | collective-permute-done | bytes 32800 | tf_op jit(solution)/shard_map/ppermute | solution.py:58
  30.6 1.1 %collective-permute-done.9.refs_2_ = bf16[8,2048]{1,0:T(8,128)(2,1)S(1)} collective-permute-done((bf16[8,2048]{1,0:T(8,128)(2,1)S(1)}, bf16[8,2048]{1,0:T(8,128)(2,1)S(1)}, u32[]{:S(2)}, u32[]{:S(2)}) %collective-permute-start.9) | collective-permute-done | bytes 32800 | tf_op jit(solution)/shard_map/ppermute | solution.py:58
  31.9 2.5 %collective-permute-start.11 = (bf16[8,2048]{1,0:T(8,128)(2,1)S(1)}, bf16[8,2048]{1,0:T(8,128)(2,1)S(1)}, u32[]{:S(2)}, u32[]{:S(2)}) collective-permute-start(bf16[8,2048]{1,0:T(8,128)(2,1)S(1)} %get-tuple-element.37), channel_id=1, source_target_pairs={{0,24},{4,28},{8,16},{12,20},{16,8},{20,12},{24,0},{28,4},{1,25},{... | collective-permute-start | bytes 98312 | tf_op jit(solution)/shard_map/ppermute | solution.py:58
  34.8 0.6 %collective-permute-start.13 = (bf16[8,2048]{1,0:T(8,128)(2,1)S(1)}, bf16[8,2048]{1,0:T(8,128)(2,1)S(1)}, u32[]{:S(2)}, u32[]{:S(2)}) collective-permute-start(bf16[8,2048]{1,0:T(8,128)(2,1)S(1)} %get-tuple-element.37), channel_id=1, source_target_pairs={{0,8},{4,12},{8,0},{12,4},{16,24},{20,28},{24,16},{28,20},{1,9},{5... | collective-permute-start | bytes 98312 | tf_op jit(solution)/shard_map/ppermute | solution.py:58
  35.4 1.5 %collective-permute-done.11 = bf16[8,2048]{1,0:T(8,128)(2,1)S(1)} collective-permute-done((bf16[8,2048]{1,0:T(8,128)(2,1)S(1)}, bf16[8,2048]{1,0:T(8,128)(2,1)S(1)}, u32[]{:S(2)}, u32[]{:S(2)}) %collective-permute-start.11) | collective-permute-done | bytes 32800 | tf_op jit(solution)/shard_map/ppermute | solution.py:58
  36.9 1.3 %collective-permute-done.12 = bf16[8,2048]{1,0:T(8,128)(2,1)S(1)} collective-permute-done((bf16[8,2048]{1,0:T(8,128)(2,1)S(1)}, bf16[8,2048]{1,0:T(8,128)(2,1)S(1)}, u32[]{:S(2)}, u32[]{:S(2)}) %collective-permute-start.12) | collective-permute-done | bytes 32800 | tf_op jit(solution)/shard_map/ppermute | solution.py:58
  38.8 0.9 %mlp.1 = bf16[16,8,512]{2,1,0:T(8,128)(2,1)S(1)} custom-call(bf16[1,8,2048]{2,1,0:T(8,128)(2,1)S(1)} %bitcast.21, bf16[1,8,2048]{2,1,0:T(8,128)(2,1)S(1)} %bitcast.22, bf16[1,8,2048]{2,1,0:T(8,128)(2,1)S(1)} %bitcast.23, bf16[1,8,2048]{2,1,0:T(8,128)(2,1)S(1)} %bitcast.24, bf16[2048,256]{1,0:T(8,128)(2,1)S(1)} %copy-done.3, bf16[256,2048]{1,0:T(8,128)(2,1)S(1)} %copy-done.4, ...), custom_call_target="tpu_custom_call" | custom-call | tf_op jit(solution)/shard_map/mlp/pallas_call | solution.py:422
  39.7 10.1 %all_to_all.5.recv_ref = bf16[16,8,512]{2,1,0:T(8,128)(2,1)S(1)} all-to-all(bf16[16,8,512]{2,1,0:T(8,128)(2,1)S(1)} %mlp.1), channel_id=1, replica_groups={{26,24,8,9,27,16,19,18,1,11,10,25,3,0,17,2},{30,28,12,13,31,20,23,22,5,..., dimensions={0} | all-to-all | bytes 262144 | tf_op jit(solution)/shard_map/all_to_all | solution.py:498
  49.8 0.6 %finish.1 = bf16[8,512]{1,0:T(8,128)(2,1)} custom-call(bf16[16,8,512]{2,1,0:T(8,128)(2,1)S(1)} %all_to_all.5.recv_ref, f32[8,512]{1,0:T(8,128)S(1)} %get-tuple-element.38.columns_ref), custom_call_target="tpu_custom_call" | custom-call | tf_op jit(solution)/shard_map/finish/pallas_call | solution.py:442
  (33 shorter events, 3.6 us)
Async XLA Ops:
  0.6 38.1 %collective-permute-start.14 = (bf16[2048,256]{1,0:T(8,128)(2,1)}, bf16[2048,256]{1,0:T(8,128)(2,1)S(1)}, u32[]{:S(2)}, u32[]{:S(2)}) collective-permute-start(bf16[2048,256]{1,0:T(8,128)(2,1)} %refs_4_.3), channel_id=1, source_target_pairs={{0,4},{4,0},{8,12},{12,8},{16,20},{20,16},{24,28},{28,24},{1,5},{5... | collective-permute-start | bytes 3145736 | tf_op jit(solution)/shard_map/ppermute | solution.py:58
  1.1 37.6 %collective-permute-start.15 = (bf16[256,2048]{1,0:T(8,128)(2,1)}, bf16[256,2048]{1,0:T(8,128)(2,1)S(1)}, u32[]{:S(2)}, u32[]{:S(2)}) collective-permute-start(bf16[256,2048]{1,0:T(8,128)(2,1)} %refs_5_.3), channel_id=1, source_target_pairs={{0,4},{4,0},{8,12},{12,8},{16,20},{20,16},{24,28},{28,24},{1,5},{5... | collective-permute-start | bytes 3145736 | tf_op jit(solution)/shard_map/ppermute | solution.py:58
  1.2 7.1 %collective-permute-start = (bf16[8,2048]{1,0:T(8,128)(2,1)}, bf16[8,2048]{1,0:T(8,128)(2,1)S(1)}, u32[]{:S(2)}, u32[]{:S(2)}) collective-permute-start(bf16[8,2048]{1,0:T(8,128)(2,1)} %refs_2_.1), channel_id=1, source_target_pairs={{0,24},{4,28},{8,16},{12,20},{16,8},{20,12},{24,0},{28,4},{1,25},{... | collective-permute-start | bytes 98312 | tf_op jit(solution)/shard_map/ppermute | solution.py:58
  5.1 4.1 %collective-permute-start.1 = (bf16[8,2048]{1,0:T(8,128)(2,1)}, bf16[8,2048]{1,0:T(8,128)(2,1)S(1)}, u32[]{:S(2)}, u32[]{:S(2)}) collective-permute-start(bf16[8,2048]{1,0:T(8,128)(2,1)} %refs_2_.1), channel_id=1, source_target_pairs={{0,16},{4,20},{8,24},{12,28},{16,0},{20,4},{24,8},{28,12},{1,17},{... | collective-permute-start | bytes 98312 | tf_op jit(solution)/shard_map/ppermute | solution.py:58
  5.6 4.1 %collective-permute-start.2 = (bf16[8,2048]{1,0:T(8,128)(2,1)}, bf16[8,2048]{1,0:T(8,128)(2,1)S(1)}, u32[]{:S(2)}, u32[]{:S(2)}) collective-permute-start(bf16[8,2048]{1,0:T(8,128)(2,1)} %refs_2_.1), channel_id=1, source_target_pairs={{0,8},{4,12},{8,0},{12,4},{16,24},{20,28},{24,16},{28,20},{1,9},{5... | collective-permute-start | bytes 98312 | tf_op jit(solution)/shard_map/ppermute | solution.py:58
  9.8 1.4 %collective-permute-start.3 = (bf16[4,8,2048]{2,1,0:T(8,128)(2,1)S(1)}, bf16[4,8,2048]{2,1,0:T(8,128)(2,1)S(1)}, u32[]{:S(2)}, u32[]{:S(2)}) collective-permute-start(bf16[4,8,2048]{2,1,0:T(8,128)(2,1)S(1)} %pad_maximum_fusion), channel_id=1, source_target_pairs={{0,4},{4,0},{8,12},{12,8},{16,20},{20,16},{24,28},{28,24},{1,5},{5... | collective-permute-start | bytes 393224 | tf_op jit(solution)/shard_map/ppermute | solution.py:58
  11.2 7.5 %copy-start = (bf16[2048,512]{1,0:T(8,128)(2,1)S(1)}, bf16[2048,512]{1,0:T(8,128)(2,1)}, u32[]{:S(2)}) copy-start(bf16[2048,512]{1,0:T(8,128)(2,1)} %wk.1) | copy-start | bytes 6291460
  11.2 7.5 %copy-start.1 = (bf16[2048,512]{1,0:T(8,128)(2,1)S(1)}, bf16[2048,512]{1,0:T(8,128)(2,1)}, u32[]{:S(2)}) copy-start(bf16[2048,512]{1,0:T(8,128)(2,1)} %wv.1) | copy-start | bytes 6291460
  15.1 4.8 %collective-permute-start.4 = (bf16[2,8,640]{2,1,0:T(8,128)(2,1)S(1)}, bf16[2,8,640]{2,1,0:T(8,128)(2,1)S(1)}, u32[]{:S(2)}, u32[]{:S(2)}) collective-permute-start(bf16[2,8,640]{2,1,0:T(8,128)(2,1)S(1)} %get-tuple-element.28), channel_id=1, source_target_pairs={{0,24},{4,28},{8,16},{12,20},{16,8},{20,12},{24,0},{28,4},{1,25},{... | collective-permute-start | bytes 61448 | tf_op jit(solution)/shard_map/ppermute | solution.py:58
  16.7 3.8 %collective-permute-start.5 = (bf16[2,8,640]{2,1,0:T(8,128)(2,1)S(1)}, bf16[2,8,640]{2,1,0:T(8,128)(2,1)S(1)}, u32[]{:S(2)}, u32[]{:S(2)}) collective-permute-start(bf16[2,8,640]{2,1,0:T(8,128)(2,1)S(1)} %get-tuple-element.29), channel_id=1, source_target_pairs={{0,16},{4,20},{8,24},{12,28},{16,0},{20,4},{24,8},{28,12},{1,17},{... | collective-permute-start | bytes 61448 | tf_op jit(solution)/shard_map/ppermute | solution.py:58
  17.2 3.8 %collective-permute-start.6 = (bf16[2,8,640]{2,1,0:T(8,128)(2,1)S(1)}, bf16[2,8,640]{2,1,0:T(8,128)(2,1)S(1)}, u32[]{:S(2)}, u32[]{:S(2)}) collective-permute-start(bf16[2,8,640]{2,1,0:T(8,128)(2,1)S(1)} %get-tuple-element.30), channel_id=1, source_target_pairs={{0,8},{4,12},{8,0},{12,4},{16,24},{20,28},{24,16},{28,20},{1,9},{5... | collective-permute-start | bytes 61448 | tf_op jit(solution)/shard_map/ppermute | solution.py:58
  18.7 3.6 %copy-start.2 = (bf16[512,2048]{1,0:T(8,128)(2,1)S(1)}, bf16[512,2048]{1,0:T(8,128)(2,1)}, u32[]{:S(2)}) copy-start(bf16[512,2048]{1,0:T(8,128)(2,1)} %refs_6_.1) | copy-start | bytes 6291460
  19.9 11.7 %copy-start.5 = (f32[2048]{0:T(1024)S(1)}, f32[2048]{0:T(1024)}, u32[]{:S(2)}) copy-start(f32[2048]{0:T(1024)} %param.19) | copy-start | bytes 24580
  19.9 18.9 %copy-start.3 = (bf16[2048,256]{1,0:T(8,128)(2,1)S(1)}, bf16[2048,256]{1,0:T(8,128)(2,1)}, u32[]{:S(2)}) copy-start(bf16[2048,256]{1,0:T(8,128)(2,1)} %refs_4_.3) | copy-start | bytes 3145732
  19.9 18.9 %copy-start.4 = (bf16[256,2048]{1,0:T(8,128)(2,1)S(1)}, bf16[256,2048]{1,0:T(8,128)(2,1)}, u32[]{:S(2)}) copy-start(bf16[256,2048]{1,0:T(8,128)(2,1)} %refs_5_.3) | copy-start | bytes 3145732
  21.0 1.3 %collective-permute-start.7 = (bf16[4,8,640]{2,1,0:T(8,128)(2,1)S(1)}, bf16[4,8,640]{2,1,0:T(8,128)(2,1)S(1)}, u32[]{:S(2)}, u32[]{:S(2)}) collective-permute-start(bf16[4,8,640]{2,1,0:T(8,128)(2,1)S(1)} %pad_maximum_fusion.1), channel_id=1, source_target_pairs={{0,4},{4,0},{8,12},{12,8},{16,20},{20,16},{24,28},{28,24},{1,5},{5... | collective-permute-start | bytes 122888 | tf_op jit(solution)/shard_map/ppermute | solution.py:58
  22.9 5.7 %collective-permute-start.10 = (bf16[8,2048]{1,0:T(8,128)(2,1)S(1)}, bf16[8,2048]{1,0:T(8,128)(2,1)S(1)}, u32[]{:S(2)}, u32[]{:S(2)}) collective-permute-start(bf16[8,2048]{1,0:T(8,128)(2,1)S(1)} %get-tuple-element.36), channel_id=1, source_target_pairs={{0,3},{1,2},{2,1},{3,0},{4,7},{5,6},{6,5},{7,4},{8,11},{9,10},{10,... | collective-permute-start | bytes 98312 | tf_op jit(solution)/shard_map/ppermute | solution.py:58
  26.5 4.1 %collective-permute-start.8 = (bf16[8,2048]{1,0:T(8,128)(2,1)S(1)}, bf16[8,2048]{1,0:T(8,128)(2,1)S(1)}, u32[]{:S(2)}, u32[]{:S(2)}) collective-permute-start(bf16[8,2048]{1,0:T(8,128)(2,1)S(1)} %get-tuple-element.36), channel_id=1, source_target_pairs={{0,1},{1,0},{2,3},{3,2},{4,5},{5,4},{6,7},{7,6},{8,9},{9,8},{10,11... | collective-permute-start | bytes 98312 | tf_op jit(solution)/shard_map/ppermute | solution.py:58
  26.5 5.2 %collective-permute-start.9 = (bf16[8,2048]{1,0:T(8,128)(2,1)S(1)}, bf16[8,2048]{1,0:T(8,128)(2,1)S(1)}, u32[]{:S(2)}, u32[]{:S(2)}) collective-permute-start(bf16[8,2048]{1,0:T(8,128)(2,1)S(1)} %get-tuple-element.36), channel_id=1, source_target_pairs={{0,2},{1,3},{2,0},{3,1},{4,6},{5,7},{6,4},{7,5},{8,10},{9,11},{10,... | collective-permute-start | bytes 98312 | tf_op jit(solution)/shard_map/ppermute | solution.py:58
  31.9 5.1 %collective-permute-start.11 = (bf16[8,2048]{1,0:T(8,128)(2,1)S(1)}, bf16[8,2048]{1,0:T(8,128)(2,1)S(1)}, u32[]{:S(2)}, u32[]{:S(2)}) collective-permute-start(bf16[8,2048]{1,0:T(8,128)(2,1)S(1)} %get-tuple-element.37), channel_id=1, source_target_pairs={{0,24},{4,28},{8,16},{12,20},{16,8},{20,12},{24,0},{28,4},{1,25},{... | collective-permute-start | bytes 98312 | tf_op jit(solution)/shard_map/ppermute | solution.py:58
  34.3 3.9 %collective-permute-start.12 = (bf16[8,2048]{1,0:T(8,128)(2,1)S(1)}, bf16[8,2048]{1,0:T(8,128)(2,1)S(1)}, u32[]{:S(2)}, u32[]{:S(2)}) collective-permute-start(bf16[8,2048]{1,0:T(8,128)(2,1)S(1)} %get-tuple-element.37), channel_id=1, source_target_pairs={{0,16},{4,20},{8,24},{12,28},{16,0},{20,4},{24,8},{28,12},{1,17},{... | collective-permute-start | bytes 98312 | tf_op jit(solution)/shard_map/ppermute | solution.py:58
  34.8 3.9 %collective-permute-start.13 = (bf16[8,2048]{1,0:T(8,128)(2,1)S(1)}, bf16[8,2048]{1,0:T(8,128)(2,1)S(1)}, u32[]{:S(2)}, u32[]{:S(2)}) collective-permute-start(bf16[8,2048]{1,0:T(8,128)(2,1)S(1)} %get-tuple-element.37), channel_id=1, source_target_pairs={{0,8},{4,12},{8,0},{12,4},{16,24},{20,28},{24,16},{28,20},{1,9},{5... | collective-permute-start | bytes 98312 | tf_op jit(solution)/shard_map/ppermute | solution.py:58

commit v6 on v5

--- a/solution.py
+++ b/solution.py
@@ -486,7 +486,7 @@
     landed = scatter_far(sends)
     landed.append(scatter_near(near, landed[1:]))
     part, sent = merge(landed, self_part, out_weight)
-    others = [swap(sent, "tp", m) for m in range(1, tp_count)]
+    others = [swap(sent, "tp", m) for m in [tp_count - 1] + list(range(1, tp_count - 1))]
     normed, columns = middle(part, others, tokens, second_gain[None])
     all_normed = [part[None] for part in [normed] + gather_far(normed)]
     term = mlp(all_normed, up_weight, down_weight, up_peer, down_peer)

time: 50.6 us -> 49.9 us (0.986)
  transfers between devices with their start and end apart: 16 -> 16, of which waited for: 12 -> 11; matrix products, arithmetic and copies ran while one was open for 0% -> 0% of each run, Pallas kernels for 17% -> 17%
where the time goes in v6:
time: 49.9 us; the launch traced here: 49.7 us
  starting transfers between devices  16.5 us (33%)
  waiting for transfers between devices  12.5 us (25%)
  Pallas kernels  10.1 us (20%)
  blocking collectives  9.86 us (20%)
  between operations  0.73 us (1%)
    ppermute x16, starting transfers between devices, swap(): return lax.ppermute(x, axis, [(i, i ^ offset) for i in range(n)])  16.5 us
    ppermute x16, waiting for transfers between devices, swap(): return lax.ppermute(x, axis, [(i, i ^ offset) for i in range(n)])  12.5 us
    all_to_all x1, blocking collectives, body(): lax.all_to_all(term, ('req', 'tp'), split_axis=0, concat_axis=0, tiled=Tr...  9.86 us
    pallas_call x1, Pallas kernels, attend(): pl.pallas_call(functools.partial(attention_kernel, req_count, len(tokens)...  3.91 us
    pallas_call x1, Pallas kernels, load(): pl.pallas_call(functools.partial(load_kernel, len(sources)), out_shape=[p...  2.64 us
    pallas_call x1, Pallas kernels, own_part(): pl.pallas_call(own_kernel, out_shape=[jax.ShapeDtypeStruct((own_rows, hea...  1.26 us
  transfers between devices with their start and end apart: 16, of which 11 were waited for; matrix products, arithmetic and copies ran while one was open for 0% of the time, Pallas kernels for 17%

profile of v6, /device:TPU:0, one launch (start us, length us, event | category | flops | bytes accessed | tf_op | source)
XLA Modules:
  0.0 49.7 jit_solution(7474563862683031357)
XLA Ops:
  0.6 0.5 %collective-permute-start.14 = (bf16[2048,256]{1,0:T(8,128)(2,1)}, bf16[2048,256]{1,0:T(8,128)(2,1)S(1)}, u32[]{:S(2)}, u32[]{:S(2)}) collective-permute-start(bf16[2048,256]{1,0:T(8,128)(2,1)} %refs_4_.3), channel_id=1, source_target_pairs={{0,4},{4,0},{8,12},{12,8},{16,20},{20,16},{24,28},{28,24},{1,5},{5... | collective-permute-start | bytes 3145736 | tf_op jit(solution)/shard_map/ppermute | solution.py:58
  1.2 3.9 %collective-permute-start = (bf16[8,2048]{1,0:T(8,128)(2,1)}, bf16[8,2048]{1,0:T(8,128)(2,1)S(1)}, u32[]{:S(2)}, u32[]{:S(2)}) collective-permute-start(bf16[8,2048]{1,0:T(8,128)(2,1)} %refs_2_.1), channel_id=1, source_target_pairs={{0,24},{4,28},{8,16},{12,20},{16,8},{20,12},{24,0},{28,4},{1,25},{... | collective-permute-start | bytes 98312 | tf_op jit(solution)/shard_map/ppermute | solution.py:58
  5.7 2.6 %load.1 = (bf16[8,2048]{1,0:T(8,128)(2,1)S(1)}, f32[1,2048]{1,0:T(1,128)S(1)}, bf16[2048,512]{1,0:T(8,128)(2,1)S(1)}, bf16[3072,512]{1,0:T(8,128)(2,1)S(1)}, s32[2,64,128]{2,1,0:T(8,128)S(1)}) custom-call(s32[1,64]{1,0:T(1,128)} %bitcast.28, s32[1,64]{1,0:T(1,128)} %bitcast.29, bf16[8,2048]{1,0:T(8,128)(2,1)} %refs_2_.1, f32[1,2048]{1,0:T(1,128)} %bitcast.27, ...), custom_call_target="tpu_custom_call" | custom-call | bytes 6328320 | tf_op jit(solution)/shard_map/load/pallas_call | solution.py:126
  8.3 0.9 %collective-permute-done.1 = bf16[8,2048]{1,0:T(8,128)(2,1)S(1)} collective-permute-done((bf16[8,2048]{1,0:T(8,128)(2,1)}, bf16[8,2048]{1,0:T(8,128)(2,1)S(1)}, u32[]{:S(2)}, u32[]{:S(2)}) %collective-permute-start.1) | collective-permute-done | bytes 32800 | tf_op jit(solution)/shard_map/ppermute | solution.py:58
  9.8 1.3 %collective-permute-done.3.refs_4_ = bf16[4,8,2048]{2,1,0:T(8,128)(2,1)S(1)} collective-permute-done((bf16[4,8,2048]{2,1,0:T(8,128)(2,1)S(1)}, bf16[4,8,2048]{2,1,0:T(8,128)(2,1)S(1)}, u32[]{:S(2)}, u32[]{:S(2)}) %collective-permute-start.3) | collective-permute-done | bytes 131104 | tf_op jit(solution)/shard_map/ppermute | solution.py:58
  11.2 3.9 %attention.1 = (bf16[2,8,640]{2,1,0:T(8,128)(2,1)S(1)}, bf16[2,8,640]{2,1,0:T(8,128)(2,1)S(1)}, bf16[2,8,640]{2,1,0:T(8,128)(2,1)S(1)}, bf16[2,8,640]{2,1,0:T(8,...) custom-call(bf16[1,8,2048]{2,1,0:T(8,128)(2,1)S(1)} %bitcast.14, bf16[1,8,2048]{2,1,0:T(8,128)(2,1)S(1)} %bitcast.16, ...), custom_call_target="tpu_custom_call" | custom-call | tf_op jit(solution)/shard_map/attention/pallas_call | solution.py:264
  15.1 1.6 %collective-permute-start.4 = (bf16[2,8,640]{2,1,0:T(8,128)(2,1)S(1)}, bf16[2,8,640]{2,1,0:T(8,128)(2,1)S(1)}, u32[]{:S(2)}, u32[]{:S(2)}) collective-permute-start(bf16[2,8,640]{2,1,0:T(8,128)(2,1)S(1)} %get-tuple-element.28), channel_id=1, source_target_pairs={{0,24},{4,28},{8,16},{12,20},{16,8},{20,12},{24,0},{28,4},{1,25},{... | collective-permute-start | bytes 61448 | tf_op jit(solution)/shard_map/ppermute | solution.py:58
  17.2 1.4 %collective-permute-start.6 = (bf16[2,8,640]{2,1,0:T(8,128)(2,1)S(1)}, bf16[2,8,640]{2,1,0:T(8,128)(2,1)S(1)}, u32[]{:S(2)}, u32[]{:S(2)}) collective-permute-start(bf16[2,8,640]{2,1,0:T(8,128)(2,1)S(1)} %get-tuple-element.30), channel_id=1, source_target_pairs={{0,8},{4,12},{8,0},{12,4},{16,24},{20,28},{24,16},{28,20},{1,9},{5... | collective-permute-start | bytes 61448 | tf_op jit(solution)/shard_map/ppermute | solution.py:58
  18.7 1.3 %own.1 = (bf16[8,512]{1,0:T(8,128)(2,1)}, bf16[8,512]{1,0:T(8,128)(2,1)}, f32[8,640]{1,0:T(8,128)S(1)}, bf16[8,640]{1,0:T(8,128)(2,1)S(1)}) custom-call(bf16[16,2048]{1,0:T(8,128)(2,1)S(1)} %get-tuple-element.31.normed_ref, f32[16,512]{1,0:T(8,128)S(1)} %get-tuple-element.32.queries_ref, bf16[2048,512]{1,0:T(8,128)(2,1)S(1)} %copy-done, ...), custom_call_target="tpu_custom_call" | custom-call | tf_op jit(solution)/shard_map/own/pallas_call | solution.py:312
  19.9 0.6 %collective-permute-done.5.refs_2_ = bf16[2,8,640]{2,1,0:T(8,128)(2,1)S(1)} collective-permute-done((bf16[2,8,640]{2,1,0:T(8,128)(2,1)S(1)}, bf16[2,8,640]{2,1,0:T(8,128)(2,1)S(1)}, u32[]{:S(2)}, u32[]{:S(2)}) %collective-permute-start.5) | collective-permute-done | bytes 20512 | tf_op jit(solution)/shard_map/ppermute | solution.py:58
  21.1 1.2 %collective-permute-done.7.refs_4_ = bf16[4,8,640]{2,1,0:T(8,128)(2,1)S(1)} collective-permute-done((bf16[4,8,640]{2,1,0:T(8,128)(2,1)S(1)}, bf16[4,8,640]{2,1,0:T(8,128)(2,1)S(1)}, u32[]{:S(2)}, u32[]{:S(2)}) %collective-permute-start.7) | collective-permute-done | bytes 40992 | tf_op jit(solution)/shard_map/ppermute | solution.py:58
  22.3 0.6 %merge.1 = (f32[8,2048]{1,0:T(8,128)S(1)}, bf16[8,2048]{1,0:T(8,128)(2,1)S(1)}) custom-call(bf16[2,8,640]{2,1,0:T(8,128)(2,1)S(1)} %get-tuple-element.27.group_ref.refs_0_, bf16[2,8,640]{2,1,0:T(8,128)(2,1)S(1)} %collective-permute-done.4.refs_1_, bf16[2,8,640]{2,1,0:T(8,128)(2,1)S(1)} %collective-permute-done.5.refs_2_, ...), custom_call_target="tpu_custom_call" | custom-call | tf_op jit(solution)/shard_map/merge/pallas_call | solution.py:360
  22.9 2.6 %collective-permute-start.10 = (bf16[8,2048]{1,0:T(8,128)(2,1)S(1)}, bf16[8,2048]{1,0:T(8,128)(2,1)S(1)}, u32[]{:S(2)}, u32[]{:S(2)}) collective-permute-start(bf16[8,2048]{1,0:T(8,128)(2,1)S(1)} %get-tuple-element.36), channel_id=1, source_target_pairs={{0,2},{1,3},{2,0},{3,1},{4,6},{5,7},{6,4},{7,5},{8,10},{9,11},{10,... | collective-permute-start | bytes 98312 | tf_op jit(solution)/shard_map/ppermute | solution.py:58
  25.5 1.3 %collective-permute-start.8 = (bf16[8,2048]{1,0:T(8,128)(2,1)S(1)}, bf16[8,2048]{1,0:T(8,128)(2,1)S(1)}, u32[]{:S(2)}, u32[]{:S(2)}) collective-permute-start(bf16[8,2048]{1,0:T(8,128)(2,1)S(1)} %get-tuple-element.36), channel_id=1, source_target_pairs={{0,3},{1,2},{2,1},{3,0},{4,7},{5,6},{6,5},{7,4},{8,11},{9,10},{10,... | collective-permute-start | bytes 98312 | tf_op jit(solution)/shard_map/ppermute | solution.py:58
  27.1 1.0 %collective-permute-done.10.refs_3_ = bf16[8,2048]{1,0:T(8,128)(2,1)S(1)} collective-permute-done((bf16[8,2048]{1,0:T(8,128)(2,1)S(1)}, bf16[8,2048]{1,0:T(8,128)(2,1)S(1)}, u32[]{:S(2)}, u32[]{:S(2)}) %collective-permute-start.10) | collective-permute-done | bytes 32800 | tf_op jit(solution)/shard_map/ppermute | solution.py:58
  28.0 3.1 %collective-permute-done.8.refs_1_ = bf16[8,2048]{1,0:T(8,128)(2,1)S(1)} collective-permute-done((bf16[8,2048]{1,0:T(8,128)(2,1)S(1)}, bf16[8,2048]{1,0:T(8,128)(2,1)S(1)}, u32[]{:S(2)}, u32[]{:S(2)}) %collective-permute-start.8) | collective-permute-done | bytes 32800 | tf_op jit(solution)/shard_map/ppermute | solution.py:58
  31.4 2.4 %collective-permute-start.11 = (bf16[8,2048]{1,0:T(8,128)(2,1)S(1)}, bf16[8,2048]{1,0:T(8,128)(2,1)S(1)}, u32[]{:S(2)}, u32[]{:S(2)}) collective-permute-start(bf16[8,2048]{1,0:T(8,128)(2,1)S(1)} %get-tuple-element.37), channel_id=1, source_target_pairs={{0,24},{4,28},{8,16},{12,20},{16,8},{20,12},{24,0},{28,4},{1,25},{... | collective-permute-start | bytes 98312 | tf_op jit(solution)/shard_map/ppermute | solution.py:58
  33.9 0.5 %collective-permute-start.12 = (bf16[8,2048]{1,0:T(8,128)(2,1)S(1)}, bf16[8,2048]{1,0:T(8,128)(2,1)S(1)}, u32[]{:S(2)}, u32[]{:S(2)}) collective-permute-start(bf16[8,2048]{1,0:T(8,128)(2,1)S(1)} %get-tuple-element.37), channel_id=1, source_target_pairs={{0,16},{4,20},{8,24},{12,28},{16,0},{20,4},{24,8},{28,12},{1,17},{... | collective-permute-start | bytes 98312 | tf_op jit(solution)/shard_map/ppermute | solution.py:58
  34.4 0.6 %collective-permute-start.13 = (bf16[8,2048]{1,0:T(8,128)(2,1)S(1)}, bf16[8,2048]{1,0:T(8,128)(2,1)S(1)}, u32[]{:S(2)}, u32[]{:S(2)}) collective-permute-start(bf16[8,2048]{1,0:T(8,128)(2,1)S(1)} %get-tuple-element.37), channel_id=1, source_target_pairs={{0,8},{4,12},{8,0},{12,4},{16,24},{20,28},{24,16},{28,20},{1,9},{5... | collective-permute-start | bytes 98312 | tf_op jit(solution)/shard_map/ppermute | solution.py:58
  35.0 1.5 %collective-permute-done.11 = bf16[8,2048]{1,0:T(8,128)(2,1)S(1)} collective-permute-done((bf16[8,2048]{1,0:T(8,128)(2,1)S(1)}, bf16[8,2048]{1,0:T(8,128)(2,1)S(1)}, u32[]{:S(2)}, u32[]{:S(2)}) %collective-permute-start.11) | collective-permute-done | bytes 32800 | tf_op jit(solution)/shard_map/ppermute | solution.py:58
  36.5 1.3 %collective-permute-done.12 = bf16[8,2048]{1,0:T(8,128)(2,1)S(1)} collective-permute-done((bf16[8,2048]{1,0:T(8,128)(2,1)S(1)}, bf16[8,2048]{1,0:T(8,128)(2,1)S(1)}, u32[]{:S(2)}, u32[]{:S(2)}) %collective-permute-start.12) | collective-permute-done | bytes 32800 | tf_op jit(solution)/shard_map/ppermute | solution.py:58
  38.3 0.9 %mlp.1 = bf16[16,8,512]{2,1,0:T(8,128)(2,1)S(1)} custom-call(bf16[1,8,2048]{2,1,0:T(8,128)(2,1)S(1)} %bitcast.21, bf16[1,8,2048]{2,1,0:T(8,128)(2,1)S(1)} %bitcast.22, bf16[1,8,2048]{2,1,0:T(8,128)(2,1)S(1)} %bitcast.23, bf16[1,8,2048]{2,1,0:T(8,128)(2,1)S(1)} %bitcast.24, bf16[2048,256]{1,0:T(8,128)(2,1)S(1)} %copy-done.3, bf16[256,2048]{1,0:T(8,128)(2,1)S(1)} %copy-done.4, ...), custom_call_target="tpu_custom_call" | custom-call | tf_op jit(solution)/shard_map/mlp/pallas_call | solution.py:422
  39.2 9.9 %all_to_all.5.recv_ref = bf16[16,8,512]{2,1,0:T(8,128)(2,1)S(1)} all-to-all(bf16[16,8,512]{2,1,0:T(8,128)(2,1)S(1)} %mlp.1), channel_id=1, replica_groups={{26,24,8,9,27,16,19,18,1,11,10,25,3,0,17,2},{30,28,12,13,31,20,23,22,5,..., dimensions={0} | all-to-all | bytes 262144 | tf_op jit(solution)/shard_map/all_to_all | solution.py:498
  49.1 0.6 %finish.1 = bf16[8,512]{1,0:T(8,128)(2,1)} custom-call(bf16[16,8,512]{2,1,0:T(8,128)(2,1)S(1)} %all_to_all.5.recv_ref, f32[8,512]{1,0:T(8,128)S(1)} %get-tuple-element.38.columns_ref), custom_call_target="tpu_custom_call" | custom-call | tf_op jit(solution)/shard_map/finish/pallas_call | solution.py:442
  (33 shorter events, 3.3 us)
Async XLA Ops:
  0.6 37.7 %collective-permute-start.14 = (bf16[2048,256]{1,0:T(8,128)(2,1)}, bf16[2048,256]{1,0:T(8,128)(2,1)S(1)}, u32[]{:S(2)}, u32[]{:S(2)}) collective-permute-start(bf16[2048,256]{1,0:T(8,128)(2,1)} %refs_4_.3), channel_id=1, source_target_pairs={{0,4},{4,0},{8,12},{12,8},{16,20},{20,16},{24,28},{28,24},{1,5},{5... | collective-permute-start | bytes 3145736 | tf_op jit(solution)/shard_map/ppermute | solution.py:58
  1.1 37.1 %collective-permute-start.15 = (bf16[256,2048]{1,0:T(8,128)(2,1)}, bf16[256,2048]{1,0:T(8,128)(2,1)S(1)}, u32[]{:S(2)}, u32[]{:S(2)}) collective-permute-start(bf16[256,2048]{1,0:T(8,128)(2,1)} %refs_5_.3), channel_id=1, source_target_pairs={{0,4},{4,0},{8,12},{12,8},{16,20},{20,16},{24,28},{28,24},{1,5},{5... | collective-permute-start | bytes 3145736 | tf_op jit(solution)/shard_map/ppermute | solution.py:58
  1.2 7.1 %collective-permute-start = (bf16[8,2048]{1,0:T(8,128)(2,1)}, bf16[8,2048]{1,0:T(8,128)(2,1)S(1)}, u32[]{:S(2)}, u32[]{:S(2)}) collective-permute-start(bf16[8,2048]{1,0:T(8,128)(2,1)} %refs_2_.1), channel_id=1, source_target_pairs={{0,24},{4,28},{8,16},{12,20},{16,8},{20,12},{24,0},{28,4},{1,25},{... | collective-permute-start | bytes 98312 | tf_op jit(solution)/shard_map/ppermute | solution.py:58
  5.1 4.1 %collective-permute-start.1 = (bf16[8,2048]{1,0:T(8,128)(2,1)}, bf16[8,2048]{1,0:T(8,128)(2,1)S(1)}, u32[]{:S(2)}, u32[]{:S(2)}) collective-permute-start(bf16[8,2048]{1,0:T(8,128)(2,1)} %refs_2_.1), channel_id=1, source_target_pairs={{0,16},{4,20},{8,24},{12,28},{16,0},{20,4},{24,8},{28,12},{1,17},{... | collective-permute-start | bytes 98312 | tf_op jit(solution)/shard_map/ppermute | solution.py:58
  5.6 4.1 %collective-permute-start.2 = (bf16[8,2048]{1,0:T(8,128)(2,1)}, bf16[8,2048]{1,0:T(8,128)(2,1)S(1)}, u32[]{:S(2)}, u32[]{:S(2)}) collective-permute-start(bf16[8,2048]{1,0:T(8,128)(2,1)} %refs_2_.1), channel_id=1, source_target_pairs={{0,8},{4,12},{8,0},{12,4},{16,24},{20,28},{24,16},{28,20},{1,9},{5... | collective-permute-start | bytes 98312 | tf_op jit(solution)/shard_map/ppermute | solution.py:58
  9.8 1.4 %collective-permute-start.3 = (bf16[4,8,2048]{2,1,0:T(8,128)(2,1)S(1)}, bf16[4,8,2048]{2,1,0:T(8,128)(2,1)S(1)}, u32[]{:S(2)}, u32[]{:S(2)}) collective-permute-start(bf16[4,8,2048]{2,1,0:T(8,128)(2,1)S(1)} %pad_maximum_fusion), channel_id=1, source_target_pairs={{0,4},{4,0},{8,12},{12,8},{16,20},{20,16},{24,28},{28,24},{1,5},{5... | collective-permute-start | bytes 393224 | tf_op jit(solution)/shard_map/ppermute | solution.py:58
  11.2 7.5 %copy-start = (bf16[2048,512]{1,0:T(8,128)(2,1)S(1)}, bf16[2048,512]{1,0:T(8,128)(2,1)}, u32[]{:S(2)}) copy-start(bf16[2048,512]{1,0:T(8,128)(2,1)} %wk.1) | copy-start | bytes 6291460
  11.2 7.5 %copy-start.1 = (bf16[2048,512]{1,0:T(8,128)(2,1)S(1)}, bf16[2048,512]{1,0:T(8,128)(2,1)}, u32[]{:S(2)}) copy-start(bf16[2048,512]{1,0:T(8,128)(2,1)} %wv.1) | copy-start | bytes 6291460
  15.1 4.8 %collective-permute-start.4 = (bf16[2,8,640]{2,1,0:T(8,128)(2,1)S(1)}, bf16[2,8,640]{2,1,0:T(8,128)(2,1)S(1)}, u32[]{:S(2)}, u32[]{:S(2)}) collective-permute-start(bf16[2,8,640]{2,1,0:T(8,128)(2,1)S(1)} %get-tuple-element.28), channel_id=1, source_target_pairs={{0,24},{4,28},{8,16},{12,20},{16,8},{20,12},{24,0},{28,4},{1,25},{... | collective-permute-start | bytes 61448 | tf_op jit(solution)/shard_map/ppermute | solution.py:58
  16.7 3.8 %collective-permute-start.5 = (bf16[2,8,640]{2,1,0:T(8,128)(2,1)S(1)}, bf16[2,8,640]{2,1,0:T(8,128)(2,1)S(1)}, u32[]{:S(2)}, u32[]{:S(2)}) collective-permute-start(bf16[2,8,640]{2,1,0:T(8,128)(2,1)S(1)} %get-tuple-element.29), channel_id=1, source_target_pairs={{0,16},{4,20},{8,24},{12,28},{16,0},{20,4},{24,8},{28,12},{1,17},{... | collective-permute-start | bytes 61448 | tf_op jit(solution)/shard_map/ppermute | solution.py:58
  17.2 3.8 %collective-permute-start.6 = (bf16[2,8,640]{2,1,0:T(8,128)(2,1)S(1)}, bf16[2,8,640]{2,1,0:T(8,128)(2,1)S(1)}, u32[]{:S(2)}, u32[]{:S(2)}) collective-permute-start(bf16[2,8,640]{2,1,0:T(8,128)(2,1)S(1)} %get-tuple-element.30), channel_id=1, source_target_pairs={{0,8},{4,12},{8,0},{12,4},{16,24},{20,28},{24,16},{28,20},{1,9},{5... | collective-permute-start | bytes 61448 | tf_op jit(solution)/shard_map/ppermute | solution.py:58
  18.7 3.6 %copy-start.2 = (bf16[512,2048]{1,0:T(8,128)(2,1)S(1)}, bf16[512,2048]{1,0:T(8,128)(2,1)}, u32[]{:S(2)}) copy-start(bf16[512,2048]{1,0:T(8,128)(2,1)} %refs_6_.1) | copy-start | bytes 6291460
  19.9 11.3 %copy-start.5 = (f32[2048]{0:T(1024)S(1)}, f32[2048]{0:T(1024)}, u32[]{:S(2)}) copy-start(f32[2048]{0:T(1024)} %param.19) | copy-start | bytes 24580
  19.9 18.4 %copy-start.3 = (bf16[2048,256]{1,0:T(8,128)(2,1)S(1)}, bf16[2048,256]{1,0:T(8,128)(2,1)}, u32[]{:S(2)}) copy-start(bf16[2048,256]{1,0:T(8,128)(2,1)} %refs_4_.3) | copy-start | bytes 3145732
  19.9 18.4 %copy-start.4 = (bf16[256,2048]{1,0:T(8,128)(2,1)S(1)}, bf16[256,2048]{1,0:T(8,128)(2,1)}, u32[]{:S(2)}) copy-start(bf16[256,2048]{1,0:T(8,128)(2,1)} %refs_5_.3) | copy-start | bytes 3145732
  21.0 1.3 %collective-permute-start.7 = (bf16[4,8,640]{2,1,0:T(8,128)(2,1)S(1)}, bf16[4,8,640]{2,1,0:T(8,128)(2,1)S(1)}, u32[]{:S(2)}, u32[]{:S(2)}) collective-permute-start(bf16[4,8,640]{2,1,0:T(8,128)(2,1)S(1)} %pad_maximum_fusion.1), channel_id=1, source_target_pairs={{0,4},{4,0},{8,12},{12,8},{16,20},{20,16},{24,28},{28,24},{1,5},{5... | collective-permute-start | bytes 122888 | tf_op jit(solution)/shard_map/ppermute | solution.py:58
  22.9 5.2 %collective-permute-start.10 = (bf16[8,2048]{1,0:T(8,128)(2,1)S(1)}, bf16[8,2048]{1,0:T(8,128)(2,1)S(1)}, u32[]{:S(2)}, u32[]{:S(2)}) collective-permute-start(bf16[8,2048]{1,0:T(8,128)(2,1)S(1)} %get-tuple-element.36), channel_id=1, source_target_pairs={{0,2},{1,3},{2,0},{3,1},{4,6},{5,7},{6,4},{7,5},{8,10},{9,11},{10,... | collective-permute-start | bytes 98312 | tf_op jit(solution)/shard_map/ppermute | solution.py:58
  25.5 5.7 %collective-permute-start.8 = (bf16[8,2048]{1,0:T(8,128)(2,1)S(1)}, bf16[8,2048]{1,0:T(8,128)(2,1)S(1)}, u32[]{:S(2)}, u32[]{:S(2)}) collective-permute-start(bf16[8,2048]{1,0:T(8,128)(2,1)S(1)} %get-tuple-element.36), channel_id=1, source_target_pairs={{0,3},{1,2},{2,1},{3,0},{4,7},{5,6},{6,5},{7,4},{8,11},{9,10},{10,... | collective-permute-start | bytes 98312 | tf_op jit(solution)/shard_map/ppermute | solution.py:58
  26.8 4.4 %collective-permute-start.9 = (bf16[8,2048]{1,0:T(8,128)(2,1)S(1)}, bf16[8,2048]{1,0:T(8,128)(2,1)S(1)}, u32[]{:S(2)}, u32[]{:S(2)}) collective-permute-start(bf16[8,2048]{1,0:T(8,128)(2,1)S(1)} %get-tuple-element.36), channel_id=1, source_target_pairs={{0,1},{1,0},{2,3},{3,2},{4,5},{5,4},{6,7},{7,6},{8,9},{9,8},{10,11... | collective-permute-start | bytes 98312 | tf_op jit(solution)/shard_map/ppermute | solution.py:58
  31.4 5.1 %collective-permute-start.11 = (bf16[8,2048]{1,0:T(8,128)(2,1)S(1)}, bf16[8,2048]{1,0:T(8,128)(2,1)S(1)}, u32[]{:S(2)}, u32[]{:S(2)}) collective-permute-start(bf16[8,2048]{1,0:T(8,128)(2,1)S(1)} %get-tuple-element.37), channel_id=1, source_target_pairs={{0,24},{4,28},{8,16},{12,20},{16,8},{20,12},{24,0},{28,4},{1,25},{... | collective-permute-start | bytes 98312 | tf_op jit(solution)/shard_map/ppermute | solution.py:58
  33.9 3.9 %collective-permute-start.12 = (bf16[8,2048]{1,0:T(8,128)(2,1)S(1)}, bf16[8,2048]{1,0:T(8,128)(2,1)S(1)}, u32[]{:S(2)}, u32[]{:S(2)}) collective-permute-start(bf16[8,2048]{1,0:T(8,128)(2,1)S(1)} %get-tuple-element.37), channel_id=1, source_target_pairs={{0,16},{4,20},{8,24},{12,28},{16,0},{20,4},{24,8},{28,12},{1,17},{... | collective-permute-start | bytes 98312 | tf_op jit(solution)/shard_map/ppermute | solution.py:58
  34.4 3.9 %collective-permute-start.13 = (bf16[8,2048]{1,0:T(8,128)(2,1)S(1)}, bf16[8,2048]{1,0:T(8,128)(2,1)S(1)}, u32[]{:S(2)}, u32[]{:S(2)}) collective-permute-start(bf16[8,2048]{1,0:T(8,128)(2,1)S(1)} %get-tuple-element.37), channel_id=1, source_target_pairs={{0,8},{4,12},{8,0},{12,4},{16,24},{20,28},{24,16},{28,20},{1,9},{5... | collective-permute-start | bytes 98312 | tf_op jit(solution)/shard_map/ppermute | solution.py:58

commit v7 on v6

--- a/solution.py
+++ b/solution.py
@@ -45,7 +45,7 @@
     return first.astype(jnp.int32), (first + lens_col).astype(jnp.int32)
 
 
-TERM_ORDER = (14, 12, 4, 5, 15, 8, 11, 10, 1, 7, 6, 13, 3, 0, 9, 2)
+TERM_ORDER = (10, 11, 0, 2, 9, 14, 7, 4, 5, 6, 3, 13, 15, 8, 12, 1)
 
 
 def term_order(req_count, tp_count):

time: 49.9 us -> 49.4 us (0.990)
  blocking collectives: 9.86 us -> 9.36 us
where the time goes in v7:
time: 49.4 us; the launch traced here: 49.2 us
  starting transfers between devices  16.5 us (33%)
  waiting for transfers between devices  12.5 us (25%)
  Pallas kernels  10.1 us (20%)
  blocking collectives  9.36 us (19%)
  between operations  0.73 us (1%)
    ppermute x16, starting transfers between devices, swap(): return lax.ppermute(x, axis, [(i, i ^ offset) for i in range(n)])  16.5 us
    ppermute x16, waiting for transfers between devices, swap(): return lax.ppermute(x, axis, [(i, i ^ offset) for i in range(n)])  12.5 us
    all_to_all x1, blocking collectives, body(): lax.all_to_all(term, ('req', 'tp'), split_axis=0, concat_axis=0, tiled=Tr...  9.36 us
    pallas_call x1, Pallas kernels, attend(): pl.pallas_call(functools.partial(attention_kernel, req_count, len(tokens)...  3.91 us
    pallas_call x1, Pallas kernels, load(): pl.pallas_call(functools.partial(load_kernel, len(sources)), out_shape=[p...  2.64 us
    pallas_call x1, Pallas kernels, own_part(): pl.pallas_call(own_kernel, out_shape=[jax.ShapeDtypeStruct((own_rows, hea...  1.26 us
  transfers between devices with their start and end apart: 16, of which 11 were waited for; matrix products, arithmetic and copies ran while one was open for 0% of the time, Pallas kernels for 17%

profile of v7, /device:TPU:0, one launch (start us, length us, event | category | flops | bytes accessed | tf_op | source)
XLA Modules:
  0.0 49.2 jit_solution(3118640634794614732)
XLA Ops:
  0.6 0.5 %collective-permute-start.14 = (bf16[2048,256]{1,0:T(8,128)(2,1)}, bf16[2048,256]{1,0:T(8,128)(2,1)S(1)}, u32[]{:S(2)}, u32[]{:S(2)}) collective-permute-start(bf16[2048,256]{1,0:T(8,128)(2,1)} %refs_4_.3), channel_id=1, source_target_pairs={{0,4},{4,0},{8,12},{12,8},{16,20},{20,16},{24,28},{28,24},{1,5},{5... | collective-permute-start | bytes 3145736 | tf_op jit(solution)/shard_map/ppermute | solution.py:58
  1.2 3.9 %collective-permute-start = (bf16[8,2048]{1,0:T(8,128)(2,1)}, bf16[8,2048]{1,0:T(8,128)(2,1)S(1)}, u32[]{:S(2)}, u32[]{:S(2)}) collective-permute-start(bf16[8,2048]{1,0:T(8,128)(2,1)} %refs_2_.1), channel_id=1, source_target_pairs={{0,24},{4,28},{8,16},{12,20},{16,8},{20,12},{24,0},{28,4},{1,25},{... | collective-permute-start | bytes 98312 | tf_op jit(solution)/shard_map/ppermute | solution.py:58
  5.7 2.6 %load.1 = (bf16[8,2048]{1,0:T(8,128)(2,1)S(1)}, f32[1,2048]{1,0:T(1,128)S(1)}, bf16[2048,512]{1,0:T(8,128)(2,1)S(1)}, bf16[3072,512]{1,0:T(8,128)(2,1)S(1)}, s32[2,64,128]{2,1,0:T(8,128)S(1)}) custom-call(s32[1,64]{1,0:T(1,128)} %bitcast.28, s32[1,64]{1,0:T(1,128)} %bitcast.29, bf16[8,2048]{1,0:T(8,128)(2,1)} %refs_2_.1, f32[1,2048]{1,0:T(1,128)} %bitcast.27, ...), custom_call_target="tpu_custom_call" | custom-call | bytes 6328320 | tf_op jit(solution)/shard_map/load/pallas_call | solution.py:126
  8.3 0.9 %collective-permute-done.1 = bf16[8,2048]{1,0:T(8,128)(2,1)S(1)} collective-permute-done((bf16[8,2048]{1,0:T(8,128)(2,1)}, bf16[8,2048]{1,0:T(8,128)(2,1)S(1)}, u32[]{:S(2)}, u32[]{:S(2)}) %collective-permute-start.1) | collective-permute-done | bytes 32800 | tf_op jit(solution)/shard_map/ppermute | solution.py:58
  9.8 1.3 %collective-permute-done.3.refs_4_ = bf16[4,8,2048]{2,1,0:T(8,128)(2,1)S(1)} collective-permute-done((bf16[4,8,2048]{2,1,0:T(8,128)(2,1)S(1)}, bf16[4,8,2048]{2,1,0:T(8,128)(2,1)S(1)}, u32[]{:S(2)}, u32[]{:S(2)}) %collective-permute-start.3) | collective-permute-done | bytes 131104 | tf_op jit(solution)/shard_map/ppermute | solution.py:58
  11.2 3.9 %attention.1 = (bf16[2,8,640]{2,1,0:T(8,128)(2,1)S(1)}, bf16[2,8,640]{2,1,0:T(8,128)(2,1)S(1)}, bf16[2,8,640]{2,1,0:T(8,128)(2,1)S(1)}, bf16[2,8,640]{2,1,0:T(8,...) custom-call(bf16[1,8,2048]{2,1,0:T(8,128)(2,1)S(1)} %bitcast.14, bf16[1,8,2048]{2,1,0:T(8,128)(2,1)S(1)} %bitcast.16, ...), custom_call_target="tpu_custom_call" | custom-call | tf_op jit(solution)/shard_map/attention/pallas_call | solution.py:264
  15.1 1.6 %collective-permute-start.4 = (bf16[2,8,640]{2,1,0:T(8,128)(2,1)S(1)}, bf16[2,8,640]{2,1,0:T(8,128)(2,1)S(1)}, u32[]{:S(2)}, u32[]{:S(2)}) collective-permute-start(bf16[2,8,640]{2,1,0:T(8,128)(2,1)S(1)} %get-tuple-element.28), channel_id=1, source_target_pairs={{0,24},{4,28},{8,16},{12,20},{16,8},{20,12},{24,0},{28,4},{1,25},{... | collective-permute-start | bytes 61448 | tf_op jit(solution)/shard_map/ppermute | solution.py:58
  17.2 1.4 %collective-permute-start.6 = (bf16[2,8,640]{2,1,0:T(8,128)(2,1)S(1)}, bf16[2,8,640]{2,1,0:T(8,128)(2,1)S(1)}, u32[]{:S(2)}, u32[]{:S(2)}) collective-permute-start(bf16[2,8,640]{2,1,0:T(8,128)(2,1)S(1)} %get-tuple-element.30), channel_id=1, source_target_pairs={{0,8},{4,12},{8,0},{12,4},{16,24},{20,28},{24,16},{28,20},{1,9},{5... | collective-permute-start | bytes 61448 | tf_op jit(solution)/shard_map/ppermute | solution.py:58
  18.7 1.3 %own.1 = (bf16[8,512]{1,0:T(8,128)(2,1)}, bf16[8,512]{1,0:T(8,128)(2,1)}, f32[8,640]{1,0:T(8,128)S(1)}, bf16[8,640]{1,0:T(8,128)(2,1)S(1)}) custom-call(bf16[16,2048]{1,0:T(8,128)(2,1)S(1)} %get-tuple-element.31.normed_ref, f32[16,512]{1,0:T(8,128)S(1)} %get-tuple-element.32.queries_ref, bf16[2048,512]{1,0:T(8,128)(2,1)S(1)} %copy-done, ...), custom_call_target="tpu_custom_call" | custom-call | tf_op jit(solution)/shard_map/own/pallas_call | solution.py:312
  19.9 0.6 %collective-permute-done.5.refs_2_ = bf16[2,8,640]{2,1,0:T(8,128)(2,1)S(1)} collective-permute-done((bf16[2,8,640]{2,1,0:T(8,128)(2,1)S(1)}, bf16[2,8,640]{2,1,0:T(8,128)(2,1)S(1)}, u32[]{:S(2)}, u32[]{:S(2)}) %collective-permute-start.5) | collective-permute-done | bytes 20512 | tf_op jit(solution)/shard_map/ppermute | solution.py:58
  21.1 1.2 %collective-permute-done.7.refs_4_ = bf16[4,8,640]{2,1,0:T(8,128)(2,1)S(1)} collective-permute-done((bf16[4,8,640]{2,1,0:T(8,128)(2,1)S(1)}, bf16[4,8,640]{2,1,0:T(8,128)(2,1)S(1)}, u32[]{:S(2)}, u32[]{:S(2)}) %collective-permute-start.7) | collective-permute-done | bytes 40992 | tf_op jit(solution)/shard_map/ppermute | solution.py:58
  22.3 0.6 %merge.1 = (f32[8,2048]{1,0:T(8,128)S(1)}, bf16[8,2048]{1,0:T(8,128)(2,1)S(1)}) custom-call(bf16[2,8,640]{2,1,0:T(8,128)(2,1)S(1)} %get-tuple-element.27.group_ref.refs_0_, bf16[2,8,640]{2,1,0:T(8,128)(2,1)S(1)} %collective-permute-done.4.refs_1_, bf16[2,8,640]{2,1,0:T(8,128)(2,1)S(1)} %collective-permute-done.5.refs_2_, ...), custom_call_target="tpu_custom_call" | custom-call | tf_op jit(solution)/shard_map/merge/pallas_call | solution.py:360
  22.9 2.6 %collective-permute-start.10 = (bf16[8,2048]{1,0:T(8,128)(2,1)S(1)}, bf16[8,2048]{1,0:T(8,128)(2,1)S(1)}, u32[]{:S(2)}, u32[]{:S(2)}) collective-permute-start(bf16[8,2048]{1,0:T(8,128)(2,1)S(1)} %get-tuple-element.36), channel_id=1, source_target_pairs={{0,2},{1,3},{2,0},{3,1},{4,6},{5,7},{6,4},{7,5},{8,10},{9,11},{10,... | collective-permute-start | bytes 98312 | tf_op jit(solution)/shard_map/ppermute | solution.py:58
  25.5 1.3 %collective-permute-start.8 = (bf16[8,2048]{1,0:T(8,128)(2,1)S(1)}, bf16[8,2048]{1,0:T(8,128)(2,1)S(1)}, u32[]{:S(2)}, u32[]{:S(2)}) collective-permute-start(bf16[8,2048]{1,0:T(8,128)(2,1)S(1)} %get-tuple-element.36), channel_id=1, source_target_pairs={{0,3},{1,2},{2,1},{3,0},{4,7},{5,6},{6,5},{7,4},{8,11},{9,10},{10,... | collective-permute-start | bytes 98312 | tf_op jit(solution)/shard_map/ppermute | solution.py:58
  27.1 1.0 %collective-permute-done.10.refs_3_ = bf16[8,2048]{1,0:T(8,128)(2,1)S(1)} collective-permute-done((bf16[8,2048]{1,0:T(8,128)(2,1)S(1)}, bf16[8,2048]{1,0:T(8,128)(2,1)S(1)}, u32[]{:S(2)}, u32[]{:S(2)}) %collective-permute-start.10) | collective-permute-done | bytes 32800 | tf_op jit(solution)/shard_map/ppermute | solution.py:58
  28.0 3.1 %collective-permute-done.8.refs_1_ = bf16[8,2048]{1,0:T(8,128)(2,1)S(1)} collective-permute-done((bf16[8,2048]{1,0:T(8,128)(2,1)S(1)}, bf16[8,2048]{1,0:T(8,128)(2,1)S(1)}, u32[]{:S(2)}, u32[]{:S(2)}) %collective-permute-start.8) | collective-permute-done | bytes 32800 | tf_op jit(solution)/shard_map/ppermute | solution.py:58
  31.4 2.4 %collective-permute-start.11 = (bf16[8,2048]{1,0:T(8,128)(2,1)S(1)}, bf16[8,2048]{1,0:T(8,128)(2,1)S(1)}, u32[]{:S(2)}, u32[]{:S(2)}) collective-permute-start(bf16[8,2048]{1,0:T(8,128)(2,1)S(1)} %get-tuple-element.37), channel_id=1, source_target_pairs={{0,24},{4,28},{8,16},{12,20},{16,8},{20,12},{24,0},{28,4},{1,25},{... | collective-permute-start | bytes 98312 | tf_op jit(solution)/shard_map/ppermute | solution.py:58
  33.9 0.5 %collective-permute-start.12 = (bf16[8,2048]{1,0:T(8,128)(2,1)S(1)}, bf16[8,2048]{1,0:T(8,128)(2,1)S(1)}, u32[]{:S(2)}, u32[]{:S(2)}) collective-permute-start(bf16[8,2048]{1,0:T(8,128)(2,1)S(1)} %get-tuple-element.37), channel_id=1, source_target_pairs={{0,16},{4,20},{8,24},{12,28},{16,0},{20,4},{24,8},{28,12},{1,17},{... | collective-permute-start | bytes 98312 | tf_op jit(solution)/shard_map/ppermute | solution.py:58
  34.4 0.6 %collective-permute-start.13 = (bf16[8,2048]{1,0:T(8,128)(2,1)S(1)}, bf16[8,2048]{1,0:T(8,128)(2,1)S(1)}, u32[]{:S(2)}, u32[]{:S(2)}) collective-permute-start(bf16[8,2048]{1,0:T(8,128)(2,1)S(1)} %get-tuple-element.37), channel_id=1, source_target_pairs={{0,8},{4,12},{8,0},{12,4},{16,24},{20,28},{24,16},{28,20},{1,9},{5... | collective-permute-start | bytes 98312 | tf_op jit(solution)/shard_map/ppermute | solution.py:58
  35.0 1.5 %collective-permute-done.11 = bf16[8,2048]{1,0:T(8,128)(2,1)S(1)} collective-permute-done((bf16[8,2048]{1,0:T(8,128)(2,1)S(1)}, bf16[8,2048]{1,0:T(8,128)(2,1)S(1)}, u32[]{:S(2)}, u32[]{:S(2)}) %collective-permute-start.11) | collective-permute-done | bytes 32800 | tf_op jit(solution)/shard_map/ppermute | solution.py:58
  36.5 1.3 %collective-permute-done.12 = bf16[8,2048]{1,0:T(8,128)(2,1)S(1)} collective-permute-done((bf16[8,2048]{1,0:T(8,128)(2,1)S(1)}, bf16[8,2048]{1,0:T(8,128)(2,1)S(1)}, u32[]{:S(2)}, u32[]{:S(2)}) %collective-permute-start.12) | collective-permute-done | bytes 32800 | tf_op jit(solution)/shard_map/ppermute | solution.py:58
  38.3 0.9 %mlp.1 = bf16[16,8,512]{2,1,0:T(8,128)(2,1)S(1)} custom-call(bf16[1,8,2048]{2,1,0:T(8,128)(2,1)S(1)} %bitcast.21, bf16[1,8,2048]{2,1,0:T(8,128)(2,1)S(1)} %bitcast.22, bf16[1,8,2048]{2,1,0:T(8,128)(2,1)S(1)} %bitcast.23, bf16[1,8,2048]{2,1,0:T(8,128)(2,1)S(1)} %bitcast.24, bf16[2048,256]{1,0:T(8,128)(2,1)S(1)} %copy-done.3, bf16[256,2048]{1,0:T(8,128)(2,1)S(1)} %copy-done.4, ...), custom_call_target="tpu_custom_call" | custom-call | tf_op jit(solution)/shard_map/mlp/pallas_call | solution.py:422
  39.2 9.4 %all_to_all.5.recv_ref = bf16[16,8,512]{2,1,0:T(8,128)(2,1)S(1)} all-to-all(bf16[16,8,512]{2,1,0:T(8,128)(2,1)S(1)} %mlp.1), channel_id=1, replica_groups={{18,19,0,2,17,26,11,8,9,10,3,25,27,16,24,1},{22,23,4,6,21,30,15,12,13,1..., dimensions={0} | all-to-all | bytes 262144 | tf_op jit(solution)/shard_map/all_to_all | solution.py:498
  48.6 0.6 %finish.1 = bf16[8,512]{1,0:T(8,128)(2,1)} custom-call(bf16[16,8,512]{2,1,0:T(8,128)(2,1)S(1)} %all_to_all.5.recv_ref, f32[8,512]{1,0:T(8,128)S(1)} %get-tuple-element.38.columns_ref), custom_call_target="tpu_custom_call" | custom-call | tf_op jit(solution)/shard_map/finish/pallas_call | solution.py:442
  (33 shorter events, 3.3 us)
Async XLA Ops:
  0.6 37.7 %collective-permute-start.14 = (bf16[2048,256]{1,0:T(8,128)(2,1)}, bf16[2048,256]{1,0:T(8,128)(2,1)S(1)}, u32[]{:S(2)}, u32[]{:S(2)}) collective-permute-start(bf16[2048,256]{1,0:T(8,128)(2,1)} %refs_4_.3), channel_id=1, source_target_pairs={{0,4},{4,0},{8,12},{12,8},{16,20},{20,16},{24,28},{28,24},{1,5},{5... | collective-permute-start | bytes 3145736 | tf_op jit(solution)/shard_map/ppermute | solution.py:58
  1.1 37.1 %collective-permute-start.15 = (bf16[256,2048]{1,0:T(8,128)(2,1)}, bf16[256,2048]{1,0:T(8,128)(2,1)S(1)}, u32[]{:S(2)}, u32[]{:S(2)}) collective-permute-start(bf16[256,2048]{1,0:T(8,128)(2,1)} %refs_5_.3), channel_id=1, source_target_pairs={{0,4},{4,0},{8,12},{12,8},{16,20},{20,16},{24,28},{28,24},{1,5},{5... | collective-permute-start | bytes 3145736 | tf_op jit(solution)/shard_map/ppermute | solution.py:58
  1.2 7.1 %collective-permute-start = (bf16[8,2048]{1,0:T(8,128)(2,1)}, bf16[8,2048]{1,0:T(8,128)(2,1)S(1)}, u32[]{:S(2)}, u32[]{:S(2)}) collective-permute-start(bf16[8,2048]{1,0:T(8,128)(2,1)} %refs_2_.1), channel_id=1, source_target_pairs={{0,24},{4,28},{8,16},{12,20},{16,8},{20,12},{24,0},{28,4},{1,25},{... | collective-permute-start | bytes 98312 | tf_op jit(solution)/shard_map/ppermute | solution.py:58
  5.1 4.1 %collective-permute-start.1 = (bf16[8,2048]{1,0:T(8,128)(2,1)}, bf16[8,2048]{1,0:T(8,128)(2,1)S(1)}, u32[]{:S(2)}, u32[]{:S(2)}) collective-permute-start(bf16[8,2048]{1,0:T(8,128)(2,1)} %refs_2_.1), channel_id=1, source_target_pairs={{0,16},{4,20},{8,24},{12,28},{16,0},{20,4},{24,8},{28,12},{1,17},{... | collective-permute-start | bytes 98312 | tf_op jit(solution)/shard_map/ppermute | solution.py:58
  5.6 4.1 %collective-permute-start.2 = (bf16[8,2048]{1,0:T(8,128)(2,1)}, bf16[8,2048]{1,0:T(8,128)(2,1)S(1)}, u32[]{:S(2)}, u32[]{:S(2)}) collective-permute-start(bf16[8,2048]{1,0:T(8,128)(2,1)} %refs_2_.1), channel_id=1, source_target_pairs={{0,8},{4,12},{8,0},{12,4},{16,24},{20,28},{24,16},{28,20},{1,9},{5... | collective-permute-start | bytes 98312 | tf_op jit(solution)/shard_map/ppermute | solution.py:58
  9.8 1.4 %collective-permute-start.3 = (bf16[4,8,2048]{2,1,0:T(8,128)(2,1)S(1)}, bf16[4,8,2048]{2,1,0:T(8,128)(2,1)S(1)}, u32[]{:S(2)}, u32[]{:S(2)}) collective-permute-start(bf16[4,8,2048]{2,1,0:T(8,128)(2,1)S(1)} %pad_maximum_fusion), channel_id=1, source_target_pairs={{0,4},{4,0},{8,12},{12,8},{16,20},{20,16},{24,28},{28,24},{1,5},{5... | collective-permute-start | bytes 393224 | tf_op jit(solution)/shard_map/ppermute | solution.py:58
  11.2 7.5 %copy-start = (bf16[2048,512]{1,0:T(8,128)(2,1)S(1)}, bf16[2048,512]{1,0:T(8,128)(2,1)}, u32[]{:S(2)}) copy-start(bf16[2048,512]{1,0:T(8,128)(2,1)} %wk.1) | copy-start | bytes 6291460
  11.2 7.5 %copy-start.1 = (bf16[2048,512]{1,0:T(8,128)(2,1)S(1)}, bf16[2048,512]{1,0:T(8,128)(2,1)}, u32[]{:S(2)}) copy-start(bf16[2048,512]{1,0:T(8,128)(2,1)} %wv.1) | copy-start | bytes 6291460
  15.1 4.8 %collective-permute-start.4 = (bf16[2,8,640]{2,1,0:T(8,128)(2,1)S(1)}, bf16[2,8,640]{2,1,0:T(8,128)(2,1)S(1)}, u32[]{:S(2)}, u32[]{:S(2)}) collective-permute-start(bf16[2,8,640]{2,1,0:T(8,128)(2,1)S(1)} %get-tuple-element.28), channel_id=1, source_target_pairs={{0,24},{4,28},{8,16},{12,20},{16,8},{20,12},{24,0},{28,4},{1,25},{... | collective-permute-start | bytes 61448 | tf_op jit(solution)/shard_map/ppermute | solution.py:58
  16.7 3.8 %collective-permute-start.5 = (bf16[2,8,640]{2,1,0:T(8,128)(2,1)S(1)}, bf16[2,8,640]{2,1,0:T(8,128)(2,1)S(1)}, u32[]{:S(2)}, u32[]{:S(2)}) collective-permute-start(bf16[2,8,640]{2,1,0:T(8,128)(2,1)S(1)} %get-tuple-element.29), channel_id=1, source_target_pairs={{0,16},{4,20},{8,24},{12,28},{16,0},{20,4},{24,8},{28,12},{1,17},{... | collective-permute-start | bytes 61448 | tf_op jit(solution)/shard_map/ppermute | solution.py:58
  17.2 3.8 %collective-permute-start.6 = (bf16[2,8,640]{2,1,0:T(8,128)(2,1)S(1)}, bf16[2,8,640]{2,1,0:T(8,128)(2,1)S(1)}, u32[]{:S(2)}, u32[]{:S(2)}) collective-permute-start(bf16[2,8,640]{2,1,0:T(8,128)(2,1)S(1)} %get-tuple-element.30), channel_id=1, source_target_pairs={{0,8},{4,12},{8,0},{12,4},{16,24},{20,28},{24,16},{28,20},{1,9},{5... | collective-permute-start | bytes 61448 | tf_op jit(solution)/shard_map/ppermute | solution.py:58
  18.7 3.6 %copy-start.2 = (bf16[512,2048]{1,0:T(8,128)(2,1)S(1)}, bf16[512,2048]{1,0:T(8,128)(2,1)}, u32[]{:S(2)}) copy-start(bf16[512,2048]{1,0:T(8,128)(2,1)} %refs_6_.1) | copy-start | bytes 6291460
  19.9 11.3 %copy-start.5 = (f32[2048]{0:T(1024)S(1)}, f32[2048]{0:T(1024)}, u32[]{:S(2)}) copy-start(f32[2048]{0:T(1024)} %param.19) | copy-start | bytes 24580
  19.9 18.4 %copy-start.3 = (bf16[2048,256]{1,0:T(8,128)(2,1)S(1)}, bf16[2048,256]{1,0:T(8,128)(2,1)}, u32[]{:S(2)}) copy-start(bf16[2048,256]{1,0:T(8,128)(2,1)} %refs_4_.3) | copy-start | bytes 3145732
  19.9 18.4 %copy-start.4 = (bf16[256,2048]{1,0:T(8,128)(2,1)S(1)}, bf16[256,2048]{1,0:T(8,128)(2,1)}, u32[]{:S(2)}) copy-start(bf16[256,2048]{1,0:T(8,128)(2,1)} %refs_5_.3) | copy-start | bytes 3145732
  21.0 1.3 %collective-permute-start.7 = (bf16[4,8,640]{2,1,0:T(8,128)(2,1)S(1)}, bf16[4,8,640]{2,1,0:T(8,128)(2,1)S(1)}, u32[]{:S(2)}, u32[]{:S(2)}) collective-permute-start(bf16[4,8,640]{2,1,0:T(8,128)(2,1)S(1)} %pad_maximum_fusion.1), channel_id=1, source_target_pairs={{0,4},{4,0},{8,12},{12,8},{16,20},{20,16},{24,28},{28,24},{1,5},{5... | collective-permute-start | bytes 122888 | tf_op jit(solution)/shard_map/ppermute | solution.py:58
  22.9 5.2 %collective-permute-start.10 = (bf16[8,2048]{1,0:T(8,128)(2,1)S(1)}, bf16[8,2048]{1,0:T(8,128)(2,1)S(1)}, u32[]{:S(2)}, u32[]{:S(2)}) collective-permute-start(bf16[8,2048]{1,0:T(8,128)(2,1)S(1)} %get-tuple-element.36), channel_id=1, source_target_pairs={{0,2},{1,3},{2,0},{3,1},{4,6},{5,7},{6,4},{7,5},{8,10},{9,11},{10,... | collective-permute-start | bytes 98312 | tf_op jit(solution)/shard_map/ppermute | solution.py:58
  25.5 5.7 %collective-permute-start.8 = (bf16[8,2048]{1,0:T(8,128)(2,1)S(1)}, bf16[8,2048]{1,0:T(8,128)(2,1)S(1)}, u32[]{:S(2)}, u32[]{:S(2)}) collective-permute-start(bf16[8,2048]{1,0:T(8,128)(2,1)S(1)} %get-tuple-element.36), channel_id=1, source_target_pairs={{0,3},{1,2},{2,1},{3,0},{4,7},{5,6},{6,5},{7,4},{8,11},{9,10},{10,... | collective-permute-start | bytes 98312 | tf_op jit(solution)/shard_map/ppermute | solution.py:58
  26.8 4.4 %collective-permute-start.9 = (bf16[8,2048]{1,0:T(8,128)(2,1)S(1)}, bf16[8,2048]{1,0:T(8,128)(2,1)S(1)}, u32[]{:S(2)}, u32[]{:S(2)}) collective-permute-start(bf16[8,2048]{1,0:T(8,128)(2,1)S(1)} %get-tuple-element.36), channel_id=1, source_target_pairs={{0,1},{1,0},{2,3},{3,2},{4,5},{5,4},{6,7},{7,6},{8,9},{9,8},{10,11... | collective-permute-start | bytes 98312 | tf_op jit(solution)/shard_map/ppermute | solution.py:58
  31.4 5.1 %collective-permute-start.11 = (bf16[8,2048]{1,0:T(8,128)(2,1)S(1)}, bf16[8,2048]{1,0:T(8,128)(2,1)S(1)}, u32[]{:S(2)}, u32[]{:S(2)}) collective-permute-start(bf16[8,2048]{1,0:T(8,128)(2,1)S(1)} %get-tuple-element.37), channel_id=1, source_target_pairs={{0,24},{4,28},{8,16},{12,20},{16,8},{20,12},{24,0},{28,4},{1,25},{... | collective-permute-start | bytes 98312 | tf_op jit(solution)/shard_map/ppermute | solution.py:58
  33.9 3.9 %collective-permute-start.12 = (bf16[8,2048]{1,0:T(8,128)(2,1)S(1)}, bf16[8,2048]{1,0:T(8,128)(2,1)S(1)}, u32[]{:S(2)}, u32[]{:S(2)}) collective-permute-start(bf16[8,2048]{1,0:T(8,128)(2,1)S(1)} %get-tuple-element.37), channel_id=1, source_target_pairs={{0,16},{4,20},{8,24},{12,28},{16,0},{20,4},{24,8},{28,12},{1,17},{... | collective-permute-start | bytes 98312 | tf_op jit(solution)/shard_map/ppermute | solution.py:58
  34.4 3.9 %collective-permute-start.13 = (bf16[8,2048]{1,0:T(8,128)(2,1)S(1)}, bf16[8,2048]{1,0:T(8,128)(2,1)S(1)}, u32[]{:S(2)}, u32[]{:S(2)}) collective-permute-start(bf16[8,2048]{1,0:T(8,128)(2,1)S(1)} %get-tuple-element.37), channel_id=1, source_target_pairs={{0,8},{4,12},{8,0},{12,4},{16,24},{20,28},{24,16},{28,20},{1,9},{5... | collective-permute-start | bytes 98312 | tf_op jit(solution)/shard_map/ppermute | solution.py:58

commit v8 on v7

--- a/solution.py
+++ b/solution.py
@@ -106,7 +106,11 @@
     bounds_ref, lens, order, sems = refs[2 * n - 2 :]
     targets = (lens, order) + targets
     copies = [
-        pltpu.make_async_copy(source.at[pl.ds(0, target.shape[0])], target, sems.at[k])
+        pltpu.make_async_copy(
+            source if source.shape == target.shape else source.at[pl.ds(0, target.shape[0])],
+            target,
+            sems.at[k],
+        )
         for k, (source, target) in enumerate(zip(sources, targets))
     ]
     for copy in copies:

time: 49.4 us -> 49.4 us (level)
  no operation moved by 1% of the time
where the time goes in v8:
time: 49.4 us; the launch traced here: 49.2 us
  starting transfers between devices  16.5 us (33%)
  waiting for transfers between devices  12.5 us (25%)
  Pallas kernels  10.1 us (20%)
  blocking collectives  9.36 us (19%)
  between operations  0.73 us (1%)
    ppermute x16, starting transfers between devices, swap(): return lax.ppermute(x, axis, [(i, i ^ offset) for i in range(n)])  16.5 us
    ppermute x16, waiting for transfers between devices, swap(): return lax.ppermute(x, axis, [(i, i ^ offset) for i in range(n)])  12.5 us
    all_to_all x1, blocking collectives, body(): lax.all_to_all(term, ('req', 'tp'), split_axis=0, concat_axis=0, tiled=Tr...  9.36 us
    pallas_call x1, Pallas kernels, attend(): pl.pallas_call(functools.partial(attention_kernel, req_count, len(tokens)...  3.91 us
    pallas_call x1, Pallas kernels, load(): pl.pallas_call(functools.partial(load_kernel, len(sources)), out_shape=[p...  2.64 us
    pallas_call x1, Pallas kernels, own_part(): pl.pallas_call(own_kernel, out_shape=[jax.ShapeDtypeStruct((own_rows, hea...  1.26 us
  transfers between devices with their start and end apart: 16, of which 11 were waited for; matrix products, arithmetic and copies ran while one was open for 0% of the time, Pallas kernels for 17%

profile of v8, /device:TPU:0, one launch (start us, length us, event | category | flops | bytes accessed | tf_op | source)
XLA Modules:
  0.0 49.2 jit_solution(3118640634794614732)
XLA Ops:
  0.6 0.5 %collective-permute-start.14 = (bf16[2048,256]{1,0:T(8,128)(2,1)}, bf16[2048,256]{1,0:T(8,128)(2,1)S(1)}, u32[]{:S(2)}, u32[]{:S(2)}) collective-permute-start(bf16[2048,256]{1,0:T(8,128)(2,1)} %refs_4_.3), channel_id=1, source_target_pairs={{0,4},{4,0},{8,12},{12,8},{16,20},{20,16},{24,28},{28,24},{1,5},{5... | collective-permute-start | bytes 3145736 | tf_op jit(solution)/shard_map/ppermute | solution.py:58
  1.2 3.9 %collective-permute-start = (bf16[8,2048]{1,0:T(8,128)(2,1)}, bf16[8,2048]{1,0:T(8,128)(2,1)S(1)}, u32[]{:S(2)}, u32[]{:S(2)}) collective-permute-start(bf16[8,2048]{1,0:T(8,128)(2,1)} %refs_2_.1), channel_id=1, source_target_pairs={{0,24},{4,28},{8,16},{12,20},{16,8},{20,12},{24,0},{28,4},{1,25},{... | collective-permute-start | bytes 98312 | tf_op jit(solution)/shard_map/ppermute | solution.py:58
  5.7 2.6 %load.1 = (bf16[8,2048]{1,0:T(8,128)(2,1)S(1)}, f32[1,2048]{1,0:T(1,128)S(1)}, bf16[2048,512]{1,0:T(8,128)(2,1)S(1)}, bf16[3072,512]{1,0:T(8,128)(2,1)S(1)}, s32[2,64,128]{2,1,0:T(8,128)S(1)}) custom-call(s32[1,64]{1,0:T(1,128)} %bitcast.28, s32[1,64]{1,0:T(1,128)} %bitcast.29, bf16[8,2048]{1,0:T(8,128)(2,1)} %refs_2_.1, f32[1,2048]{1,0:T(1,128)} %bitcast.27, ...), custom_call_target="tpu_custom_call" | custom-call | bytes 6328320 | tf_op jit(solution)/shard_map/load/pallas_call | solution.py:130
  8.3 0.9 %collective-permute-done.1 = bf16[8,2048]{1,0:T(8,128)(2,1)S(1)} collective-permute-done((bf16[8,2048]{1,0:T(8,128)(2,1)}, bf16[8,2048]{1,0:T(8,128)(2,1)S(1)}, u32[]{:S(2)}, u32[]{:S(2)}) %collective-permute-start.1) | collective-permute-done | bytes 32800 | tf_op jit(solution)/shard_map/ppermute | solution.py:58
  9.8 1.3 %collective-permute-done.3.refs_4_ = bf16[4,8,2048]{2,1,0:T(8,128)(2,1)S(1)} collective-permute-done((bf16[4,8,2048]{2,1,0:T(8,128)(2,1)S(1)}, bf16[4,8,2048]{2,1,0:T(8,128)(2,1)S(1)}, u32[]{:S(2)}, u32[]{:S(2)}) %collective-permute-start.3) | collective-permute-done | bytes 131104 | tf_op jit(solution)/shard_map/ppermute | solution.py:58
  11.2 3.9 %attention.1 = (bf16[2,8,640]{2,1,0:T(8,128)(2,1)S(1)}, bf16[2,8,640]{2,1,0:T(8,128)(2,1)S(1)}, bf16[2,8,640]{2,1,0:T(8,128)(2,1)S(1)}, bf16[2,8,640]{2,1,0:T(8,...) custom-call(bf16[1,8,2048]{2,1,0:T(8,128)(2,1)S(1)} %bitcast.14, bf16[1,8,2048]{2,1,0:T(8,128)(2,1)S(1)} %bitcast.16, ...), custom_call_target="tpu_custom_call" | custom-call | tf_op jit(solution)/shard_map/attention/pallas_call | solution.py:268
  15.1 1.6 %collective-permute-start.4 = (bf16[2,8,640]{2,1,0:T(8,128)(2,1)S(1)}, bf16[2,8,640]{2,1,0:T(8,128)(2,1)S(1)}, u32[]{:S(2)}, u32[]{:S(2)}) collective-permute-start(bf16[2,8,640]{2,1,0:T(8,128)(2,1)S(1)} %get-tuple-element.28), channel_id=1, source_target_pairs={{0,24},{4,28},{8,16},{12,20},{16,8},{20,12},{24,0},{28,4},{1,25},{... | collective-permute-start | bytes 61448 | tf_op jit(solution)/shard_map/ppermute | solution.py:58
  17.2 1.4 %collective-permute-start.6 = (bf16[2,8,640]{2,1,0:T(8,128)(2,1)S(1)}, bf16[2,8,640]{2,1,0:T(8,128)(2,1)S(1)}, u32[]{:S(2)}, u32[]{:S(2)}) collective-permute-start(bf16[2,8,640]{2,1,0:T(8,128)(2,1)S(1)} %get-tuple-element.30), channel_id=1, source_target_pairs={{0,8},{4,12},{8,0},{12,4},{16,24},{20,28},{24,16},{28,20},{1,9},{5... | collective-permute-start | bytes 61448 | tf_op jit(solution)/shard_map/ppermute | solution.py:58
  18.7 1.3 %own.1 = (bf16[8,512]{1,0:T(8,128)(2,1)}, bf16[8,512]{1,0:T(8,128)(2,1)}, f32[8,640]{1,0:T(8,128)S(1)}, bf16[8,640]{1,0:T(8,128)(2,1)S(1)}) custom-call(bf16[16,2048]{1,0:T(8,128)(2,1)S(1)} %get-tuple-element.31.normed_ref, f32[16,512]{1,0:T(8,128)S(1)} %get-tuple-element.32.queries_ref, bf16[2048,512]{1,0:T(8,128)(2,1)S(1)} %copy-done, ...), custom_call_target="tpu_custom_call" | custom-call | tf_op jit(solution)/shard_map/own/pallas_call | solution.py:316
  19.9 0.6 %collective-permute-done.5.refs_2_ = bf16[2,8,640]{2,1,0:T(8,128)(2,1)S(1)} collective-permute-done((bf16[2,8,640]{2,1,0:T(8,128)(2,1)S(1)}, bf16[2,8,640]{2,1,0:T(8,128)(2,1)S(1)}, u32[]{:S(2)}, u32[]{:S(2)}) %collective-permute-start.5) | collective-permute-done | bytes 20512 | tf_op jit(solution)/shard_map/ppermute | solution.py:58
  21.1 1.2 %collective-permute-done.7.refs_4_ = bf16[4,8,640]{2,1,0:T(8,128)(2,1)S(1)} collective-permute-done((bf16[4,8,640]{2,1,0:T(8,128)(2,1)S(1)}, bf16[4,8,640]{2,1,0:T(8,128)(2,1)S(1)}, u32[]{:S(2)}, u32[]{:S(2)}) %collective-permute-start.7) | collective-permute-done | bytes 40992 | tf_op jit(solution)/shard_map/ppermute | solution.py:58
  22.3 0.6 %merge.1 = (f32[8,2048]{1,0:T(8,128)S(1)}, bf16[8,2048]{1,0:T(8,128)(2,1)S(1)}) custom-call(bf16[2,8,640]{2,1,0:T(8,128)(2,1)S(1)} %get-tuple-element.27.group_ref.refs_0_, bf16[2,8,640]{2,1,0:T(8,128)(2,1)S(1)} %collective-permute-done.4.refs_1_, bf16[2,8,640]{2,1,0:T(8,128)(2,1)S(1)} %collective-permute-done.5.refs_2_, ...), custom_call_target="tpu_custom_call" | custom-call | tf_op jit(solution)/shard_map/merge/pallas_call | solution.py:364
  22.9 2.6 %collective-permute-start.10 = (bf16[8,2048]{1,0:T(8,128)(2,1)S(1)}, bf16[8,2048]{1,0:T(8,128)(2,1)S(1)}, u32[]{:S(2)}, u32[]{:S(2)}) collective-permute-start(bf16[8,2048]{1,0:T(8,128)(2,1)S(1)} %get-tuple-element.36), channel_id=1, source_target_pairs={{0,2},{1,3},{2,0},{3,1},{4,6},{5,7},{6,4},{7,5},{8,10},{9,11},{10,... | collective-permute-start | bytes 98312 | tf_op jit(solution)/shard_map/ppermute | solution.py:58
  25.5 1.3 %collective-permute-start.8 = (bf16[8,2048]{1,0:T(8,128)(2,1)S(1)}, bf16[8,2048]{1,0:T(8,128)(2,1)S(1)}, u32[]{:S(2)}, u32[]{:S(2)}) collective-permute-start(bf16[8,2048]{1,0:T(8,128)(2,1)S(1)} %get-tuple-element.36), channel_id=1, source_target_pairs={{0,3},{1,2},{2,1},{3,0},{4,7},{5,6},{6,5},{7,4},{8,11},{9,10},{10,... | collective-permute-start | bytes 98312 | tf_op jit(solution)/shard_map/ppermute | solution.py:58
  27.1 1.0 %collective-permute-done.10.refs_3_ = bf16[8,2048]{1,0:T(8,128)(2,1)S(1)} collective-permute-done((bf16[8,2048]{1,0:T(8,128)(2,1)S(1)}, bf16[8,2048]{1,0:T(8,128)(2,1)S(1)}, u32[]{:S(2)}, u32[]{:S(2)}) %collective-permute-start.10) | collective-permute-done | bytes 32800 | tf_op jit(solution)/shard_map/ppermute | solution.py:58
  28.0 3.1 %collective-permute-done.8.refs_1_ = bf16[8,2048]{1,0:T(8,128)(2,1)S(1)} collective-permute-done((bf16[8,2048]{1,0:T(8,128)(2,1)S(1)}, bf16[8,2048]{1,0:T(8,128)(2,1)S(1)}, u32[]{:S(2)}, u32[]{:S(2)}) %collective-permute-start.8) | collective-permute-done | bytes 32800 | tf_op jit(solution)/shard_map/ppermute | solution.py:58
  31.4 2.4 %collective-permute-start.11 = (bf16[8,2048]{1,0:T(8,128)(2,1)S(1)}, bf16[8,2048]{1,0:T(8,128)(2,1)S(1)}, u32[]{:S(2)}, u32[]{:S(2)}) collective-permute-start(bf16[8,2048]{1,0:T(8,128)(2,1)S(1)} %get-tuple-element.37), channel_id=1, source_target_pairs={{0,24},{4,28},{8,16},{12,20},{16,8},{20,12},{24,0},{28,4},{1,25},{... | collective-permute-start | bytes 98312 | tf_op jit(solution)/shard_map/ppermute | solution.py:58
  33.9 0.5 %collective-permute-start.12 = (bf16[8,2048]{1,0:T(8,128)(2,1)S(1)}, bf16[8,2048]{1,0:T(8,128)(2,1)S(1)}, u32[]{:S(2)}, u32[]{:S(2)}) collective-permute-start(bf16[8,2048]{1,0:T(8,128)(2,1)S(1)} %get-tuple-element.37), channel_id=1, source_target_pairs={{0,16},{4,20},{8,24},{12,28},{16,0},{20,4},{24,8},{28,12},{1,17},{... | collective-permute-start | bytes 98312 | tf_op jit(solution)/shard_map/ppermute | solution.py:58
  34.4 0.6 %collective-permute-start.13 = (bf16[8,2048]{1,0:T(8,128)(2,1)S(1)}, bf16[8,2048]{1,0:T(8,128)(2,1)S(1)}, u32[]{:S(2)}, u32[]{:S(2)}) collective-permute-start(bf16[8,2048]{1,0:T(8,128)(2,1)S(1)} %get-tuple-element.37), channel_id=1, source_target_pairs={{0,8},{4,12},{8,0},{12,4},{16,24},{20,28},{24,16},{28,20},{1,9},{5... | collective-permute-start | bytes 98312 | tf_op jit(solution)/shard_map/ppermute | solution.py:58
  35.0 1.5 %collective-permute-done.11 = bf16[8,2048]{1,0:T(8,128)(2,1)S(1)} collective-permute-done((bf16[8,2048]{1,0:T(8,128)(2,1)S(1)}, bf16[8,2048]{1,0:T(8,128)(2,1)S(1)}, u32[]{:S(2)}, u32[]{:S(2)}) %collective-permute-start.11) | collective-permute-done | bytes 32800 | tf_op jit(solution)/shard_map/ppermute | solution.py:58
  36.5 1.3 %collective-permute-done.12 = bf16[8,2048]{1,0:T(8,128)(2,1)S(1)} collective-permute-done((bf16[8,2048]{1,0:T(8,128)(2,1)S(1)}, bf16[8,2048]{1,0:T(8,128)(2,1)S(1)}, u32[]{:S(2)}, u32[]{:S(2)}) %collective-permute-start.12) | collective-permute-done | bytes 32800 | tf_op jit(solution)/shard_map/ppermute | solution.py:58
  38.3 0.9 %mlp.1 = bf16[16,8,512]{2,1,0:T(8,128)(2,1)S(1)} custom-call(bf16[1,8,2048]{2,1,0:T(8,128)(2,1)S(1)} %bitcast.21, bf16[1,8,2048]{2,1,0:T(8,128)(2,1)S(1)} %bitcast.22, bf16[1,8,2048]{2,1,0:T(8,128)(2,1)S(1)} %bitcast.23, bf16[1,8,2048]{2,1,0:T(8,128)(2,1)S(1)} %bitcast.24, bf16[2048,256]{1,0:T(8,128)(2,1)S(1)} %copy-done.3, bf16[256,2048]{1,0:T(8,128)(2,1)S(1)} %copy-done.4, ...), custom_call_target="tpu_custom_call" | custom-call | tf_op jit(solution)/shard_map/mlp/pallas_call | solution.py:426
  39.2 9.4 %all_to_all.5.recv_ref = bf16[16,8,512]{2,1,0:T(8,128)(2,1)S(1)} all-to-all(bf16[16,8,512]{2,1,0:T(8,128)(2,1)S(1)} %mlp.1), channel_id=1, replica_groups={{18,19,0,2,17,26,11,8,9,10,3,25,27,16,24,1},{22,23,4,6,21,30,15,12,13,1..., dimensions={0} | all-to-all | bytes 262144 | tf_op jit(solution)/shard_map/all_to_all | solution.py:502
  48.6 0.6 %finish.1 = bf16[8,512]{1,0:T(8,128)(2,1)} custom-call(bf16[16,8,512]{2,1,0:T(8,128)(2,1)S(1)} %all_to_all.5.recv_ref, f32[8,512]{1,0:T(8,128)S(1)} %get-tuple-element.38.columns_ref), custom_call_target="tpu_custom_call" | custom-call | tf_op jit(solution)/shard_map/finish/pallas_call | solution.py:446
  (33 shorter events, 3.3 us)
Async XLA Ops:
  0.6 37.7 %collective-permute-start.14 = (bf16[2048,256]{1,0:T(8,128)(2,1)}, bf16[2048,256]{1,0:T(8,128)(2,1)S(1)}, u32[]{:S(2)}, u32[]{:S(2)}) collective-permute-start(bf16[2048,256]{1,0:T(8,128)(2,1)} %refs_4_.3), channel_id=1, source_target_pairs={{0,4},{4,0},{8,12},{12,8},{16,20},{20,16},{24,28},{28,24},{1,5},{5... | collective-permute-start | bytes 3145736 | tf_op jit(solution)/shard_map/ppermute | solution.py:58
  1.1 37.1 %collective-permute-start.15 = (bf16[256,2048]{1,0:T(8,128)(2,1)}, bf16[256,2048]{1,0:T(8,128)(2,1)S(1)}, u32[]{:S(2)}, u32[]{:S(2)}) collective-permute-start(bf16[256,2048]{1,0:T(8,128)(2,1)} %refs_5_.3), channel_id=1, source_target_pairs={{0,4},{4,0},{8,12},{12,8},{16,20},{20,16},{24,28},{28,24},{1,5},{5... | collective-permute-start | bytes 3145736 | tf_op jit(solution)/shard_map/ppermute | solution.py:58
  1.2 7.1 %collective-permute-start = (bf16[8,2048]{1,0:T(8,128)(2,1)}, bf16[8,2048]{1,0:T(8,128)(2,1)S(1)}, u32[]{:S(2)}, u32[]{:S(2)}) collective-permute-start(bf16[8,2048]{1,0:T(8,128)(2,1)} %refs_2_.1), channel_id=1, source_target_pairs={{0,24},{4,28},{8,16},{12,20},{16,8},{20,12},{24,0},{28,4},{1,25},{... | collective-permute-start | bytes 98312 | tf_op jit(solution)/shard_map/ppermute | solution.py:58
  5.1 4.1 %collective-permute-start.1 = (bf16[8,2048]{1,0:T(8,128)(2,1)}, bf16[8,2048]{1,0:T(8,128)(2,1)S(1)}, u32[]{:S(2)}, u32[]{:S(2)}) collective-permute-start(bf16[8,2048]{1,0:T(8,128)(2,1)} %refs_2_.1), channel_id=1, source_target_pairs={{0,16},{4,20},{8,24},{12,28},{16,0},{20,4},{24,8},{28,12},{1,17},{... | collective-permute-start | bytes 98312 | tf_op jit(solution)/shard_map/ppermute | solution.py:58
  5.6 4.1 %collective-permute-start.2 = (bf16[8,2048]{1,0:T(8,128)(2,1)}, bf16[8,2048]{1,0:T(8,128)(2,1)S(1)}, u32[]{:S(2)}, u32[]{:S(2)}) collective-permute-start(bf16[8,2048]{1,0:T(8,128)(2,1)} %refs_2_.1), channel_id=1, source_target_pairs={{0,8},{4,12},{8,0},{12,4},{16,24},{20,28},{24,16},{28,20},{1,9},{5... | collective-permute-start | bytes 98312 | tf_op jit(solution)/shard_map/ppermute | solution.py:58
  9.8 1.4 %collective-permute-start.3 = (bf16[4,8,2048]{2,1,0:T(8,128)(2,1)S(1)}, bf16[4,8,2048]{2,1,0:T(8,128)(2,1)S(1)}, u32[]{:S(2)}, u32[]{:S(2)}) collective-permute-start(bf16[4,8,2048]{2,1,0:T(8,128)(2,1)S(1)} %pad_maximum_fusion), channel_id=1, source_target_pairs={{0,4},{4,0},{8,12},{12,8},{16,20},{20,16},{24,28},{28,24},{1,5},{5... | collective-permute-start | bytes 393224 | tf_op jit(solution)/shard_map/ppermute | solution.py:58
  11.2 7.5 %copy-start = (bf16[2048,512]{1,0:T(8,128)(2,1)S(1)}, bf16[2048,512]{1,0:T(8,128)(2,1)}, u32[]{:S(2)}) copy-start(bf16[2048,512]{1,0:T(8,128)(2,1)} %wk.1) | copy-start | bytes 6291460
  11.2 7.5 %copy-start.1 = (bf16[2048,512]{1,0:T(8,128)(2,1)S(1)}, bf16[2048,512]{1,0:T(8,128)(2,1)}, u32[]{:S(2)}) copy-start(bf16[2048,512]{1,0:T(8,128)(2,1)} %wv.1) | copy-start | bytes 6291460
  15.1 4.8 %collective-permute-start.4 = (bf16[2,8,640]{2,1,0:T(8,128)(2,1)S(1)}, bf16[2,8,640]{2,1,0:T(8,128)(2,1)S(1)}, u32[]{:S(2)}, u32[]{:S(2)}) collective-permute-start(bf16[2,8,640]{2,1,0:T(8,128)(2,1)S(1)} %get-tuple-element.28), channel_id=1, source_target_pairs={{0,24},{4,28},{8,16},{12,20},{16,8},{20,12},{24,0},{28,4},{1,25},{... | collective-permute-start | bytes 61448 | tf_op jit(solution)/shard_map/ppermute | solution.py:58
  16.7 3.8 %collective-permute-start.5 = (bf16[2,8,640]{2,1,0:T(8,128)(2,1)S(1)}, bf16[2,8,640]{2,1,0:T(8,128)(2,1)S(1)}, u32[]{:S(2)}, u32[]{:S(2)}) collective-permute-start(bf16[2,8,640]{2,1,0:T(8,128)(2,1)S(1)} %get-tuple-element.29), channel_id=1, source_target_pairs={{0,16},{4,20},{8,24},{12,28},{16,0},{20,4},{24,8},{28,12},{1,17},{... | collective-permute-start | bytes 61448 | tf_op jit(solution)/shard_map/ppermute | solution.py:58
  17.2 3.8 %collective-permute-start.6 = (bf16[2,8,640]{2,1,0:T(8,128)(2,1)S(1)}, bf16[2,8,640]{2,1,0:T(8,128)(2,1)S(1)}, u32[]{:S(2)}, u32[]{:S(2)}) collective-permute-start(bf16[2,8,640]{2,1,0:T(8,128)(2,1)S(1)} %get-tuple-element.30), channel_id=1, source_target_pairs={{0,8},{4,12},{8,0},{12,4},{16,24},{20,28},{24,16},{28,20},{1,9},{5... | collective-permute-start | bytes 61448 | tf_op jit(solution)/shard_map/ppermute | solution.py:58
  18.7 3.6 %copy-start.2 = (bf16[512,2048]{1,0:T(8,128)(2,1)S(1)}, bf16[512,2048]{1,0:T(8,128)(2,1)}, u32[]{:S(2)}) copy-start(bf16[512,2048]{1,0:T(8,128)(2,1)} %refs_6_.1) | copy-start | bytes 6291460
  19.9 11.3 %copy-start.5 = (f32[2048]{0:T(1024)S(1)}, f32[2048]{0:T(1024)}, u32[]{:S(2)}) copy-start(f32[2048]{0:T(1024)} %param.19) | copy-start | bytes 24580
  19.9 18.4 %copy-start.3 = (bf16[2048,256]{1,0:T(8,128)(2,1)S(1)}, bf16[2048,256]{1,0:T(8,128)(2,1)}, u32[]{:S(2)}) copy-start(bf16[2048,256]{1,0:T(8,128)(2,1)} %refs_4_.3) | copy-start | bytes 3145732
  19.9 18.4 %copy-start.4 = (bf16[256,2048]{1,0:T(8,128)(2,1)S(1)}, bf16[256,2048]{1,0:T(8,128)(2,1)}, u32[]{:S(2)}) copy-start(bf16[256,2048]{1,0:T(8,128)(2,1)} %refs_5_.3) | copy-start | bytes 3145732
  21.0 1.3 %collective-permute-start.7 = (bf16[4,8,640]{2,1,0:T(8,128)(2,1)S(1)}, bf16[4,8,640]{2,1,0:T(8,128)(2,1)S(1)}, u32[]{:S(2)}, u32[]{:S(2)}) collective-permute-start(bf16[4,8,640]{2,1,0:T(8,128)(2,1)S(1)} %pad_maximum_fusion.1), channel_id=1, source_target_pairs={{0,4},{4,0},{8,12},{12,8},{16,20},{20,16},{24,28},{28,24},{1,5},{5... | collective-permute-start | bytes 122888 | tf_op jit(solution)/shard_map/ppermute | solution.py:58
  22.9 5.2 %collective-permute-start.10 = (bf16[8,2048]{1,0:T(8,128)(2,1)S(1)}, bf16[8,2048]{1,0:T(8,128)(2,1)S(1)}, u32[]{:S(2)}, u32[]{:S(2)}) collective-permute-start(bf16[8,2048]{1,0:T(8,128)(2,1)S(1)} %get-tuple-element.36), channel_id=1, source_target_pairs={{0,2},{1,3},{2,0},{3,1},{4,6},{5,7},{6,4},{7,5},{8,10},{9,11},{10,... | collective-permute-start | bytes 98312 | tf_op jit(solution)/shard_map/ppermute | solution.py:58
  25.5 5.7 %collective-permute-start.8 = (bf16[8,2048]{1,0:T(8,128)(2,1)S(1)}, bf16[8,2048]{1,0:T(8,128)(2,1)S(1)}, u32[]{:S(2)}, u32[]{:S(2)}) collective-permute-start(bf16[8,2048]{1,0:T(8,128)(2,1)S(1)} %get-tuple-element.36), channel_id=1, source_target_pairs={{0,3},{1,2},{2,1},{3,0},{4,7},{5,6},{6,5},{7,4},{8,11},{9,10},{10,... | collective-permute-start | bytes 98312 | tf_op jit(solution)/shard_map/ppermute | solution.py:58
  26.8 4.4 %collective-permute-start.9 = (bf16[8,2048]{1,0:T(8,128)(2,1)S(1)}, bf16[8,2048]{1,0:T(8,128)(2,1)S(1)}, u32[]{:S(2)}, u32[]{:S(2)}) collective-permute-start(bf16[8,2048]{1,0:T(8,128)(2,1)S(1)} %get-tuple-element.36), channel_id=1, source_target_pairs={{0,1},{1,0},{2,3},{3,2},{4,5},{5,4},{6,7},{7,6},{8,9},{9,8},{10,11... | collective-permute-start | bytes 98312 | tf_op jit(solution)/shard_map/ppermute | solution.py:58
  31.4 5.1 %collective-permute-start.11 = (bf16[8,2048]{1,0:T(8,128)(2,1)S(1)}, bf16[8,2048]{1,0:T(8,128)(2,1)S(1)}, u32[]{:S(2)}, u32[]{:S(2)}) collective-permute-start(bf16[8,2048]{1,0:T(8,128)(2,1)S(1)} %get-tuple-element.37), channel_id=1, source_target_pairs={{0,24},{4,28},{8,16},{12,20},{16,8},{20,12},{24,0},{28,4},{1,25},{... | collective-permute-start | bytes 98312 | tf_op jit(solution)/shard_map/ppermute | solution.py:58
  33.9 3.9 %collective-permute-start.12 = (bf16[8,2048]{1,0:T(8,128)(2,1)S(1)}, bf16[8,2048]{1,0:T(8,128)(2,1)S(1)}, u32[]{:S(2)}, u32[]{:S(2)}) collective-permute-start(bf16[8,2048]{1,0:T(8,128)(2,1)S(1)} %get-tuple-element.37), channel_id=1, source_target_pairs={{0,16},{4,20},{8,24},{12,28},{16,0},{20,4},{24,8},{28,12},{1,17},{... | collective-permute-start | bytes 98312 | tf_op jit(solution)/shard_map/ppermute | solution.py:58
  34.4 3.9 %collective-permute-start.13 = (bf16[8,2048]{1,0:T(8,128)(2,1)S(1)}, bf16[8,2048]{1,0:T(8,128)(2,1)S(1)}, u32[]{:S(2)}, u32[]{:S(2)}) collective-permute-start(bf16[8,2048]{1,0:T(8,128)(2,1)S(1)} %get-tuple-element.37), channel_id=1, source_target_pairs={{0,8},{4,12},{8,0},{12,4},{16,24},{20,28},{24,16},{28,20},{1,9},{5... | collective-permute-start | bytes 98312 | tf_op jit(solution)/shard_map/ppermute | solution.py:58

commit v9 on v8

--- a/solution.py
+++ b/solution.py
@@ -45,7 +45,7 @@
     return first.astype(jnp.int32), (first + lens_col).astype(jnp.int32)
 
 
-TERM_ORDER = (10, 11, 0, 2, 9, 14, 7, 4, 5, 6, 3, 13, 15, 8, 12, 1)
+TERM_ORDER = (10, 11, 0, 9, 2, 14, 7, 4, 5, 6, 1, 13, 15, 8, 12, 3)
 
 
 def term_order(req_count, tp_count):

time: 49.4 us -> 49.5 us (level)
  no operation moved by 1% of the time
where the time goes in v9:
time: 49.5 us; the launch traced here: 49.3 us
  starting transfers between devices  16.5 us (33%)
  waiting for transfers between devices  12.5 us (25%)
  Pallas kernels  10.1 us (20%)
  blocking collectives  9.45 us (19%)
  between operations  0.73 us (1%)
    ppermute x16, starting transfers between devices, swap(): return lax.ppermute(x, axis, [(i, i ^ offset) for i in range(n)])  16.5 us
    ppermute x16, waiting for transfers between devices, swap(): return lax.ppermute(x, axis, [(i, i ^ offset) for i in range(n)])  12.5 us
    all_to_all x1, blocking collectives, body(): lax.all_to_all(term, ('req', 'tp'), split_axis=0, concat_axis=0, tiled=Tr...  9.45 us
    pallas_call x1, Pallas kernels, attend(): pl.pallas_call(functools.partial(attention_kernel, req_count, len(tokens)...  3.91 us
    pallas_call x1, Pallas kernels, load(): pl.pallas_call(functools.partial(load_kernel, len(sources)), out_shape=[p...  2.64 us
    pallas_call x1, Pallas kernels, own_part(): pl.pallas_call(own_kernel, out_shape=[jax.ShapeDtypeStruct((own_rows, hea...  1.26 us
  transfers between devices with their start and end apart: 16, of which 11 were waited for; matrix products, arithmetic and copies ran while one was open for 0% of the time, Pallas kernels for 17%

profile of v9, /device:TPU:0, one launch (start us, length us, event | category | flops | bytes accessed | tf_op | source)
XLA Modules:
  0.0 49.3 jit_solution(16693722558607453899)
XLA Ops:
  0.6 0.5 %collective-permute-start.14 = (bf16[2048,256]{1,0:T(8,128)(2,1)}, bf16[2048,256]{1,0:T(8,128)(2,1)S(1)}, u32[]{:S(2)}, u32[]{:S(2)}) collective-permute-start(bf16[2048,256]{1,0:T(8,128)(2,1)} %refs_4_.3), channel_id=1, source_target_pairs={{0,4},{4,0},{8,12},{12,8},{16,20},{20,16},{24,28},{28,24},{1,5},{5... | collective-permute-start | bytes 3145736 | tf_op jit(solution)/shard_map/ppermute | solution.py:58
  1.2 3.9 %collective-permute-start = (bf16[8,2048]{1,0:T(8,128)(2,1)}, bf16[8,2048]{1,0:T(8,128)(2,1)S(1)}, u32[]{:S(2)}, u32[]{:S(2)}) collective-permute-start(bf16[8,2048]{1,0:T(8,128)(2,1)} %refs_2_.1), channel_id=1, source_target_pairs={{0,24},{4,28},{8,16},{12,20},{16,8},{20,12},{24,0},{28,4},{1,25},{... | collective-permute-start | bytes 98312 | tf_op jit(solution)/shard_map/ppermute | solution.py:58
  5.7 2.6 %load.1 = (bf16[8,2048]{1,0:T(8,128)(2,1)S(1)}, f32[1,2048]{1,0:T(1,128)S(1)}, bf16[2048,512]{1,0:T(8,128)(2,1)S(1)}, bf16[3072,512]{1,0:T(8,128)(2,1)S(1)}, s32[2,64,128]{2,1,0:T(8,128)S(1)}) custom-call(s32[1,64]{1,0:T(1,128)} %bitcast.28, s32[1,64]{1,0:T(1,128)} %bitcast.29, bf16[8,2048]{1,0:T(8,128)(2,1)} %refs_2_.1, f32[1,2048]{1,0:T(1,128)} %bitcast.27, ...), custom_call_target="tpu_custom_call" | custom-call | bytes 6328320 | tf_op jit(solution)/shard_map/load/pallas_call | solution.py:130
  8.3 0.9 %collective-permute-done.1 = bf16[8,2048]{1,0:T(8,128)(2,1)S(1)} collective-permute-done((bf16[8,2048]{1,0:T(8,128)(2,1)}, bf16[8,2048]{1,0:T(8,128)(2,1)S(1)}, u32[]{:S(2)}, u32[]{:S(2)}) %collective-permute-start.1) | collective-permute-done | bytes 32800 | tf_op jit(solution)/shard_map/ppermute | solution.py:58
  9.8 1.3 %collective-permute-done.3.refs_4_ = bf16[4,8,2048]{2,1,0:T(8,128)(2,1)S(1)} collective-permute-done((bf16[4,8,2048]{2,1,0:T(8,128)(2,1)S(1)}, bf16[4,8,2048]{2,1,0:T(8,128)(2,1)S(1)}, u32[]{:S(2)}, u32[]{:S(2)}) %collective-permute-start.3) | collective-permute-done | bytes 131104 | tf_op jit(solution)/shard_map/ppermute | solution.py:58
  11.2 3.9 %attention.1 = (bf16[2,8,640]{2,1,0:T(8,128)(2,1)S(1)}, bf16[2,8,640]{2,1,0:T(8,128)(2,1)S(1)}, bf16[2,8,640]{2,1,0:T(8,128)(2,1)S(1)}, bf16[2,8,640]{2,1,0:T(8,...) custom-call(bf16[1,8,2048]{2,1,0:T(8,128)(2,1)S(1)} %bitcast.14, bf16[1,8,2048]{2,1,0:T(8,128)(2,1)S(1)} %bitcast.16, ...), custom_call_target="tpu_custom_call" | custom-call | tf_op jit(solution)/shard_map/attention/pallas_call | solution.py:268
  15.1 1.6 %collective-permute-start.4 = (bf16[2,8,640]{2,1,0:T(8,128)(2,1)S(1)}, bf16[2,8,640]{2,1,0:T(8,128)(2,1)S(1)}, u32[]{:S(2)}, u32[]{:S(2)}) collective-permute-start(bf16[2,8,640]{2,1,0:T(8,128)(2,1)S(1)} %get-tuple-element.28), channel_id=1, source_target_pairs={{0,24},{4,28},{8,16},{12,20},{16,8},{20,12},{24,0},{28,4},{1,25},{... | collective-permute-start | bytes 61448 | tf_op jit(solution)/shard_map/ppermute | solution.py:58
  17.2 1.4 %collective-permute-start.6 = (bf16[2,8,640]{2,1,0:T(8,128)(2,1)S(1)}, bf16[2,8,640]{2,1,0:T(8,128)(2,1)S(1)}, u32[]{:S(2)}, u32[]{:S(2)}) collective-permute-start(bf16[2,8,640]{2,1,0:T(8,128)(2,1)S(1)} %get-tuple-element.30), channel_id=1, source_target_pairs={{0,8},{4,12},{8,0},{12,4},{16,24},{20,28},{24,16},{28,20},{1,9},{5... | collective-permute-start | bytes 61448 | tf_op jit(solution)/shard_map/ppermute | solution.py:58
  18.7 1.3 %own.1 = (bf16[8,512]{1,0:T(8,128)(2,1)}, bf16[8,512]{1,0:T(8,128)(2,1)}, f32[8,640]{1,0:T(8,128)S(1)}, bf16[8,640]{1,0:T(8,128)(2,1)S(1)}) custom-call(bf16[16,2048]{1,0:T(8,128)(2,1)S(1)} %get-tuple-element.31.normed_ref, f32[16,512]{1,0:T(8,128)S(1)} %get-tuple-element.32.queries_ref, bf16[2048,512]{1,0:T(8,128)(2,1)S(1)} %copy-done, ...), custom_call_target="tpu_custom_call" | custom-call | tf_op jit(solution)/shard_map/own/pallas_call | solution.py:316
  19.9 0.6 %collective-permute-done.5.refs_2_ = bf16[2,8,640]{2,1,0:T(8,128)(2,1)S(1)} collective-permute-done((bf16[2,8,640]{2,1,0:T(8,128)(2,1)S(1)}, bf16[2,8,640]{2,1,0:T(8,128)(2,1)S(1)}, u32[]{:S(2)}, u32[]{:S(2)}) %collective-permute-start.5) | collective-permute-done | bytes 20512 | tf_op jit(solution)/shard_map/ppermute | solution.py:58
  21.1 1.2 %collective-permute-done.7.refs_4_ = bf16[4,8,640]{2,1,0:T(8,128)(2,1)S(1)} collective-permute-done((bf16[4,8,640]{2,1,0:T(8,128)(2,1)S(1)}, bf16[4,8,640]{2,1,0:T(8,128)(2,1)S(1)}, u32[]{:S(2)}, u32[]{:S(2)}) %collective-permute-start.7) | collective-permute-done | bytes 40992 | tf_op jit(solution)/shard_map/ppermute | solution.py:58
  22.3 0.6 %merge.1 = (f32[8,2048]{1,0:T(8,128)S(1)}, bf16[8,2048]{1,0:T(8,128)(2,1)S(1)}) custom-call(bf16[2,8,640]{2,1,0:T(8,128)(2,1)S(1)} %get-tuple-element.27.group_ref.refs_0_, bf16[2,8,640]{2,1,0:T(8,128)(2,1)S(1)} %collective-permute-done.4.refs_1_, bf16[2,8,640]{2,1,0:T(8,128)(2,1)S(1)} %collective-permute-done.5.refs_2_, ...), custom_call_target="tpu_custom_call" | custom-call | tf_op jit(solution)/shard_map/merge/pallas_call | solution.py:364
  22.9 2.6 %collective-permute-start.10 = (bf16[8,2048]{1,0:T(8,128)(2,1)S(1)}, bf16[8,2048]{1,0:T(8,128)(2,1)S(1)}, u32[]{:S(2)}, u32[]{:S(2)}) collective-permute-start(bf16[8,2048]{1,0:T(8,128)(2,1)S(1)} %get-tuple-element.36), channel_id=1, source_target_pairs={{0,2},{1,3},{2,0},{3,1},{4,6},{5,7},{6,4},{7,5},{8,10},{9,11},{10,... | collective-permute-start | bytes 98312 | tf_op jit(solution)/shard_map/ppermute | solution.py:58
  25.5 1.3 %collective-permute-start.8 = (bf16[8,2048]{1,0:T(8,128)(2,1)S(1)}, bf16[8,2048]{1,0:T(8,128)(2,1)S(1)}, u32[]{:S(2)}, u32[]{:S(2)}) collective-permute-start(bf16[8,2048]{1,0:T(8,128)(2,1)S(1)} %get-tuple-element.36), channel_id=1, source_target_pairs={{0,3},{1,2},{2,1},{3,0},{4,7},{5,6},{6,5},{7,4},{8,11},{9,10},{10,... | collective-permute-start | bytes 98312 | tf_op jit(solution)/shard_map/ppermute | solution.py:58
  27.1 1.0 %collective-permute-done.10.refs_3_ = bf16[8,2048]{1,0:T(8,128)(2,1)S(1)} collective-permute-done((bf16[8,2048]{1,0:T(8,128)(2,1)S(1)}, bf16[8,2048]{1,0:T(8,128)(2,1)S(1)}, u32[]{:S(2)}, u32[]{:S(2)}) %collective-permute-start.10) | collective-permute-done | bytes 32800 | tf_op jit(solution)/shard_map/ppermute | solution.py:58
  28.0 3.1 %collective-permute-done.8.refs_1_ = bf16[8,2048]{1,0:T(8,128)(2,1)S(1)} collective-permute-done((bf16[8,2048]{1,0:T(8,128)(2,1)S(1)}, bf16[8,2048]{1,0:T(8,128)(2,1)S(1)}, u32[]{:S(2)}, u32[]{:S(2)}) %collective-permute-start.8) | collective-permute-done | bytes 32800 | tf_op jit(solution)/shard_map/ppermute | solution.py:58
  31.4 2.4 %collective-permute-start.11 = (bf16[8,2048]{1,0:T(8,128)(2,1)S(1)}, bf16[8,2048]{1,0:T(8,128)(2,1)S(1)}, u32[]{:S(2)}, u32[]{:S(2)}) collective-permute-start(bf16[8,2048]{1,0:T(8,128)(2,1)S(1)} %get-tuple-element.37), channel_id=1, source_target_pairs={{0,24},{4,28},{8,16},{12,20},{16,8},{20,12},{24,0},{28,4},{1,25},{... | collective-permute-start | bytes 98312 | tf_op jit(solution)/shard_map/ppermute | solution.py:58
  33.9 0.5 %collective-permute-start.12 = (bf16[8,2048]{1,0:T(8,128)(2,1)S(1)}, bf16[8,2048]{1,0:T(8,128)(2,1)S(1)}, u32[]{:S(2)}, u32[]{:S(2)}) collective-permute-start(bf16[8,2048]{1,0:T(8,128)(2,1)S(1)} %get-tuple-element.37), channel_id=1, source_target_pairs={{0,16},{4,20},{8,24},{12,28},{16,0},{20,4},{24,8},{28,12},{1,17},{... | collective-permute-start | bytes 98312 | tf_op jit(solution)/shard_map/ppermute | solution.py:58
  34.4 0.6 %collective-permute-start.13 = (bf16[8,2048]{1,0:T(8,128)(2,1)S(1)}, bf16[8,2048]{1,0:T(8,128)(2,1)S(1)}, u32[]{:S(2)}, u32[]{:S(2)}) collective-permute-start(bf16[8,2048]{1,0:T(8,128)(2,1)S(1)} %get-tuple-element.37), channel_id=1, source_target_pairs={{0,8},{4,12},{8,0},{12,4},{16,24},{20,28},{24,16},{28,20},{1,9},{5... | collective-permute-start | bytes 98312 | tf_op jit(solution)/shard_map/ppermute | solution.py:58
  35.0 1.5 %collective-permute-done.11 = bf16[8,2048]{1,0:T(8,128)(2,1)S(1)} collective-permute-done((bf16[8,2048]{1,0:T(8,128)(2,1)S(1)}, bf16[8,2048]{1,0:T(8,128)(2,1)S(1)}, u32[]{:S(2)}, u32[]{:S(2)}) %collective-permute-start.11) | collective-permute-done | bytes 32800 | tf_op jit(solution)/shard_map/ppermute | solution.py:58
  36.5 1.3 %collective-permute-done.12 = bf16[8,2048]{1,0:T(8,128)(2,1)S(1)} collective-permute-done((bf16[8,2048]{1,0:T(8,128)(2,1)S(1)}, bf16[8,2048]{1,0:T(8,128)(2,1)S(1)}, u32[]{:S(2)}, u32[]{:S(2)}) %collective-permute-start.12) | collective-permute-done | bytes 32800 | tf_op jit(solution)/shard_map/ppermute | solution.py:58
  38.3 0.9 %mlp.1 = bf16[16,8,512]{2,1,0:T(8,128)(2,1)S(1)} custom-call(bf16[1,8,2048]{2,1,0:T(8,128)(2,1)S(1)} %bitcast.21, bf16[1,8,2048]{2,1,0:T(8,128)(2,1)S(1)} %bitcast.22, bf16[1,8,2048]{2,1,0:T(8,128)(2,1)S(1)} %bitcast.23, bf16[1,8,2048]{2,1,0:T(8,128)(2,1)S(1)} %bitcast.24, bf16[2048,256]{1,0:T(8,128)(2,1)S(1)} %copy-done.3, bf16[256,2048]{1,0:T(8,128)(2,1)S(1)} %copy-done.4, ...), custom_call_target="tpu_custom_call" | custom-call | tf_op jit(solution)/shard_map/mlp/pallas_call | solution.py:426
  39.2 9.5 %all_to_all.5.recv_ref = bf16[16,8,512]{2,1,0:T(8,128)(2,1)S(1)} all-to-all(bf16[16,8,512]{2,1,0:T(8,128)(2,1)S(1)} %mlp.1), channel_id=1, replica_groups={{18,19,0,17,2,26,11,8,9,10,1,25,27,16,24,3},{22,23,4,21,6,30,15,12,13,1..., dimensions={0} | all-to-all | bytes 262144 | tf_op jit(solution)/shard_map/all_to_all | solution.py:502
  48.7 0.6 %finish.1 = bf16[8,512]{1,0:T(8,128)(2,1)} custom-call(bf16[16,8,512]{2,1,0:T(8,128)(2,1)S(1)} %all_to_all.5.recv_ref, f32[8,512]{1,0:T(8,128)S(1)} %get-tuple-element.38.columns_ref), custom_call_target="tpu_custom_call" | custom-call | tf_op jit(solution)/shard_map/finish/pallas_call | solution.py:446
  (33 shorter events, 3.3 us)
Async XLA Ops:
  0.6 37.7 %collective-permute-start.14 = (bf16[2048,256]{1,0:T(8,128)(2,1)}, bf16[2048,256]{1,0:T(8,128)(2,1)S(1)}, u32[]{:S(2)}, u32[]{:S(2)}) collective-permute-start(bf16[2048,256]{1,0:T(8,128)(2,1)} %refs_4_.3), channel_id=1, source_target_pairs={{0,4},{4,0},{8,12},{12,8},{16,20},{20,16},{24,28},{28,24},{1,5},{5... | collective-permute-start | bytes 3145736 | tf_op jit(solution)/shard_map/ppermute | solution.py:58
  1.1 37.1 %collective-permute-start.15 = (bf16[256,2048]{1,0:T(8,128)(2,1)}, bf16[256,2048]{1,0:T(8,128)(2,1)S(1)}, u32[]{:S(2)}, u32[]{:S(2)}) collective-permute-start(bf16[256,2048]{1,0:T(8,128)(2,1)} %refs_5_.3), channel_id=1, source_target_pairs={{0,4},{4,0},{8,12},{12,8},{16,20},{20,16},{24,28},{28,24},{1,5},{5... | collective-permute-start | bytes 3145736 | tf_op jit(solution)/shard_map/ppermute | solution.py:58
  1.2 7.1 %collective-permute-start = (bf16[8,2048]{1,0:T(8,128)(2,1)}, bf16[8,2048]{1,0:T(8,128)(2,1)S(1)}, u32[]{:S(2)}, u32[]{:S(2)}) collective-permute-start(bf16[8,2048]{1,0:T(8,128)(2,1)} %refs_2_.1), channel_id=1, source_target_pairs={{0,24},{4,28},{8,16},{12,20},{16,8},{20,12},{24,0},{28,4},{1,25},{... | collective-permute-start | bytes 98312 | tf_op jit(solution)/shard_map/ppermute | solution.py:58
  5.1 4.1 %collective-permute-start.1 = (bf16[8,2048]{1,0:T(8,128)(2,1)}, bf16[8,2048]{1,0:T(8,128)(2,1)S(1)}, u32[]{:S(2)}, u32[]{:S(2)}) collective-permute-start(bf16[8,2048]{1,0:T(8,128)(2,1)} %refs_2_.1), channel_id=1, source_target_pairs={{0,16},{4,20},{8,24},{12,28},{16,0},{20,4},{24,8},{28,12},{1,17},{... | collective-permute-start | bytes 98312 | tf_op jit(solution)/shard_map/ppermute | solution.py:58
  5.6 4.1 %collective-permute-start.2 = (bf16[8,2048]{1,0:T(8,128)(2,1)}, bf16[8,2048]{1,0:T(8,128)(2,1)S(1)}, u32[]{:S(2)}, u32[]{:S(2)}) collective-permute-start(bf16[8,2048]{1,0:T(8,128)(2,1)} %refs_2_.1), channel_id=1, source_target_pairs={{0,8},{4,12},{8,0},{12,4},{16,24},{20,28},{24,16},{28,20},{1,9},{5... | collective-permute-start | bytes 98312 | tf_op jit(solution)/shard_map/ppermute | solution.py:58
  9.8 1.4 %collective-permute-start.3 = (bf16[4,8,2048]{2,1,0:T(8,128)(2,1)S(1)}, bf16[4,8,2048]{2,1,0:T(8,128)(2,1)S(1)}, u32[]{:S(2)}, u32[]{:S(2)}) collective-permute-start(bf16[4,8,2048]{2,1,0:T(8,128)(2,1)S(1)} %pad_maximum_fusion), channel_id=1, source_target_pairs={{0,4},{4,0},{8,12},{12,8},{16,20},{20,16},{24,28},{28,24},{1,5},{5... | collective-permute-start | bytes 393224 | tf_op jit(solution)/shard_map/ppermute | solution.py:58
  11.2 7.5 %copy-start = (bf16[2048,512]{1,0:T(8,128)(2,1)S(1)}, bf16[2048,512]{1,0:T(8,128)(2,1)}, u32[]{:S(2)}) copy-start(bf16[2048,512]{1,0:T(8,128)(2,1)} %wk.1) | copy-start | bytes 6291460
  11.2 7.5 %copy-start.1 = (bf16[2048,512]{1,0:T(8,128)(2,1)S(1)}, bf16[2048,512]{1,0:T(8,128)(2,1)}, u32[]{:S(2)}) copy-start(bf16[2048,512]{1,0:T(8,128)(2,1)} %wv.1) | copy-start | bytes 6291460
  15.1 4.8 %collective-permute-start.4 = (bf16[2,8,640]{2,1,0:T(8,128)(2,1)S(1)}, bf16[2,8,640]{2,1,0:T(8,128)(2,1)S(1)}, u32[]{:S(2)}, u32[]{:S(2)}) collective-permute-start(bf16[2,8,640]{2,1,0:T(8,128)(2,1)S(1)} %get-tuple-element.28), channel_id=1, source_target_pairs={{0,24},{4,28},{8,16},{12,20},{16,8},{20,12},{24,0},{28,4},{1,25},{... | collective-permute-start | bytes 61448 | tf_op jit(solution)/shard_map/ppermute | solution.py:58
  16.7 3.8 %collective-permute-start.5 = (bf16[2,8,640]{2,1,0:T(8,128)(2,1)S(1)}, bf16[2,8,640]{2,1,0:T(8,128)(2,1)S(1)}, u32[]{:S(2)}, u32[]{:S(2)}) collective-permute-start(bf16[2,8,640]{2,1,0:T(8,128)(2,1)S(1)} %get-tuple-element.29), channel_id=1, source_target_pairs={{0,16},{4,20},{8,24},{12,28},{16,0},{20,4},{24,8},{28,12},{1,17},{... | collective-permute-start | bytes 61448 | tf_op jit(solution)/shard_map/ppermute | solution.py:58
  17.2 3.8 %collective-permute-start.6 = (bf16[2,8,640]{2,1,0:T(8,128)(2,1)S(1)}, bf16[2,8,640]{2,1,0:T(8,128)(2,1)S(1)}, u32[]{:S(2)}, u32[]{:S(2)}) collective-permute-start(bf16[2,8,640]{2,1,0:T(8,128)(2,1)S(1)} %get-tuple-element.30), channel_id=1, source_target_pairs={{0,8},{4,12},{8,0},{12,4},{16,24},{20,28},{24,16},{28,20},{1,9},{5... | collective-permute-start | bytes 61448 | tf_op jit(solution)/shard_map/ppermute | solution.py:58
  18.7 3.6 %copy-start.2 = (bf16[512,2048]{1,0:T(8,128)(2,1)S(1)}, bf16[512,2048]{1,0:T(8,128)(2,1)}, u32[]{:S(2)}) copy-start(bf16[512,2048]{1,0:T(8,128)(2,1)} %refs_6_.1) | copy-start | bytes 6291460
  19.9 11.3 %copy-start.5 = (f32[2048]{0:T(1024)S(1)}, f32[2048]{0:T(1024)}, u32[]{:S(2)}) copy-start(f32[2048]{0:T(1024)} %param.19) | copy-start | bytes 24580
  19.9 18.4 %copy-start.3 = (bf16[2048,256]{1,0:T(8,128)(2,1)S(1)}, bf16[2048,256]{1,0:T(8,128)(2,1)}, u32[]{:S(2)}) copy-start(bf16[2048,256]{1,0:T(8,128)(2,1)} %refs_4_.3) | copy-start | bytes 3145732
  19.9 18.4 %copy-start.4 = (bf16[256,2048]{1,0:T(8,128)(2,1)S(1)}, bf16[256,2048]{1,0:T(8,128)(2,1)}, u32[]{:S(2)}) copy-start(bf16[256,2048]{1,0:T(8,128)(2,1)} %refs_5_.3) | copy-start | bytes 3145732
  21.0 1.3 %collective-permute-start.7 = (bf16[4,8,640]{2,1,0:T(8,128)(2,1)S(1)}, bf16[4,8,640]{2,1,0:T(8,128)(2,1)S(1)}, u32[]{:S(2)}, u32[]{:S(2)}) collective-permute-start(bf16[4,8,640]{2,1,0:T(8,128)(2,1)S(1)} %pad_maximum_fusion.1), channel_id=1, source_target_pairs={{0,4},{4,0},{8,12},{12,8},{16,20},{20,16},{24,28},{28,24},{1,5},{5... | collective-permute-start | bytes 122888 | tf_op jit(solution)/shard_map/ppermute | solution.py:58
  22.9 5.2 %collective-permute-start.10 = (bf16[8,2048]{1,0:T(8,128)(2,1)S(1)}, bf16[8,2048]{1,0:T(8,128)(2,1)S(1)}, u32[]{:S(2)}, u32[]{:S(2)}) collective-permute-start(bf16[8,2048]{1,0:T(8,128)(2,1)S(1)} %get-tuple-element.36), channel_id=1, source_target_pairs={{0,2},{1,3},{2,0},{3,1},{4,6},{5,7},{6,4},{7,5},{8,10},{9,11},{10,... | collective-permute-start | bytes 98312 | tf_op jit(solution)/shard_map/ppermute | solution.py:58
  25.5 5.7 %collective-permute-start.8 = (bf16[8,2048]{1,0:T(8,128)(2,1)S(1)}, bf16[8,2048]{1,0:T(8,128)(2,1)S(1)}, u32[]{:S(2)}, u32[]{:S(2)}) collective-permute-start(bf16[8,2048]{1,0:T(8,128)(2,1)S(1)} %get-tuple-element.36), channel_id=1, source_target_pairs={{0,3},{1,2},{2,1},{3,0},{4,7},{5,6},{6,5},{7,4},{8,11},{9,10},{10,... | collective-permute-start | bytes 98312 | tf_op jit(solution)/shard_map/ppermute | solution.py:58
  26.8 4.4 %collective-permute-start.9 = (bf16[8,2048]{1,0:T(8,128)(2,1)S(1)}, bf16[8,2048]{1,0:T(8,128)(2,1)S(1)}, u32[]{:S(2)}, u32[]{:S(2)}) collective-permute-start(bf16[8,2048]{1,0:T(8,128)(2,1)S(1)} %get-tuple-element.36), channel_id=1, source_target_pairs={{0,1},{1,0},{2,3},{3,2},{4,5},{5,4},{6,7},{7,6},{8,9},{9,8},{10,11... | collective-permute-start | bytes 98312 | tf_op jit(solution)/shard_map/ppermute | solution.py:58
  31.4 5.1 %collective-permute-start.11 = (bf16[8,2048]{1,0:T(8,128)(2,1)S(1)}, bf16[8,2048]{1,0:T(8,128)(2,1)S(1)}, u32[]{:S(2)}, u32[]{:S(2)}) collective-permute-start(bf16[8,2048]{1,0:T(8,128)(2,1)S(1)} %get-tuple-element.37), channel_id=1, source_target_pairs={{0,24},{4,28},{8,16},{12,20},{16,8},{20,12},{24,0},{28,4},{1,25},{... | collective-permute-start | bytes 98312 | tf_op jit(solution)/shard_map/ppermute | solution.py:58
  33.9 3.9 %collective-permute-start.12 = (bf16[8,2048]{1,0:T(8,128)(2,1)S(1)}, bf16[8,2048]{1,0:T(8,128)(2,1)S(1)}, u32[]{:S(2)}, u32[]{:S(2)}) collective-permute-start(bf16[8,2048]{1,0:T(8,128)(2,1)S(1)} %get-tuple-element.37), channel_id=1, source_target_pairs={{0,16},{4,20},{8,24},{12,28},{16,0},{20,4},{24,8},{28,12},{1,17},{... | collective-permute-start | bytes 98312 | tf_op jit(solution)/shard_map/ppermute | solution.py:58
  34.4 3.9 %collective-permute-start.13 = (bf16[8,2048]{1,0:T(8,128)(2,1)S(1)}, bf16[8,2048]{1,0:T(8,128)(2,1)S(1)}, u32[]{:S(2)}, u32[]{:S(2)}) collective-permute-start(bf16[8,2048]{1,0:T(8,128)(2,1)S(1)} %get-tuple-element.37), channel_id=1, source_target_pairs={{0,8},{4,12},{8,0},{12,4},{16,24},{20,28},{24,16},{28,20},{1,9},{5... | collective-permute-start | bytes 98312 | tf_op jit(solution)/shard_map/ppermute | solution.py:58
